TPU v7x, 32 devices: a whole 2x2x4 slice. The times are simulated.
32 devices in a mesh: seq: 4 (over x, core), batch: 8 (over z, y).
Axes of the slice: x: 2, y: 2, z: 4, core: 2. Of those that a mesh axis runs over, the one named last changes fastest.
Arguments:
- tokens: bfloat16 [8, 1024, 2048], P('batch', 'seq'), may hold values from -6 to 6
- decays: float32 [8, 16, 1024], P('batch', None, 'seq'), may hold values from 0.1 to 1
- out_grad: bfloat16 [8, 1024, 2048], P('batch', 'seq'), may hold values from -6 to 6
- mixer_gain: bfloat16 [2048], P(('seq', 'batch')), may hold values from 0.5 to 1.5
- query_weight: bfloat16 [2048, 2048], P(None, ('seq', 'batch')), may hold values from -0.125 to 0.125
- key_weight: bfloat16 [2048, 2048], P(None, ('seq', 'batch')), may hold values from -0.125 to 0.125
- value_weight: bfloat16 [2048, 4096], P(None, ('seq', 'batch')), may hold values from -0.125 to 0.125
- beta_weight: bfloat16 [2048, 16], P(('seq', 'batch')), may hold values from -0.25 to 0.25
- outgate_weight: bfloat16 [2048, 4096], P(None, ('seq', 'batch')), may hold values from -0.125 to 0.125
- query_conv: bfloat16 [4, 2048], P(None, ('seq', 'batch')), may hold values from -3 to 3
- key_conv: bfloat16 [4, 2048], P(None, ('seq', 'batch')), may hold values from -3 to 3
- value_conv: bfloat16 [4, 4096], P(None, ('seq', 'batch')), may hold values from -3 to 3
- head_gain: bfloat16 [256], P(('seq', 'batch')), may hold values from 0.5 to 1.5
- output_weight: bfloat16 [4096, 2048], P(('seq', 'batch')), may hold values from -0.125 to 0.125
- feed_gain: bfloat16 [2048], P(('seq', 'batch')), may hold values from 0.5 to 1.5
- feed_gate: bfloat16 [2048, 5632], P(None, ('seq', 'batch')), may hold values from -0.125 to 0.125
- feed_up: bfloat16 [2048, 5632], P(None, ('seq', 'batch')), may hold values from -0.125 to 0.125
- feed_down: bfloat16 [5632, 2048], P(('seq', 'batch')), may hold values from -0.109375 to 0.109375
Outputs:
- block_out: bfloat16 [8, 1024, 2048], P('batch', 'seq')
- tokens_grad: bfloat16 [8, 1024, 2048], P('batch', 'seq')
- mixer_gain_grad: float32 [2048], P(('seq', 'batch'))
- query_weight_grad: float32 [2048, 2048], P(None, ('seq', 'batch'))
- key_weight_grad: float32 [2048, 2048], P(None, ('seq', 'batch'))
- value_weight_grad: float32 [2048, 4096], P(None, ('seq', 'batch'))
- beta_weight_grad: float32 [2048, 16], P(('seq', 'batch'))
- outgate_weight_grad: float32 [2048, 4096], P(None, ('seq', 'batch'))
- query_conv_grad: float32 [4, 2048], P(None, ('seq', 'batch'))
- key_conv_grad: float32 [4, 2048], P(None, ('seq', 'batch'))
- value_conv_grad: float32 [4, 4096], P(None, ('seq', 'batch'))
- head_gain_grad: float32 [256], P(('seq', 'batch'))
- output_weight_grad: float32 [4096, 2048], P(('seq', 'batch'))
- feed_gain_grad: float32 [2048], P(('seq', 'batch'))
- feed_gate_grad: float32 [2048, 5632], P(None, ('seq', 'batch'))
- feed_up_grad: float32 [2048, 5632], P(None, ('seq', 'batch'))
- descent_projection_adjoint: float32 [5632, 2048], P(('seq', 'batch'))
All inputs are finite; a program needn't handle non-finite values.
Results may differ from a plain program's by a relative error of at most 0.024.
Values may be sent and summed in bfloat16 or wider, within the bound.
No kernel may reach another device: no remote copies, remote signals or barrier semaphores. Data moves between devices by JAX's collectives and lax.ppermute only.
A program may use at most 576 MiB of HBM per device.

v0:
```python
import jax
import jax.numpy as jnp
from jax import lax
from jax.sharding import PartitionSpec as P

H = 16
DK = 128
DV = 256
STRETCH = 64
KERNEL = 4


EPS_NORM = 1e-05
EPS_UNIT = 1e-06
FULL_PRODUCT = lax.Precision.HIGHEST


def shortened(value):

    def short(part):
        return part.astype(jnp.bfloat16) if part.dtype == jnp.float32 else part

    return jax.tree.map(short, value)


def product(left_side, right_side):
    return jnp.dot(left_side, right_side, preferred_element_type=jnp.float32)


def product_tn(left_side, right_side):
    return lax.dot_general(
        left_side, right_side, (((0,), (0,)), ((), ())), preferred_element_type=jnp.float32
    )


def product_nt(left_side, right_side):
    return lax.dot_general(
        left_side, right_side, (((1,), (1,)), ((), ())), preferred_element_type=jnp.float32
    )


def rounded(values):
    return lax.optimization_barrier(values.astype(jnp.bfloat16)).astype(jnp.float32)


def rms_scale(values, gain_vals):
    return (
        values * lax.rsqrt(jnp.mean(values * values, axis=-1, keepdims=True) + EPS_NORM) * gain_vals
    )


def unit_rows(values):
    return values * lax.rsqrt(jnp.sum(values * values, axis=-1, keepdims=True) + EPS_UNIT)


def stretch_parts(queries, key_rows, value_rows, beta_vals, log_decay):
    block_len = log_decay.shape[-1]
    key_width = key_rows.shape[-1]
    totals = jnp.cumsum(log_decay, axis=-1)
    row_index = lax.broadcasted_iota(jnp.int32, (block_len, block_len), 0)
    col_index = lax.broadcasted_iota(jnp.int32, (block_len, block_len), 1)
    lower_mask = row_index >= col_index
    strict_mask = row_index > col_index
    log_gap = totals[..., :, None] - totals[..., None, :]
    decay_ratio = jnp.where(lower_mask, jnp.exp(jnp.where(lower_mask, log_gap, 0.0)), 0.0)
    keys_keys = jnp.einsum("...ck,...dk->...cd", key_rows, key_rows, precision=FULL_PRODUCT)
    query_keys = jnp.einsum("...ck,...dk->...cd", queries, key_rows, precision=FULL_PRODUCT)
    coupling = jnp.where(strict_mask, beta_vals[..., :, None] * decay_ratio * keys_keys, 0.0)
    system = coupling + jnp.eye(block_len, dtype=jnp.float32)
    growth = jnp.exp(totals)
    right_side = jnp.concatenate(
        [(beta_vals * growth)[..., None] * key_rows, beta_vals[..., None] * value_rows], axis=-1
    )
    solved = jax.scipy.linalg.solve_triangular(system, right_side, lower=True, unit_diagonal=True)
    weight_part = solved[..., :key_width]
    value_part = solved[..., key_width:]
    scores = decay_ratio * query_keys
    shard_local_output = jnp.einsum(
        "...ct,...tv->...cv", scores, value_part, precision=FULL_PRODUCT
    )
    initial_query = growth[..., None] * queries - jnp.einsum(
        "...ct,...tk->...ck", scores, weight_part, precision=FULL_PRODUCT
    )
    last_total = totals[..., -1:]
    fadeout = jnp.exp(last_total - totals)
    state_transition = jnp.exp(last_total)[..., None] * jnp.eye(
        key_width, dtype=jnp.float32
    ) - jnp.einsum(
        "...ck,...cj->...kj", key_rows, fadeout[..., None] * weight_part, precision=FULL_PRODUCT
    )
    state_increment = jnp.einsum(
        "...ck,...cv->...kv", key_rows, fadeout[..., None] * value_part, precision=FULL_PRODUCT
    )
    return (shard_local_output, initial_query, state_transition, state_increment)


def device_state(queries, key_rows, value_rows, beta_vals, log_decay):
    row_count = queries.shape[0]
    blocks = row_count // STRETCH
    heads_count = beta_vals.shape[1]

    def split_heads(values):
        return values.reshape(blocks, STRETCH, heads_count, values.shape[-1]).transpose(2, 0, 1, 3)

    stretch_sets = stretch_parts(
        split_heads(queries),
        split_heads(key_rows),
        split_heads(value_rows),
        beta_vals.reshape(blocks, STRETCH, heads_count).transpose(2, 0, 1),
        log_decay.reshape(heads_count, blocks, STRETCH),
    )

    def follow(prefix, block_item):
        prefix_trans, prefix_increment = prefix
        shard_local_output, initial_query, state_transition, state_increment = block_item
        block_out = shard_local_output + jnp.einsum(
            "gtn,gnq->gtq", initial_query, prefix_increment, precision=FULL_PRODUCT
        )
        query_eff = jnp.einsum("hck,hkj->hcj", initial_query, prefix_trans, precision=FULL_PRODUCT)
        new_trans = jnp.einsum(
            "hkj,hjl->hkl", state_transition, prefix_trans, precision=FULL_PRODUCT
        )
        new_incr = (
            jnp.einsum("zrm,zmd->zrd", state_transition, prefix_increment, precision=FULL_PRODUCT)
            + state_increment
        )
        return ((new_trans, new_incr), (block_out, query_eff))

    identity_mat = jnp.broadcast_to(jnp.eye(DK, dtype=jnp.float32), (heads_count, DK, DK))
    zero_state = jnp.zeros((heads_count, DK, DV), jnp.float32)
    block_items = tuple((jnp.moveaxis(member, 1, 0) for member in stretch_sets))
    (dev_trans, dev_incr), (outs_all, query_all) = lax.scan(
        follow, (identity_mat, zero_state), block_items
    )
    shard_output = outs_all.transpose(1, 0, 2, 3).reshape(heads_count, row_count, DV)
    partial_probe_vector = query_all.transpose(1, 0, 2, 3).reshape(heads_count, row_count, DK)
    return (shard_output, partial_probe_vector, dev_trans, dev_incr)


def activate(extended, kernels, heads_count):
    row_count = extended.shape[0] - (KERNEL - 1)
    summed = kernels[0] * extended[0:row_count]
    for offset in range(1, KERNEL):
        summed = summed + kernels[offset] * extended[offset : offset + row_count]
    smooth = jax.nn.silu(summed)
    key_width = heads_count * DK
    queries = unit_rows(smooth[:, :key_width].reshape(row_count, heads_count, DK))
    key_rows = unit_rows(smooth[:, key_width : 2 * key_width].reshape(row_count, heads_count, DK))
    value_rows = smooth[:, 2 * key_width :].reshape(row_count, heads_count, DV)
    return (queries, key_rows, value_rows)


def gate_out(head_vals, gate_vals, gain_vals):
    row_count = gate_vals.shape[0]
    heads_count = head_vals.shape[0]
    normed = rms_scale(head_vals, gain_vals)
    gate_act = jax.nn.silu(gate_vals).reshape(row_count, heads_count, DV).transpose(1, 0, 2)
    return (normed * gate_act).transpose(1, 0, 2).reshape(row_count, heads_count * DV)


def seq_rows(members):
    return jax.tree.map(
        lambda part, own: part.astype(own.dtype),
        lax.all_gather(shortened(members), "seq", axis=0, tiled=True),
        members,
    )


def seq_sums(members):
    return jax.tree.map(
        lambda part: part.astype(jnp.float32),
        lax.psum_scatter(shortened(members), "seq", scatter_dimension=0, tiled=True),
    )


def heads_layout(
    tokens,
    decays,
    out_grad,
    mixer_gain,
    query_weight,
    key_weight,
    value_weight,
    beta_weight,
    outgate_weight,
    query_conv,
    key_conv,
    value_conv,
    head_gain,
    output_weight,
    feed_gain,
    feed_gate,
    feed_up,
    feed_down,
):
    source = tokens[0]
    source_f = source.astype(jnp.float32)
    row_count = source.shape[0]
    seq_count = lax.axis_size("seq")
    seq_pos = lax.axis_index("seq")
    heads_here = H // seq_count
    full_len = row_count * seq_count
    rim_rows = KERNEL - 1
    key_here = heads_here * DK
    (
        part_gain,
        part_query,
        part_key,
        part_value,
        part_beta,
        part_outgate,
        part_query_conv,
        part_key_conv,
        part_value_conv,
        part_head_gain,
        part_output,
        part_feed_gain,
        part_feed_gate,
        part_feed_up,
        part_feed_down,
    ) = (
        lax.all_gather(mixer_gain, "batch", axis=0, tiled=True),
        lax.all_gather(query_weight, "batch", axis=1, tiled=True),
        lax.all_gather(key_weight, "batch", axis=1, tiled=True),
        lax.all_gather(value_weight, "batch", axis=1, tiled=True),
        lax.all_gather(beta_weight, "batch", axis=0, tiled=True),
        lax.all_gather(outgate_weight, "batch", axis=1, tiled=True),
        lax.all_gather(query_conv, "batch", axis=1, tiled=True),
        lax.all_gather(key_conv, "batch", axis=1, tiled=True),
        lax.all_gather(value_conv, "batch", axis=1, tiled=True),
        lax.all_gather(head_gain, "batch", axis=0, tiled=True),
        lax.all_gather(output_weight, "batch", axis=0, tiled=True),
        lax.all_gather(feed_gain, "batch", axis=0, tiled=True),
        lax.all_gather(feed_gate, "batch", axis=1, tiled=True),
        lax.all_gather(feed_up, "batch", axis=1, tiled=True),
        lax.all_gather(feed_down, "batch", axis=0, tiled=True),
    )
    whole_gain, whole_beta, complete_branch_scaling, whole_feed_gain = seq_rows(
        (part_gain, part_beta, part_head_gain, part_feed_gain)
    )
    gain_f = whole_gain.astype(jnp.float32)
    normed = rms_scale(source_f, gain_f).astype(jnp.bfloat16)
    log_decay = jnp.log(decays[0])
    spread = lax.dynamic_update_slice(
        jnp.zeros((H, full_len), jnp.float32), log_decay, (jnp.int32(0), seq_pos * row_count)
    )
    (seq_decay,) = seq_sums((spread,))
    (seq_normed,) = seq_rows((normed,))
    query_pre = product(seq_normed, part_query)
    key_pre = product(seq_normed, part_key)
    value_pre = product(seq_normed, part_value)
    gate_pre = product(seq_normed, part_outgate)
    beta_cols = lax.dynamic_slice_in_dim(whole_beta, seq_pos * heads_here, heads_here, 1)
    beta_pre = product(seq_normed, beta_cols)
    packed = jnp.concatenate([query_pre, key_pre, value_pre], axis=1).astype(jnp.bfloat16)
    extended_f = jnp.concatenate(
        [jnp.zeros((rim_rows, packed.shape[1]), jnp.bfloat16), packed], axis=0
    ).astype(jnp.float32)
    kernels = jnp.concatenate([part_query_conv, part_key_conv, part_value_conv], axis=1).astype(
        jnp.float32
    )
    queries, key_rows, value_rows = activate(extended_f, kernels, heads_here)
    query_low = rounded(queries)
    key_low = rounded(key_rows)
    value_low = rounded(value_rows)
    beta_vals = jax.nn.sigmoid(beta_pre)

    def run_heads(query_in, key_in, value_in, beta_in):
        return device_state(query_in, key_in, value_in, beta_in, seq_decay)[0]

    head_outputs, heads_pull = jax.vjp(run_heads, query_low, key_low, value_low, beta_vals)
    head_gain_f = complete_branch_scaling.astype(jnp.float32)
    mixed = gate_out(head_outputs, gate_pre, head_gain_f).astype(jnp.bfloat16)
    (branch_part,) = seq_sums((product(mixed, part_output),))
    middle = source_f + branch_part
    feed_gain_f = whole_feed_gain.astype(jnp.float32)
    feed_in = rms_scale(middle, feed_gain_f).astype(jnp.bfloat16)
    seq_feed, seq_grad = seq_rows((feed_in, out_grad[0]))
    gate_vals = product(seq_feed, part_feed_gate)
    up_vals = product(seq_feed, part_feed_up)
    hidden = (jax.nn.silu(gate_vals) * up_vals).astype(jnp.bfloat16)
    (down_part,) = seq_sums((product(hidden, part_feed_down),))
    result = middle + down_part
    block_out = result.astype(jnp.bfloat16)[None]
    d_hidden = product_nt(seq_grad, part_feed_down)
    down_term = product_tn(hidden, seq_grad)
    gate_sig = jax.nn.sigmoid(gate_vals)
    d_gate = (d_hidden * up_vals * gate_sig * (1.0 + gate_vals * (1.0 - gate_sig))).astype(
        jnp.bfloat16
    )
    d_up = (d_hidden * gate_vals * gate_sig).astype(jnp.bfloat16)
    gate_term = product_tn(seq_feed, d_gate)
    up_term = product_tn(seq_feed, d_up)
    (d_feed_in,) = seq_sums((product_nt(d_gate, part_feed_gate) + product_nt(d_up, part_feed_up),))
    feed_pull = jax.vjp(rms_scale, middle, feed_gain_f)[1]
    d_mid_norm, feed_gain_term = feed_pull(d_feed_in)
    d_middle = out_grad[0].astype(jnp.float32) + d_mid_norm
    d_branch = d_middle.astype(jnp.bfloat16)
    (seq_branch,) = seq_rows((d_branch,))
    output_term = product_tn(mixed, seq_branch)
    d_mixed = product_nt(seq_branch, part_output)
    gate_pull = jax.vjp(gate_out, head_outputs, gate_pre, head_gain_f)[1]
    heads_gradient, d_gate_pre, head_gain_term = gate_pull(d_mixed)
    d_gate_low = d_gate_pre.astype(jnp.bfloat16)
    d_queries, d_keys, d_values, d_betas = heads_pull(heads_gradient)
    d_beta_low = (d_betas * beta_vals * (1.0 - beta_vals)).astype(jnp.bfloat16)
    act_pull = jax.vjp(
        lambda widened_source, kern_in: activate(widened_source, kern_in, heads_here),
        extended_f,
        kernels,
    )[1]
    d_extended, kernel_term = act_pull((d_queries, d_keys, d_values))
    d_packed_low = d_extended[rim_rows:].astype(jnp.bfloat16)
    d_query_low = d_packed_low[:, :key_here]
    reduced_lookup_adjoint = d_packed_low[:, key_here : 2 * key_here]
    d_value_low = d_packed_low[:, 2 * key_here :]
    d_normed_full = (
        product_nt(d_query_low, part_query)
        + product_nt(reduced_lookup_adjoint, part_key)
        + product_nt(d_value_low, part_value)
        + product_nt(d_gate_low, part_outgate)
        + product_nt(d_beta_low, beta_cols)
    )
    query_term = product_tn(seq_normed, d_query_low)
    key_term = product_tn(seq_normed, reduced_lookup_adjoint)
    value_term = product_tn(seq_normed, d_value_low)
    outgate_term = product_tn(seq_normed, d_gate_low)
    beta_local = product_tn(seq_normed, d_beta_low)
    beta_place = lax.dynamic_update_slice(
        jnp.zeros(whole_beta.shape, jnp.float32), beta_local, (jnp.int32(0), seq_pos * heads_here)
    )
    query_conv_term = kernel_term[:, :key_here]
    key_conv_term = kernel_term[:, key_here : 2 * key_here]
    value_conv_term = kernel_term[:, 2 * key_here :]
    (d_normed,) = seq_sums((d_normed_full,))
    mixer_pull = jax.vjp(rms_scale, source_f, gain_f)[1]
    d_src_norm, mixer_gain_term = mixer_pull(d_normed)
    tokens_grad = (d_middle + d_src_norm).astype(jnp.bfloat16)[None]
    small_parts = seq_sums((mixer_gain_term, feed_gain_term, head_gain_term, beta_place))
    grads = (
        lax.psum_scatter(
            small_parts[0].astype(jnp.bfloat16), "batch", scatter_dimension=0, tiled=True
        ).astype(jnp.float32),
        lax.psum_scatter(
            query_term.astype(jnp.bfloat16), "batch", scatter_dimension=1, tiled=True
        ).astype(jnp.float32),
        lax.psum_scatter(
            key_term.astype(jnp.bfloat16), "batch", scatter_dimension=1, tiled=True
        ).astype(jnp.float32),
        lax.psum_scatter(
            value_term.astype(jnp.bfloat16), "batch", scatter_dimension=1, tiled=True
        ).astype(jnp.float32),
        lax.psum_scatter(
            small_parts[3].astype(jnp.bfloat16), "batch", scatter_dimension=0, tiled=True
        ).astype(jnp.float32),
        lax.psum_scatter(
            outgate_term.astype(jnp.bfloat16), "batch", scatter_dimension=1, tiled=True
        ).astype(jnp.float32),
        lax.psum_scatter(
            query_conv_term.astype(jnp.bfloat16), "batch", scatter_dimension=1, tiled=True
        ).astype(jnp.float32),
        lax.psum_scatter(
            key_conv_term.astype(jnp.bfloat16), "batch", scatter_dimension=1, tiled=True
        ).astype(jnp.float32),
        lax.psum_scatter(
            value_conv_term.astype(jnp.bfloat16), "batch", scatter_dimension=1, tiled=True
        ).astype(jnp.float32),
        lax.psum_scatter(
            small_parts[2].astype(jnp.bfloat16), "batch", scatter_dimension=0, tiled=True
        ).astype(jnp.float32),
        lax.psum_scatter(
            output_term.astype(jnp.bfloat16), "batch", scatter_dimension=0, tiled=True
        ).astype(jnp.float32),
        lax.psum_scatter(
            small_parts[1].astype(jnp.bfloat16), "batch", scatter_dimension=0, tiled=True
        ).astype(jnp.float32),
        lax.psum_scatter(
            gate_term.astype(jnp.bfloat16), "batch", scatter_dimension=1, tiled=True
        ).astype(jnp.float32),
        lax.psum_scatter(
            up_term.astype(jnp.bfloat16), "batch", scatter_dimension=1, tiled=True
        ).astype(jnp.float32),
        lax.psum_scatter(
            down_term.astype(jnp.bfloat16), "batch", scatter_dimension=0, tiled=True
        ).astype(jnp.float32),
    )
    return (
        block_out,
        tokens_grad,
        grads[0],
        grads[1],
        grads[2],
        grads[3],
        grads[4],
        grads[5],
        grads[6],
        grads[7],
        grads[8],
        grads[9],
        grads[10],
        grads[11],
        grads[12],
        grads[13],
        grads[14],
    )


def local(
    tokens,
    decays,
    out_grad,
    mixer_gain,
    query_weight,
    key_weight,
    value_weight,
    beta_weight,
    outgate_weight,
    query_conv,
    key_conv,
    value_conv,
    head_gain,
    output_weight,
    feed_gain,
    feed_gate,
    feed_up,
    feed_down,
):
    return heads_layout(
        tokens,
        decays,
        out_grad,
        mixer_gain,
        query_weight,
        key_weight,
        value_weight,
        beta_weight,
        outgate_weight,
        query_conv,
        key_conv,
        value_conv,
        head_gain,
        output_weight,
        feed_gain,
        feed_gate,
        feed_up,
        feed_down,
    )


def solution(mesh):
    in_specs = (
        P("batch", "seq", None),
        P("batch", None, "seq"),
        P("batch", "seq", None),
        P(("seq", "batch")),
        P(None, ("seq", "batch")),
        P(None, ("seq", "batch")),
        P(None, ("seq", "batch")),
        P(("seq", "batch"), None),
        P(None, ("seq", "batch")),
        P(None, ("seq", "batch")),
        P(None, ("seq", "batch")),
        P(None, ("seq", "batch")),
        P(("seq", "batch")),
        P(("seq", "batch"), None),
        P(("seq", "batch")),
        P(None, ("seq", "batch")),
        P(None, ("seq", "batch")),
        P(("seq", "batch"), None),
    )
    out_specs = (
        P("batch", "seq", None),
        P("batch", "seq", None),
        P(("seq", "batch")),
        P(None, ("seq", "batch")),
        P(None, ("seq", "batch")),
        P(None, ("seq", "batch")),
        P(("seq", "batch"), None),
        P(None, ("seq", "batch")),
        P(None, ("seq", "batch")),
        P(None, ("seq", "batch")),
        P(None, ("seq", "batch")),
        P(("seq", "batch")),
        P(("seq", "batch"), None),
        P(("seq", "batch")),
        P(None, ("seq", "batch")),
        P(None, ("seq", "batch")),
        P(("seq", "batch"), None),
    )
    return jax.shard_map(local, mesh=mesh, in_specs=in_specs, out_specs=out_specs, check_vma=False)
```

profile of v0, /device:TPU:0, one launch (start us, length us, event | category | flops | bytes accessed | tf_op | source)
XLA Modules:
  0.0 2681.7 jit_solution(4077468585564915307)
XLA Ops:
  12.5 23.1 all-reduce.26
  49.4 16.3 all_gather.71
  65.7 18.3 all-gather.2
  84.1 16.3 all-gather.1
  114.2 30.6 %all-gather.4 = bf16[8,64,16]{1,2,0:T(8,128)(2,1)S(1)} all-gather(bf16[1,64,16]{1,2,0:T(8,128)(2,1)S(1)} %bitcast.498), channel_id=1, replica_groups=mesh['seq'=4,'batch'=8] {'batch'}, dimensions={0}, use_global_device_ids=true | all-gather | bytes 18432 | tf_op jit(solution)/shard_map/all_gather | solution.py:226
  160.7 18.9 all-gather.21.cloned.1.call-done
  184.8 70.2 %all-gather.25.cloned.1.call-done = bf16[2048,1024]{1,0:T(8,128)(2,1)} async-done(((bf16[2048,128]{1,0:T(8,128)(2,1)}), bf16[2048,1024]{1,0:T(8,128)(2,1)}) %all-gather.25.cloned.1.call-update) | async-done | bytes 4194320 | tf_op jit(solution)/shard_map/all_gather | solution.py:225
  294.6 315.2 %custom-call.10 = f32[4,16,1,64,64]{3,4,2,1,0:T(8,128)S(1)} custom-call(f32[4,16,1,64,64]{4,3,2,1,0:T(8,128)} %add_bitcast_fusion), custom_call_target="InvertDiagBlocksLowerTriangular" | custom-call | tf_op jit(solution)/shard_map/jvp(jit(_solve_triangular))/vmap(vmap())/triangular_solve | solution.py:74
  649.3 76.8 %while.38 = (s32[]{:T(128)}, f32[4,128,256]{2,1,0:T(8,128)S(1)}, f32[16,4,64,256]{3,2,0,1:T(8,128)}, f32[16,4,128,256]{3,2,1,0:T(8,128)}, f32[16,4,128,128]{3,2,...) while((s32[]{:T(128)}, f32[4,128,256]{2,1,0:T(8,128)S(1)}, ...), condition=%wide.region_6.7_spmd.clone, body=%wide.region_5.6_spmd.clone.sunk | while | flops 302579712 | bytes 5115003 | solution.py:132
  768.2 36.9 %reduce-scatter.30.cloned.1.call-done = bf16[256,2048]{1,0:T(8,128)(2,1)} async-done(((bf16[1024,2048]{1,0:T(8,128)(2,1)}), bf16[256,2048]{1,0:T(8,128)(2,1)}) %reduce-scatter.30.cloned.1.call-update) | async-done | bytes 1048592 | tf_op jit(solution)/shard_map/reduce_scatter | solution.py:172
  811.3 88.9 %all-gather.33.cloned.1.call-done = bf16[2048,1408]{0,1:T(8,128)(2,1)} async-done(((bf16[2048,176]{0,1:T(8,128)(2,1)}), bf16[2048,1408]{0,1:T(8,128)(2,1)}) %all-gather.33.cloned.1.call-update) | async-done | bytes 5767184 | tf_op jit(solution)/shard_map/all_gather | solution.py:234
  900.1 34.9 %all-gather.31.cloned.1.call-done = bf16[1024,2048]{1,0:T(8,128)(2,1)} async-done(((bf16[256,2048]{1,0:T(8,128)(2,1)}), bf16[1024,2048]{1,0:T(8,128)(2,1)}) %all-gather.31.cloned.1.call-update) | async-done | bytes 4194320 | tf_op jit(solution)/shard_map/all_gather | solution.py:164
  947.2 82.8 %all-gather.35.cloned.1.call-done = bf16[2048,1408]{0,1:T(8,128)(2,1)} async-done(((bf16[2048,176]{0,1:T(8,128)(2,1)}), bf16[2048,1408]{0,1:T(8,128)(2,1)}) %all-gather.35.cloned.1.call-update) | async-done | bytes 5767184 | tf_op jit(solution)/shard_map/all_gather | solution.py:235
  1041.8 22.6 all-gather.41.cloned.1.call-done
  1064.3 95.0 %all-gather.37.cloned.1.call-done = bf16[1408,2048]{1,0:T(8,128)(2,1)} async-done(((bf16[176,2048]{1,0:T(8,128)(2,1)}), bf16[1408,2048]{1,0:T(8,128)(2,1)}) %all-gather.37.cloned.1.call-update) | async-done | bytes 5767184 | tf_op jit(solution)/shard_map/all_gather | solution.py:236
  1159.3 15.7 multiply_convert_fusion
  1194.4 42.8 %reduce-scatter.34.cloned.1.call-done = bf16[256,2048]{1,0:T(8,128)(2,1)} async-done(((bf16[1024,2048]{1,0:T(8,128)(2,1)}), bf16[256,2048]{1,0:T(8,128)(2,1)}) %reduce-scatter.34.cloned.1.call-update) | async-done | bytes 1048592 | tf_op jit(solution)/shard_map/reduce_scatter | solution.py:172
  1244.1 34.6 %all-gather.39.cloned.1.call-done = bf16[1024,2048]{1,0:T(8,128)(2,1)} async-done(((bf16[256,2048]{1,0:T(8,128)(2,1)}), bf16[1024,2048]{1,0:T(8,128)(2,1)}) %all-gather.39.cloned.1.call-update) | async-done | bytes 4194320 | tf_op jit(solution)/shard_map/all_gather | solution.py:164
  1317.9 169.6 %while.39 = (s32[]{:T(128)}, f32[4,128,256]{2,1,0:T(8,128)S(1)}, f32[16,4,64,256]{3,2,1,0:T(8,128)}, f32[16,4,64,128]{3,2,1,0:T(8,128)}, f32[16,4,128,128]{2,3,1...) while((s32[]{:T(128)}, f32[4,128,256]{2,1,0:T(8,128)S(1)}, ...), condition=%wide.region_15.16_spmd.clone, body=%wide.region_14.15_spmd.clone.sunk | while | flops 604504064 | bytes 6557864 | solution.py:132
  1837.6 65.7 %reduce-scatter.50.cloned.1.call-done = bf16[176,2048]{1,0:T(8,128)(2,1)} async-done(((bf16[1408,2048]{1,0:T(8,128)(2,1)}), bf16[176,2048]{1,0:T(8,128)(2,1)}) %reduce-scatter.50.cloned.1.call-update) | async-done | bytes 720912 | tf_op jit(solution)/shard_map/reduce_scatter | solution.py:383
  1905.6 62.5 %reduce-scatter.58.cloned.1.call-done = bf16[64,4]{1,0:T(8,128)(2,1)} async-done(((bf16[512,4]{1,0:T(8,128)(2,1)}), bf16[64,4]{1,0:T(8,128)(2,1)}) %reduce-scatter.58.cloned.1.call-update) | async-done | bytes 528
  1969.6 62.6 %reduce-scatter.60.cloned.1.call-done = bf16[64,4]{1,0:T(8,128)(2,1)} async-done(((bf16[512,4]{1,0:T(8,128)(2,1)}), bf16[64,4]{1,0:T(8,128)(2,1)}) %reduce-scatter.60.cloned.1.call-update) | async-done | bytes 528
  2033.6 63.1 %reduce-scatter.62.cloned.1.call-done = bf16[128,4]{1,0:T(8,128)(2,1)} async-done(((bf16[1024,4]{1,0:T(8,128)(2,1)}), bf16[128,4]{1,0:T(8,128)(2,1)}) %reduce-scatter.62.cloned.1.call-update) | async-done | bytes 1040
  2098.2 62.7 %reduce-scatter.54.cloned.1.call-done = bf16[64,16]{1,0:T(8,128)(2,1)} async-done(((bf16[512,16]{1,0:T(8,128)(2,1)}), bf16[64,16]{1,0:T(8,128)(2,1)}) %reduce-scatter.54.cloned.1.call-update) | async-done | bytes 2064
  2162.3 69.4 %reduce-scatter.38.cloned.1.call-done = bf16[2048,64]{0,1:T(8,128)(2,1)} async-done(((bf16[2048,512]{0,1:T(8,128)(2,1)}), bf16[2048,64]{0,1:T(8,128)(2,1)}) %reduce-scatter.38.cloned.1.call-update) | async-done | bytes 262160 | tf_op jit(solution)/shard_map/reduce_scatter | solution.py:344
  2233.4 68.8 %reduce-scatter.40.cloned.1.call-done = bf16[2048,64]{0,1:T(8,128)(2,1)} async-done(((bf16[2048,512]{0,1:T(8,128)(2,1)}), bf16[2048,64]{0,1:T(8,128)(2,1)}) %reduce-scatter.40.cloned.1.call-update) | async-done | bytes 262160 | tf_op jit(solution)/shard_map/reduce_scatter | solution.py:347
  2304.0 44.4 %reduce-scatter.36.cloned.1.call-done = bf16[256,2048]{1,0:T(8,128)(2,1)} async-done(((bf16[1024,2048]{1,0:T(8,128)(2,1)}), bf16[256,2048]{1,0:T(8,128)(2,1)}) %reduce-scatter.36.cloned.1.call-update) | async-done | bytes 1048592 | tf_op jit(solution)/shard_map/reduce_scatter | solution.py:172
  2357.1 82.9 %reduce-scatter.52.cloned.1.call-done = bf16[128,2048]{1,0:T(8,128)(2,1)} async-done(((bf16[1024,2048]{1,0:T(8,128)(2,1)}), bf16[128,2048]{1,0:T(8,128)(2,1)}) %reduce-scatter.52.cloned.1.call-update) | async-done | bytes 524304
  2444.1 87.4 %reduce-scatter.56.cloned.1.call-done = bf16[128,2048]{1,0:T(8,128)(2,1)} async-done(((bf16[1024,2048]{1,0:T(8,128)(2,1)}), bf16[128,2048]{1,0:T(8,128)(2,1)}) %reduce-scatter.56.cloned.1.call-update) | async-done | bytes 524304
  2535.7 87.1 %reduce-scatter.44.cloned.1.call-done = bf16[128,2048]{1,0:T(8,128)(2,1)} async-done(((bf16[1024,2048]{1,0:T(8,128)(2,1)}), bf16[128,2048]{1,0:T(8,128)(2,1)}) %reduce-scatter.44.cloned.1.call-update) | async-done | bytes 524304 | tf_op jit(solution)/shard_map/reduce_scatter | solution.py:371
  2624.9 20.2 all-reduce.25
  2646.9 22.9 reduce-scatter.32.cloned.1.call-done
  (639 shorter events, 896.7 us)
Async XLA Ops:
  7.2 143.3 %all-gather.19.cloned.1.call-start = ((), (), s32[]{:S(2)}) async-start(), calls=%async_computation.17 | async-start | bytes 5242880 | tf_op jit(solution)/shard_map/all_gather | solution.py:164
  46.0 109.1 %all-gather.23.cloned.1.call-start = ((), (), s32[]{:S(2)}) async-start(), calls=%async_computation.19 | async-start | bytes 2359296 | tf_op jit(solution)/shard_map/all_gather | solution.py:224
  46.8 132.7 %all-gather.21.cloned.1.call-start = ((), (), s32[]{:S(2)}) async-start(), calls=%async_computation.18 | async-start | bytes 2359296 | tf_op jit(solution)/shard_map/all_gather | solution.py:223
  47.5 207.4 %all-gather.25.cloned.1.call-start = ((), (), s32[]{:S(2)}) async-start(), calls=%async_computation.20 | async-start | bytes 4718592 | tf_op jit(solution)/shard_map/all_gather | solution.py:225
  48.1 680.9 %all-gather.27.cloned.1.call-start = ((), (), s32[]{:S(2)}) async-start(), calls=%async_computation.21 | async-start | bytes 4718592 | tf_op jit(solution)/shard_map/all_gather | solution.py:227
  48.7 704.1 %all-gather.29.cloned.1.call-start = ((), (), s32[]{:S(2)}) async-start(), calls=%async_computation.22 | async-start | bytes 4718592 | tf_op jit(solution)/shard_map/all_gather | solution.py:232
  49.3 755.8 %reduce-scatter.30.cloned.1.call-start = ((), (), s32[]{:S(2)}) async-start(), calls=%async_computation.23 | async-start | bytes 5242880 | tf_op jit(solution)/shard_map/reduce_scatter | solution.py:172
  49.4 563.4 %copy-start.52 = (pred[64,64]{1,0:T(8,128)(4,1)}, pred[64,64]{1,0:T(8,128)(4,1)S(1)}, u32[]{:S(2)}) copy-start(pred[64,64]{1,0:T(8,128)(4,1)S(1)} %get-tuple-element.522) | copy-start | bytes 12292
  762.2 137.9 %all-gather.33.cloned.1.call-start = ((), (), s32[]{:S(2)}) async-start(), calls=%async_computation.25 | async-start | bytes 6488064 | tf_op jit(solution)/shard_map/all_gather | solution.py:234
  762.9 172.1 %all-gather.31.cloned.1.call-start = ((), (), s32[]{:S(2)}) async-start(), calls=%async_computation.24 | async-start | bytes 5242880 | tf_op jit(solution)/shard_map/all_gather | solution.py:164
  809.3 220.7 %all-gather.35.cloned.1.call-start = ((), (), s32[]{:S(2)}) async-start(), calls=%async_computation.26 | async-start | bytes 6488064 | tf_op jit(solution)/shard_map/all_gather | solution.py:235
  809.9 254.4 %all-gather.41.cloned.1.call-start = ((), (), s32[]{:S(2)}) async-start(), calls=%async_computation.39 | async-start | bytes 5242880 | tf_op jit(solution)/shard_map/all_gather | solution.py:164
  810.7 348.6 %all-gather.37.cloned.1.call-start = ((), (), s32[]{:S(2)}) async-start(), calls=%async_computation.27 | async-start | bytes 6488064 | tf_op jit(solution)/shard_map/all_gather | solution.py:236
  811.2 426.0 %reduce-scatter.34.cloned.1.call-start = ((), (), s32[]{:S(2)}) async-start(), calls=%async_computation.29 | async-start | bytes 5242880 | tf_op jit(solution)/shard_map/reduce_scatter | solution.py:172
  1194.4 84.3 %all-gather.39.cloned.1.call-start = ((), (), s32[]{:S(2)}) async-start(), calls=%async_computation.30 | async-start | bytes 5242880 | tf_op jit(solution)/shard_map/all_gather | solution.py:164
  1244.1 463.8 %reduce-scatter.42.cloned.1.call-start = ((), (), s32[]{:S(2)}) async-start(), calls=%async_computation.34 | async-start | bytes 81920 | tf_op jit(solution)/shard_map/reduce_scatter | solution.py:172
  1542.2 290.6 %reduce-scatter.46.cloned.1.call-start = ((), (), s32[]{:S(2)}) async-start(), calls=%async_computation.36 | async-start | bytes 6488064 | tf_op jit(solution)/shard_map/reduce_scatter | solution.py:377
  1552.7 282.4 %reduce-scatter.48.cloned.1.call-start = ((), (), s32[]{:S(2)}) async-start(), calls=%async_computation.37 | async-start | bytes 6488064 | tf_op jit(solution)/shard_map/reduce_scatter | solution.py:380
  1563.3 340.0 %reduce-scatter.50.cloned.1.call-start = ((), (), s32[]{:S(2)}) async-start(), calls=%async_computation.38 | async-start | bytes 6488064 | tf_op jit(solution)/shard_map/reduce_scatter | solution.py:383
  1573.9 394.3 %reduce-scatter.58.cloned.1.call-start = ((), (), s32[]{:S(2)}) async-start(), calls=%async_computation.43 | async-start | bytes 147456
  1682.4 349.8 %reduce-scatter.60.cloned.1.call-start = ((), (), s32[]{:S(2)}) async-start(), calls=%async_computation.44 | async-start | bytes 147456
  1697.4 399.3 %reduce-scatter.62.cloned.1.call-start = ((), (), s32[]{:S(2)}) async-start(), calls=%async_computation.45 | async-start | bytes 294912
  1698.4 462.5 %reduce-scatter.54.cloned.1.call-start = ((), (), s32[]{:S(2)}) async-start(), calls=%async_computation.41 | async-start | bytes 147456
  1709.4 522.2 %reduce-scatter.38.cloned.1.call-start = ((), (), s32[]{:S(2)}) async-start(), calls=%async_computation.32 | async-start | bytes 2359296 | tf_op jit(solution)/shard_map/reduce_scatter | solution.py:344
  1715.7 586.5 %reduce-scatter.40.cloned.1.call-start = ((), (), s32[]{:S(2)}) async-start(), calls=%async_computation.33 | async-start | bytes 2359296 | tf_op jit(solution)/shard_map/reduce_scatter | solution.py:347
  1735.9 612.5 %reduce-scatter.36.cloned.1.call-start = ((), (), s32[]{:S(2)}) async-start(), calls=%async_computation.31 | async-start | bytes 5242880 | tf_op jit(solution)/shard_map/reduce_scatter | solution.py:172
  1774.3 665.6 %reduce-scatter.52.cloned.1.call-start = ((), (), s32[]{:S(2)}) async-start(), calls=%async_computation.40 | async-start | bytes 4718592
  1791.0 740.5 %reduce-scatter.56.cloned.1.call-start = ((), (), s32[]{:S(2)}) async-start(), calls=%async_computation.42 | async-start | bytes 4718592
  1807.5 815.3 %reduce-scatter.44.cloned.1.call-start = ((), (), s32[]{:S(2)}) async-start(), calls=%async_computation.35 | async-start | bytes 4718592 | tf_op jit(solution)/shard_map/reduce_scatter | solution.py:371
  1817.3 852.5 %reduce-scatter.32.cloned.1.call-start = ((), (), s32[]{:S(2)}) async-start(), calls=%async_computation.28 | async-start | bytes 5242880 | tf_op jit(solution)/shard_map/reduce_scatter | solution.py:172
  1830.1 518.3 %copy-start.6 = (bf16[1,256,2048]{2,1,0:T(8,128)(2,1)S(1)}, bf16[1,256,2048]{2,1,0:T(8,128)(2,1)}, u32[]{:S(2)}) copy-start(bf16[1,256,2048]{2,1,0:T(8,128)(2,1)} %param.22) | copy-start | bytes 3145732
  1830.1 518.3 %copy-start.71 = (f32[4,1,512]{2,1,0:T(1,128)S(1)}, f32[4,1,512]{2,1,0:T(1,128)}, u32[]{:S(2)}) copy-start(f32[4,1,512]{2,1,0:T(1,128)} %copy-done.70) | copy-start | bytes 24580
  (108 other events, 7448.2 us)
Sparse Core Ops, SparseCore 0:
  46.1 31.7 all-gather.18
  80.0 49.5 all-gather.22
  131.7 47.7 all-gather.20
  181.4 73.4 all-gather.24
  256.8 73.4 all-gather.26
  332.4 73.0 all-gather.28
  762.3 42.7 reduce-scatter.29
  807.5 92.6 all-gather.32
  902.4 32.6 all-gather.30
  937.3 92.6 all-gather.34
  1031.6 32.6 all-gather.40
  1066.6 92.6 all-gather.36
  1194.5 42.6 reduce-scatter.33
  1244.2 34.4 all-gather.38
  1542.3 19.4 reduce-scatter.41
  1565.7 109.9 reduce-scatter.45
  1679.7 109.7 reduce-scatter.47
  1793.5 109.7 reduce-scatter.49
  1907.5 60.6 reduce-scatter.57
  1972.3 59.8 reduce-scatter.59
  2036.5 60.2 reduce-scatter.61
  2101.0 59.8 reduce-scatter.53
  2164.8 66.7 reduce-scatter.37
  2235.4 66.6 reduce-scatter.39
  2304.9 43.4 reduce-scatter.35
  2351.8 88.0 reduce-scatter.51
  2443.9 87.6 reduce-scatter.55
  2535.2 87.6 reduce-scatter.43
  2625.5 44.2 reduce-scatter.31
where the time goes:
time: 2690 us; the launch traced here: 2680 us
  waiting for transfers between devices  1310 us (49%)
  matrix products  539 us (20%)
  other arithmetic  492 us (18%)
  blocking collectives  158 us (6%)
  local copies, waits for them, and re-layouts  156 us (6%)
    unnamed x35, waiting for transfers between devices  427 us
    another operation x5, other arithmetic, stretch_parts(): jax.scipy.linalg.solve_triangular(system, right_side, lower=True, unit_di...  318 us
    reduce_scatter x5, waiting for transfers between devices, seq_sums(): lax.psum_scatter(shortened(members), 'seq', scatter_dimension=0, tiled=True)  147 us
    dot_general x48, matrix products, follow(): jnp.einsum('gtn,gnq->gtq', initial_query, prefix_increment, precision=FUL...  100 us
    all_gather x1, waiting for transfers between devices, heads_layout(): lax.all_gather(feed_down, 'batch', axis=0, tiled=True)  95 us
    all_gather x4, waiting for transfers between devices, seq_rows(): lax.all_gather(shortened(members), 'seq', axis=0, tiled=True)  92.1 us
    dot_general x48, matrix products, follow(): jnp.einsum('zrm,zmd->zrd', state_transition, prefix_increment, precision=...  90.8 us
    all_gather x1, waiting for transfers between devices, heads_layout(): lax.all_gather(feed_gate, 'batch', axis=1, tiled=True)  88.9 us
  transfers between devices with their start and end apart: 29, of which 22 were waited for; matrix products, arithmetic and copies ran while one was open for 32% of the time, Pallas kernels for 0%

commit v1 on v0

v1 whole, which is shorter than its diff:
```python
import functools

import jax
import jax.numpy as jnp
from jax import lax
from jax.experimental import pallas as pl
from jax.experimental.pallas import tpu as pltpu
from jax.sharding import PartitionSpec as P

H = 16
DK = 128
DV = 256
CHUNK = 128
KERNEL = 4
HALO = 16
EPS_NORM = 1e-05
EPS_UNIT = 1e-06
F32 = jnp.float32
BF16 = jnp.bfloat16


def mm(a, b):
    return jnp.dot(a.astype(BF16), b.astype(BF16), preferred_element_type=F32)


def mm_nt(a, b):
    return lax.dot_general(
        a.astype(BF16), b.astype(BF16), (((1,), (1,)), ((), ())), preferred_element_type=F32
    )


def mm_tn(a, b):
    return lax.dot_general(
        a.astype(BF16), b.astype(BF16), (((0,), (0,)), ((), ())), preferred_element_type=F32
    )


def split_pair(a):
    high = a.astype(BF16)
    return high, (a - high.astype(F32)).astype(BF16)


def mm_fine(a, b):
    a_high, a_low = split_pair(a)
    b_high, b_low = split_pair(b)
    return (
        jnp.dot(a_high, b_high, preferred_element_type=F32)
        + jnp.dot(a_high, b_low, preferred_element_type=F32)
        + jnp.dot(a_low, b_high, preferred_element_type=F32)
    )


def sigmoid(v):
    return 1.0 / (1.0 + jnp.exp(-v))


def conv_cols(ext, seq, start, width, taps, rows):
    total = None
    for tap in range(KERNEL):
        term = taps[tap : tap + 1, start : start + width] * ext[
            seq, pl.ds(8 - (KERNEL - 1) + tap, rows), start : start + width
        ]
        total = term if total is None else total + term
    return total


def lower_masks(rows):
    row = lax.broadcasted_iota(jnp.int32, (rows, rows), 0)
    col = lax.broadcasted_iota(jnp.int32, (rows, rows), 1)
    return row, col


def inverse_many(couplings, row, col):
    rows = row.shape[0]
    eye = (row == col).astype(F32)
    pair = (row // 2 == col // 2)
    out = [eye - jnp.where(pair, a, 0.0) for a in couplings]
    size = 2
    while size < rows:
        mask = (row // (2 * size) == col // (2 * size)) & (row // size != col // size)
        inner = [mm_fine(jnp.where(mask, a, 0.0), t) for a, t in zip(couplings, out)]
        out = [t - mm_fine(t, i) for t, i in zip(out, inner)]
        size *= 2
    return out


def forward_body(
    heads, place, pre, gate, cols, rows_g, taps, gain, mixed, outs, fresh, starts, solved, ext, state
):
    chunk = pl.program_id(0)
    count = pre.shape[1]
    key_all = heads * DK

    @pl.when(chunk == 0)
    def _():
        ext[:, 0:8, :] = jnp.zeros((2, 8, ext.shape[2]), F32)
        state[...] = jnp.zeros(state.shape, F32)

    row, col = lower_masks(count)
    streams = [(seq, head) for seq in range(2) for head in range(heads)]
    for seq in range(2):
        ext[seq, 8 : 8 + count, :] = pre[seq].astype(F32)
    queries, keys, values, ratios, couplings = [], [], [], [], []
    for seq, head in streams:
        q = conv_cols(ext, seq, head * DK, DK, taps, count)
        q = q * sigmoid(q)
        q = q * lax.rsqrt(jnp.sum(q * q, axis=1, keepdims=True) + EPS_UNIT)
        k = conv_cols(ext, seq, key_all + head * DK, DK, taps, count)
        k = k * sigmoid(k)
        k = k * lax.rsqrt(jnp.sum(k * k, axis=1, keepdims=True) + EPS_UNIT)
        v = conv_cols(ext, seq, 2 * key_all + head * DV, DV, taps, count)
        v = v * sigmoid(v)
        queries.append(q.astype(BF16))
        keys.append(k.astype(BF16))
        values.append(v.astype(BF16))
        g_col = cols[seq, :, 4 * head + 1 : 4 * head + 2]
        g_row = rows_g[seq, 0, head : head + 1, :]
        ratio = jnp.where(row >= col, jnp.exp(jnp.minimum(g_col - g_row, 0.0)), 0.0)
        ratios.append(ratio)
        beta = cols[seq, :, 4 * head : 4 * head + 1]
        couplings.append(jnp.where(row > col, beta * ratio * mm_nt(keys[-1], keys[-1]), 0.0))
    for seq in range(2):
        ext[seq, 0:8, :] = ext[seq, count : count + 8, :]
    inverses = inverse_many(couplings, row, col)
    for at, (seq, head) in enumerate(streams):
        q, k, v, ratio = queries[at], keys[at], values[at], ratios[at]
        beta = cols[seq, :, 4 * head : 4 * head + 1]
        grown = cols[seq, :, 4 * head + 2 : 4 * head + 3]
        fade = cols[seq, :, 4 * head + 3 : 4 * head + 4]
        held = state[at]
        held_low = held.astype(BF16)
        starts[0, at] = held_low
        inverse = inverses[at].astype(BF16)
        solved[0, at] = inverse
        right = beta * (v.astype(F32) - grown * mm(k, held_low))
        news = mm(inverse, right).astype(BF16)
        scores = ratio * mm_nt(q, k)
        out = mm(scores, news) + grown * mm(q, held_low)
        last = jnp.exp(rows_g[seq, 0, head : head + 1, count - 1 : count])
        state[at] = last * held + mm_tn(fade * k.astype(F32), news)
        place_v = slice(head * DV, head * DV + DV)
        fresh[seq, :, place_v] = news
        outs[seq, :, place_v] = out.astype(BF16)
        scale = lax.rsqrt(jnp.mean(out * out, axis=1, keepdims=True) + EPS_NORM)
        g = gate[seq, :, place_v].astype(F32)
        mixed[seq, :, place_v] = (out * scale * gain[0:1, :] * (g * sigmoid(g))).astype(BF16)


def backward_body(
    heads,
    place,
    pre,
    halo,
    d_outs,
    cols,
    rows_g,
    taps,
    fresh,
    starts,
    solved,
    d_pre,
    d_beta,
    d_taps,
    ext,
    d_ext,
    d_state,
):
    step = pl.program_id(0)
    chunk = pl.num_programs(0) - 1 - step
    count = pre.shape[1]
    key_all = heads * DK

    @pl.when(step == 0)
    def _():
        d_ext[:, count : count + 8, :] = jnp.zeros((2, 8, d_ext.shape[2]), F32)
        d_state[...] = jnp.zeros(d_state.shape, F32)
        d_taps[...] = jnp.zeros(d_taps.shape, F32)

    row, col = lower_masks(count)
    streams = [(seq, head) for seq in range(2) for head in range(heads)]
    keep = jnp.where(chunk > 0, 1.0, 0.0)
    for seq in range(2):
        ext[seq, 0:8, :] = keep * halo[seq].astype(F32)[HALO - 8 : HALO, :]
        ext[seq, 8 : 8 + count, :] = pre[seq].astype(F32)
    d_betas = []
    for at, (seq, head) in enumerate(streams):
        beta = cols[seq, :, 4 * head : 4 * head + 1]
        g_col = cols[seq, :, 4 * head + 1 : 4 * head + 2]
        grown = cols[seq, :, 4 * head + 2 : 4 * head + 3]
        fade = cols[seq, :, 4 * head + 3 : 4 * head + 4]
        g_row = rows_g[seq, 0, head : head + 1, :]
        last = jnp.exp(g_row[:, count - 1 : count])

        q_conv = conv_cols(ext, seq, head * DK, DK, taps, count)
        q_sig = sigmoid(q_conv)
        q_act = q_conv * q_sig
        q_scale = lax.rsqrt(jnp.sum(q_act * q_act, axis=1, keepdims=True) + EPS_UNIT)
        q_unit = q_act * q_scale
        k_conv = conv_cols(ext, seq, key_all + head * DK, DK, taps, count)
        k_sig = sigmoid(k_conv)
        k_act = k_conv * k_sig
        k_scale = lax.rsqrt(jnp.sum(k_act * k_act, axis=1, keepdims=True) + EPS_UNIT)
        k_unit = k_act * k_scale
        v_conv = conv_cols(ext, seq, 2 * key_all + head * DV, DV, taps, count)
        v_sig = sigmoid(v_conv)
        q, k = q_unit.astype(BF16), k_unit.astype(BF16)
        v = (v_conv * v_sig).astype(BF16).astype(F32)
        k_full = k.astype(F32)

        place_v = slice(head * DV, head * DV + DV)
        d_out = d_outs[seq, :, place_v]
        news = fresh[seq, :, place_v]
        held = starts[0, at]
        inverse = solved[0, at]
        d_held = d_state[at]
        d_held_low = d_held.astype(BF16)
        ratio = jnp.where(row >= col, jnp.exp(jnp.minimum(g_col - g_row, 0.0)), 0.0)
        scores = ratio * mm_nt(q, k)
        d_news = mm_tn(scores, d_out) + mm(fade * k_full, d_held_low)
        d_right = mm_tn(inverse, d_news)
        d_right_low = d_right.astype(BF16)
        d_couple = jnp.where(row > col, -ratio * mm_nt(d_right_low, news), 0.0)
        key_key = mm_nt(k, k)
        d_kk = beta * d_couple
        d_scores = ratio * mm_nt(d_out, news)
        out_held = mm_nt(d_out, held)
        right_held = mm_nt(d_right_low, held)
        news_held = mm_nt(news, d_held_low)
        d_q = mm(d_scores, k) + grown * out_held
        d_k = (
            mm_tn(d_scores, q)
            + mm(d_kk, k)
            + mm_tn(d_kk, k)
            + fade * news_held
            - (beta * grown) * right_held
        )
        d_v = beta * d_right
        d_betas.append(
            jnp.sum(d_right * v, axis=1, keepdims=True)
            - grown * jnp.sum(right_held * k_full, axis=1, keepdims=True)
            + jnp.sum(d_couple * key_key, axis=1, keepdims=True)
        )
        d_state[at] = (
            last * d_held
            + mm_tn(grown * q.astype(F32), d_out)
            - mm_tn((beta * grown) * k_full, d_right_low)
        )
        d_qa = q_scale * (d_q - q_unit * jnp.sum(q_unit * d_q, axis=1, keepdims=True))
        d_ka = k_scale * (d_k - k_unit * jnp.sum(k_unit * d_k, axis=1, keepdims=True))
        d_ext[seq, 0:count, head * DK : head * DK + DK] = d_qa * (
            q_sig * (1.0 + q_conv * (1.0 - q_sig))
        )
        d_ext[seq, 0:count, key_all + head * DK : key_all + head * DK + DK] = d_ka * (
            k_sig * (1.0 + k_conv * (1.0 - k_sig))
        )
        d_ext[
            seq, 0:count, 2 * key_all + head * DV : 2 * key_all + head * DV + DV
        ] = d_v * (v_sig * (1.0 + v_conv * (1.0 - v_sig)))
    for seq in range(2):
        for head in range(heads):
            beta = cols[seq, :, 4 * head : 4 * head + 1]
            d_beta[seq, :, head : head + 1] = d_betas[seq * heads + head] * beta * (1.0 - beta)
        wide = ext.shape[2]
        for start in range(0, wide, 128):
            span = slice(start, start + 128)
            total = None
            near = d_ext[seq, 0:count, span]
            for tap in range(KERNEL):
                term = taps[tap : tap + 1, span] * d_ext[seq, pl.ds(KERNEL - 1 - tap, count), span]
                total = term if total is None else total + term
                moved = ext[seq, pl.ds(8 - (KERNEL - 1) + tap, count), span]
                d_taps[tap : tap + 1, span] += jnp.sum(near * moved, axis=0, keepdims=True)
            d_pre[seq, :, span] = total.astype(BF16)
        d_ext[seq, count : count + 8, :] = d_ext[seq, 0:8, :]


def gating_body(heads, d_mixed_a, d_mixed_b, outs, gate, gain, d_outs, d_gate, d_gain):
    @pl.when(pl.program_id(0) == 0)
    def _():
        d_gain[...] = jnp.zeros(d_gain.shape, F32)

    total = None
    for seq, d_mixed in ((0, d_mixed_a), (1, d_mixed_b)):
        for head in range(heads):
            span = slice(head * DV, head * DV + DV)
            out = outs[seq, :, span].astype(F32)
            grad = d_mixed[:, span].astype(F32)
            g = gate[seq, :, span].astype(F32)
            sig = sigmoid(g)
            scale = lax.rsqrt(jnp.mean(out * out, axis=1, keepdims=True) + EPS_NORM)
            unit = out * scale
            cot = grad * (g * sig)
            term = jnp.sum(cot * unit, axis=0, keepdims=True)
            total = term if total is None else total + term
            scaled = cot * gain[0:1, :]
            d_outs[seq, :, span] = (
                scale * (scaled - unit * jnp.mean(unit * scaled, axis=1, keepdims=True))
            ).astype(BF16)
            d_gate[seq, :, span] = (
                grad * unit * gain[0:1, :] * (sig * (1.0 + g * (1.0 - sig)))
            ).astype(BF16)
    d_gain[0:1, :] += total


def chunk_place(chunk, place, per_piece):
    piece = chunk // per_piece
    return jnp.bitwise_xor(piece, place[0]) * per_piece + chunk % per_piece


def run_forward(place, piece_rows, pre, gate, cols, rows_g, taps, gain):
    _, length, wide = pre.shape
    heads = gate.shape[2] // DV
    chunks = length // CHUNK
    per_piece = piece_rows // CHUNK

    def by_rows(width):
        return pl.BlockSpec(
            (2, CHUNK, width), lambda c, at: (0, chunk_place(c, at, per_piece), 0)
        )

    grid_spec = pltpu.PrefetchScalarGridSpec(
        num_scalar_prefetch=1,
        grid=(chunks,),
        in_specs=[
            by_rows(wide),
            by_rows(heads * DV),
            by_rows(4 * heads),
            pl.BlockSpec(
                (2, 1, heads, CHUNK), lambda c, at: (0, chunk_place(c, at, per_piece), 0, 0)
            ),
            pl.BlockSpec((8, wide), lambda c, at: (0, 0)),
            pl.BlockSpec((1, DV), lambda c, at: (0, 0)),
        ],
        out_specs=[
            by_rows(heads * DV),
            by_rows(heads * DV),
            by_rows(heads * DV),
            pl.BlockSpec((1, 2 * heads, DK, DV), lambda c, at: (c, 0, 0, 0)),
            pl.BlockSpec((1, 2 * heads, CHUNK, CHUNK), lambda c, at: (c, 0, 0, 0)),
        ],
        scratch_shapes=[
            pltpu.VMEM((2, CHUNK + 8, wide), F32),
            pltpu.VMEM((2 * heads, DK, DV), F32),
        ],
    )
    rows_out = jax.ShapeDtypeStruct((2, length, heads * DV), BF16)
    return pl.pallas_call(
        functools.partial(forward_body, heads),
        grid_spec=grid_spec,
        out_shape=[
            rows_out,
            rows_out,
            rows_out,
            jax.ShapeDtypeStruct((chunks, 2 * heads, DK, DV), BF16),
            jax.ShapeDtypeStruct((chunks, 2 * heads, CHUNK, CHUNK), BF16),
        ],
        compiler_params=pltpu.CompilerParams(
            dimension_semantics=("arbitrary",), vmem_limit_bytes=40 * 1024 * 1024
        ),
        name="delta_forward",
    )(place, pre, gate, cols, rows_g, taps, gain)


def run_backward(place, piece_rows, pre, d_outs, cols, rows_g, taps, fresh, starts, solved):
    _, length, wide = pre.shape
    heads = d_outs.shape[2] // DV
    chunks = length // CHUNK
    per_piece = piece_rows // CHUNK
    per_halo = CHUNK // HALO

    def turned(step):
        return chunks - 1 - step

    def by_rows(width):
        return pl.BlockSpec(
            (2, CHUNK, width), lambda c, at: (0, chunk_place(turned(c), at, per_piece), 0)
        )

    def halo_place(step, at):
        before = jnp.maximum(turned(step) - 1, 0)
        return (0, chunk_place(before, at, per_piece) * per_halo + per_halo - 1, 0)

    grid_spec = pltpu.PrefetchScalarGridSpec(
        num_scalar_prefetch=1,
        grid=(chunks,),
        in_specs=[
            by_rows(wide),
            pl.BlockSpec((2, HALO, wide), halo_place),
            by_rows(heads * DV),
            by_rows(4 * heads),
            pl.BlockSpec(
                (2, 1, heads, CHUNK),
                lambda c, at: (0, chunk_place(turned(c), at, per_piece), 0, 0),
            ),
            pl.BlockSpec((8, wide), lambda c, at: (0, 0)),
            by_rows(heads * DV),
            pl.BlockSpec((1, 2 * heads, DK, DV), lambda c, at: (turned(c), 0, 0, 0)),
            pl.BlockSpec((1, 2 * heads, CHUNK, CHUNK), lambda c, at: (turned(c), 0, 0, 0)),
        ],
        out_specs=[
            by_rows(wide),
            by_rows(heads),
            pl.BlockSpec((8, wide), lambda c, at: (0, 0)),
        ],
        scratch_shapes=[
            pltpu.VMEM((2, CHUNK + 8, wide), F32),
            pltpu.VMEM((2, CHUNK + 8, wide), F32),
            pltpu.VMEM((2 * heads, DK, DV), F32),
        ],
    )
    return pl.pallas_call(
        functools.partial(backward_body, heads),
        grid_spec=grid_spec,
        out_shape=[
            jax.ShapeDtypeStruct((2, length, wide), BF16),
            jax.ShapeDtypeStruct((2, length, heads), F32),
            jax.ShapeDtypeStruct((8, wide), F32),
        ],
        compiler_params=pltpu.CompilerParams(
            dimension_semantics=("arbitrary",), vmem_limit_bytes=40 * 1024 * 1024
        ),
        name="delta_backward",
    )(place, pre, pre, d_outs, cols, rows_g, taps, fresh, starts, solved)


def run_gating(d_mixed_a, d_mixed_b, outs, gate, gain):
    _, length, wide = outs.shape
    heads = wide // DV
    tile = 256
    both = pl.BlockSpec((2, tile, wide), lambda c: (0, c, 0))
    one = pl.BlockSpec((tile, wide), lambda c: (c, 0))
    shape = jax.ShapeDtypeStruct((2, length, wide), BF16)
    return pl.pallas_call(
        functools.partial(gating_body, heads),
        grid=(length // tile,),
        in_specs=[one, one, both, both, pl.BlockSpec((1, DV), lambda c: (0, 0))],
        out_specs=[both, both, pl.BlockSpec((8, DV), lambda c: (0, 0))],
        out_shape=[shape, shape, jax.ShapeDtypeStruct((8, DV), F32)],
        compiler_params=pltpu.CompilerParams(
            dimension_semantics=("arbitrary",), vmem_limit_bytes=40 * 1024 * 1024
        ),
        name="gating_backward",
    )(d_mixed_a, d_mixed_b, outs, gate, gain)


def product(left_side, right_side):
    return jnp.dot(left_side, right_side, preferred_element_type=F32)


def product_tn(left_side, right_side):
    return lax.dot_general(
        left_side, right_side, (((0,), (0,)), ((), ())), preferred_element_type=F32
    )


def product_nt(left_side, right_side):
    return lax.dot_general(
        left_side, right_side, (((1,), (1,)), ((), ())), preferred_element_type=F32
    )


def rms_scale(values, gain_vals):
    return (
        values * lax.rsqrt(jnp.mean(values * values, axis=-1, keepdims=True) + EPS_NORM) * gain_vals
    )


def swap(values, axis, bit):
    count = lax.axis_size(axis)
    return lax.ppermute(values, axis, [(place, place ^ bit) for place in range(count)])


def bits_of(count):
    found = []
    bit = 1
    while bit < count:
        found.append(bit)
        bit *= 2
    return found


def after(values, *earlier):
    return lax.optimization_barrier((values, *earlier))[0]


def add_low(left_side, right_side):
    return (left_side.astype(F32) + right_side.astype(F32)).astype(BF16)


def spread_rows(own, team):
    seq_count = lax.axis_size("seq")

    def along_seq(first):
        pieces = {0: first}
        for offset in sorted(range(1, seq_count), key=lambda o: -(o & -o)):
            low = offset & -offset
            pieces[offset] = swap(pieces[offset ^ low], "seq", low)
        return [pieces[offset] for offset in range(seq_count)]

    other = swap(own, "batch", team)
    return along_seq(own), along_seq(other)


def sum_rows(part_own, part_other, team):
    seq_count = lax.axis_size("seq")
    rows = part_own.shape[0] // seq_count

    def along_seq(part):
        pieces = {at: part[at * rows : (at + 1) * rows] for at in range(seq_count)}
        for bit in bits_of(seq_count):
            for at in [place for place in pieces if place & bit]:
                came = swap(pieces.pop(at), "seq", bit)
                pieces[at ^ bit] = add_low(pieces[at ^ bit], came)
        return pieces[0]

    came = swap(along_seq(part_other), "batch", team)
    return along_seq(part_own).astype(F32) + came.astype(F32)


def spread_all(values):
    values = values[None]
    for axis in ("batch", "seq"):
        place = lax.axis_index(axis)
        for bit in bits_of(lax.axis_size(axis)):
            came = swap(values, axis, bit)
            values = jnp.where(
                (place & bit) == 0,
                jnp.concatenate([values, came], axis=0),
                jnp.concatenate([came, values], axis=0),
            )
    return values


def sum_all(values):
    for axis in ("seq", "batch"):
        place = lax.axis_index(axis)
        for bit in reversed(bits_of(lax.axis_size(axis))):
            half = values.shape[0] // 2
            upper = (place & bit) != 0
            keep = jnp.where(upper, values[half:], values[:half])
            send = jnp.where(upper, values[:half], values[half:])
            values = keep + swap(send, axis, bit)
    return values[0]


def local(
    tokens,
    decays,
    out_grad,
    mixer_gain,
    query_weight,
    key_weight,
    value_weight,
    beta_weight,
    outgate_weight,
    query_conv,
    key_conv,
    value_conv,
    head_gain,
    output_weight,
    feed_gain,
    feed_gate,
    feed_up,
    feed_down,
):
    seq_count = lax.axis_size("seq")
    batch_count = lax.axis_size("batch")
    seq_pos = lax.axis_index("seq")
    batch_pos = lax.axis_index("batch")
    devices = seq_count * batch_count
    team = devices // H
    heads = H // (2 * seq_count)
    offsets = [offset for offset in range(batch_count) if not offset & team]
    source = tokens[0]
    grad_own = out_grad[0]
    rows, model = source.shape
    length = rows * seq_count
    key_part = query_weight.shape[1]
    value_part = value_weight.shape[1]
    feed_part = feed_gate.shape[1]
    gain_part = mixer_gain.shape[0]
    head_part = head_gain.shape[0]

    small = jnp.concatenate(
        [mixer_gain, feed_gain, beta_weight.T.reshape(-1), head_gain], axis=0
    )
    small_size = small.shape[0]
    small = jnp.pad(small, (0, -small_size % 2048)).reshape(-1, 128)
    small_all = spread_all(small).reshape(devices, -1)
    gain_f = small_all[:, :gain_part].reshape(-1).astype(F32)
    feed_gain_f = small_all[:, gain_part : 2 * gain_part].reshape(-1).astype(F32)
    beta_rows = (
        small_all[:, 2 * gain_part : 2 * gain_part + H * gain_part]
        .reshape(devices, H, gain_part)
        .transpose(1, 0, 2)
        .reshape(H, model)
    )
    head_gain_all = small_all[:, small_size - head_part : small_size].reshape(-1)
    inner = batch_pos % team
    gain_blocks = head_gain_all.reshape(team, DV // team)
    head_gain_f = jnp.concatenate(
        [lax.dynamic_index_in_dim(gain_blocks, at ^ inner, 0, False) for at in range(team)], axis=0
    ).astype(F32)
    head_places = [
        seq_pos * (H // seq_count) + ((batch_pos // team) ^ (2 * head)) for head in range(heads)
    ]
    beta_own = jnp.stack(
        [lax.dynamic_index_in_dim(beta_rows, place, 0, False) for place in head_places], axis=0
    )

    taps_own = jnp.concatenate([query_conv, key_conv, value_conv], axis=1)
    taps_wide = taps_own.shape[1]
    taps_rows = jnp.pad(taps_own.reshape(-1), (0, -taps_own.size % (16 * model))).reshape(-1, model)
    shares = [
        jnp.concatenate([query_weight.T, key_weight.T, value_weight.T, taps_rows], axis=0),
        jnp.concatenate([outgate_weight.T, output_weight], axis=0),
        jnp.concatenate([feed_gate.T, feed_up.T], axis=0),
        feed_down,
    ]
    spread = []
    far_chain, near_chain = [], []
    for share in shares:
        pieces = {0: share}
        for offset in sorted(offsets[1:], key=lambda o: (-(o & -o), o)):
            low = offset & -offset
            chain = far_chain if low > team else near_chain
            send = pieces[offset ^ low]
            if len(chain) >= 2:
                send = after(send, chain[-2])
            pieces[offset] = swap(send, "batch", low)
            chain.append(pieces[offset])
        spread.append([pieces[offset] for offset in offsets])

    def joined(pieces, start, size):
        return [piece[start : start + size] for piece in pieces]

    mix_rows = jnp.concatenate(
        joined(spread[0], 0, key_part)
        + joined(spread[0], key_part, key_part)
        + joined(spread[0], 2 * key_part, value_part),
        axis=0,
    )
    taps_at = 2 * key_part + value_part
    taps_all = [
        piece[taps_at:].reshape(-1)[: KERNEL * taps_wide].reshape(KERNEL, taps_wide)
        for piece in spread[0]
    ]
    taps = jnp.concatenate(
        [piece[:, :key_part] for piece in taps_all]
        + [piece[:, key_part : 2 * key_part] for piece in taps_all]
        + [piece[:, 2 * key_part :] for piece in taps_all],
        axis=1,
    ).astype(F32)
    taps = jnp.pad(taps, ((0, 8 - KERNEL), (0, 0)))
    gate_rows = jnp.concatenate(joined(spread[1], 0, value_part), axis=0)
    out_rows = jnp.concatenate(joined(spread[1], value_part, value_part), axis=0)
    feed_rows = jnp.concatenate(
        joined(spread[2], 0, feed_part) + joined(spread[2], feed_part, feed_part), axis=0
    )
    down_rows = jnp.concatenate(spread[3], axis=0)
    feed_here = down_rows.shape[0]

    own_rows, other_rows = spread_rows(source, team)
    both_tokens = jnp.concatenate(own_rows + other_rows, axis=0)
    both_f = both_tokens.astype(F32)
    unit_f = both_f * lax.rsqrt(jnp.mean(both_f * both_f, axis=-1, keepdims=True) + EPS_NORM)
    normed = (unit_f * gain_f).astype(BF16)
    own_grads, other_grads = spread_rows(after(grad_own, other_rows[-1]), team)
    seq_grads = [jnp.concatenate(own_grads, axis=0), jnp.concatenate(other_grads, axis=0)]

    logs = jnp.log(decays[0])[None]
    logs = jnp.concatenate([logs, swap(logs, "batch", team)], axis=0)[:, None]
    for bit in bits_of(seq_count):
        logs = jnp.concatenate([logs, swap(logs, "seq", bit)], axis=1)
    head_logs = jnp.stack(
        [lax.dynamic_index_in_dim(logs, place, 2, False) for place in head_places], axis=1
    )
    chunks = length // CHUNK
    totals = jnp.cumsum(head_logs.reshape(2, heads, chunks, CHUNK), axis=-1)
    rows_g = totals.transpose(0, 2, 1, 3)
    totals_cols = totals.reshape(2, heads, length).transpose(0, 2, 1)
    fade_cols = (
        jnp.exp(totals[..., -1:] - totals).reshape(2, heads, length).transpose(0, 2, 1)
    )

    pre = product_nt(normed, mix_rows).astype(BF16).reshape(2, length, -1)
    beta_pre = product_nt(normed, beta_own).reshape(2, length, heads)
    gate_pre = product_nt(normed, gate_rows).astype(BF16).reshape(2, length, -1)
    cols = jnp.stack(
        [jax.nn.sigmoid(beta_pre), totals_cols, jnp.exp(totals_cols), fade_cols], axis=-1
    ).reshape(2, length, 4 * heads)
    place = jnp.full((1,), seq_pos, jnp.int32)
    gain_row = head_gain_f[None]
    mixed, head_outs, fresh, starts, solved = run_forward(
        place, rows, pre, gate_pre, cols, rows_g, taps, gain_row
    )
    branch = [product(mixed[at], out_rows).astype(BF16) for at in range(2)]
    source_f = source.astype(F32)
    middle = source_f + sum_rows(branch[0], branch[1], team)

    feed_in = rms_scale(middle, feed_gain_f).astype(BF16)
    own_feed, other_feed = spread_rows(feed_in, team)
    seq_feed = [jnp.concatenate(own_feed, axis=0), jnp.concatenate(other_feed, axis=0)]
    down_parts, feed_backs = [], []
    down_term, feed_term = 0.0, 0.0
    for feed, grad in zip(seq_feed, seq_grads):
        gate_vals = product_nt(feed_rows[:feed_here], feed)
        up_vals = product_nt(feed_rows[feed_here:], feed)
        gate_sig = jax.nn.sigmoid(gate_vals)
        hidden = (gate_vals * gate_sig * up_vals).astype(BF16)
        d_hidden = product_nt(down_rows, grad)
        d_gate = d_hidden * up_vals * gate_sig * (1.0 + gate_vals * (1.0 - gate_sig))
        d_up = d_hidden * gate_vals * gate_sig
        d_both = jnp.concatenate([d_gate.astype(BF16), d_up.astype(BF16)], axis=0)
        feed_backs.append(product_tn(d_both, feed_rows).astype(BF16))
        down_parts.append(product_tn(hidden, down_rows).astype(BF16))
        down_term = down_term + product(hidden, grad)
        feed_term = feed_term + product(d_both, feed)
    d_feed_in = sum_rows(feed_backs[0], feed_backs[1], team)
    feed_pull = jax.vjp(rms_scale, middle, feed_gain_f)[1]
    d_mid_norm, feed_gain_term = feed_pull(d_feed_in)
    d_middle = grad_own.astype(F32) + d_mid_norm
    d_branch = d_middle.astype(BF16)
    own_branch, other_branch = spread_rows(d_branch, team)
    both_branch = jnp.concatenate(own_branch + other_branch, axis=0)
    down_ready = [after(part, other_branch[-1]) for part in down_parts]
    block_out = (middle + sum_rows(down_ready[0], down_ready[1], team)).astype(BF16)[None]

    d_mixed = product_nt(both_branch, out_rows).astype(BF16)
    d_outs, d_gate_pre, head_gain_term = run_gating(
        d_mixed[:length], d_mixed[length:], head_outs, gate_pre, gain_row
    )
    d_pre, d_beta, d_taps = run_backward(
        place, rows, pre, d_outs, cols, rows_g, taps, fresh, starts, solved
    )
    d_beta_low = d_beta.astype(BF16)
    d_normed = [
        product(d_pre[at], mix_rows)
        + product(d_gate_pre[at], gate_rows)
        + product(d_beta_low[at], beta_own)
        for at in range(2)
    ]
    d_normed_low = [part.astype(BF16) for part in d_normed]

    output_term = product_tn(mixed.reshape(2 * length, -1), both_branch).astype(BF16)
    outgate_term = product_tn(d_gate_pre.reshape(2 * length, -1), normed).astype(BF16)
    mix_term = product_tn(d_pre.reshape(2 * length, -1), normed).astype(BF16)
    beta_term = product_tn(d_beta_low.reshape(2 * length, -1), normed)
    mixer_gain_term = sum(
        jnp.sum(d_normed[at] * unit_f[at * length : (at + 1) * length], axis=0) for at in range(2)
    )

    def collect(pieces):
        pieces = dict(zip(offsets, pieces))
        for bit in bits_of(batch_count):
            if bit == team:
                continue
            for offset in sorted((o for o in pieces if o & bit), reverse=True):
                came = swap(pieces.pop(offset), "batch", bit)
                left = pieces[offset ^ bit].astype(F32) + came.astype(F32)
                pieces[offset ^ bit] = left if offset == bit and len(pieces) == 1 else left.astype(BF16)
        return pieces[0]

    def cut(values, at, size):
        return values[at * size : (at + 1) * size]

    count = len(offsets)
    down_low = down_term.astype(BF16)
    feed_low = feed_term.astype(BF16)
    down_sum = collect([cut(down_low, at, feed_part) for at in range(count)])
    feed_sum = collect(
        [
            jnp.concatenate(
                [cut(feed_low[:feed_here], at, feed_part), cut(feed_low[feed_here:], at, feed_part)],
                axis=0,
            )
            for at in range(count)
        ]
    )
    gate_sum = collect(
        [
            jnp.concatenate(
                [cut(outgate_term, at, value_part), cut(output_term, at, value_part)], axis=0
            )
            for at in range(count)
        ]
    )
    key_here = count * key_part
    taps_low = d_taps[:KERNEL].astype(BF16)

    def taps_piece(at):
        flat = jnp.concatenate(
            [
                taps_low[:, at * key_part : (at + 1) * key_part],
                taps_low[:, key_here + at * key_part : key_here + (at + 1) * key_part],
                taps_low[:, 2 * key_here + at * value_part : 2 * key_here + (at + 1) * value_part],
            ],
            axis=1,
        ).reshape(-1)
        return jnp.pad(flat, (0, -flat.size % (16 * model))).reshape(-1, model)

    mix_sum = collect(
        [
            jnp.concatenate(
                [
                    cut(mix_term[:key_here], at, key_part),
                    cut(mix_term[key_here : 2 * key_here], at, key_part),
                    cut(mix_term[2 * key_here :], at, value_part),
                    taps_piece(at),
                ],
                axis=0,
            )
            for at in range(count)
        ]
    )
    taps_sum = mix_sum[taps_at:].reshape(-1)[: KERNEL * taps_wide].reshape(KERNEL, taps_wide)

    head_terms = head_gain_term[0].reshape(team, DV // team)
    head_terms = jnp.concatenate(
        [lax.dynamic_index_in_dim(head_terms, at ^ inner, 0, False) for at in range(team)], axis=0
    )
    beta_all = jnp.zeros((H, model), F32)
    for head in range(heads):
        beta_all = lax.dynamic_update_slice(
            beta_all, beta_term[head : head + 1], (head_places[head], jnp.int32(0))
        )
    small_terms = jnp.concatenate(
        [
            mixer_gain_term.reshape(devices, gain_part),
            feed_gain_term.reshape(devices, gain_part),
            beta_all.reshape(H, devices, gain_part).transpose(1, 0, 2).reshape(devices, -1),
            head_terms.reshape(devices, head_part),
        ],
        axis=1,
    )
    small_terms = jnp.pad(small_terms, ((0, 0), (0, -small_size % 1024)))
    small_sum = sum_all(small_terms.reshape(devices, -1, 128)).reshape(-1)
    beta_sum = small_sum[2 * gain_part : 2 * gain_part + H * gain_part].reshape(H, gain_part).T

    d_source = sum_rows(d_normed_low[0], d_normed_low[1], team)
    mixer_pull = jax.vjp(lambda vals: rms_scale(vals, gain_f), source_f)[1]
    tokens_grad = (d_middle + mixer_pull(d_source)[0]).astype(BF16)[None]

    return (
        block_out,
        tokens_grad,
        small_sum[:gain_part],
        mix_sum[:key_part].T,
        mix_sum[key_part : 2 * key_part].T,
        mix_sum[2 * key_part : taps_at].T,
        beta_sum,
        gate_sum[:value_part].T,
        taps_sum[:, :key_part],
        taps_sum[:, key_part : 2 * key_part],
        taps_sum[:, 2 * key_part :],
        small_sum[small_size - head_part : small_size],
        gate_sum[value_part:],
        small_sum[gain_part : 2 * gain_part],
        feed_sum[:feed_part].T,
        feed_sum[feed_part:].T,
        down_sum,
    )


def solution(mesh):
    in_specs = (
        P("batch", "seq", None),
        P("batch", None, "seq"),
        P("batch", "seq", None),
        P(("seq", "batch")),
        P(None, ("seq", "batch")),
        P(None, ("seq", "batch")),
        P(None, ("seq", "batch")),
        P(("seq", "batch"), None),
        P(None, ("seq", "batch")),
        P(None, ("seq", "batch")),
        P(None, ("seq", "batch")),
        P(None, ("seq", "batch")),
        P(("seq", "batch")),
        P(("seq", "batch"), None),
        P(("seq", "batch")),
        P(None, ("seq", "batch")),
        P(None, ("seq", "batch")),
        P(("seq", "batch"), None),
    )
    out_specs = (
        P("batch", "seq", None),
        P("batch", "seq", None),
        P(("seq", "batch")),
        P(None, ("seq", "batch")),
        P(None, ("seq", "batch")),
        P(None, ("seq", "batch")),
        P(("seq", "batch"), None),
        P(None, ("seq", "batch")),
        P(None, ("seq", "batch")),
        P(None, ("seq", "batch")),
        P(None, ("seq", "batch")),
        P(("seq", "batch")),
        P(("seq", "batch"), None),
        P(("seq", "batch")),
        P(None, ("seq", "batch")),
        P(None, ("seq", "batch")),
        P(("seq", "batch"), None),
    )
    return jax.shard_map(local, mesh=mesh, in_specs=in_specs, out_specs=out_specs, check_vma=False)
```

time: 2690 us -> 1100 us (0.41)
  waiting for transfers between devices: 1310 us -> 485 us
  other arithmetic: 492 us -> 81.3 us
  matrix products: 539 us -> 223 us
  blocking collectives: 158 us -> 0 us
  Pallas kernels: 0 us -> 92.5 us
  starting transfers between devices: 1.81 us -> 70.6 us
    ppermute x0 -> x93, waiting for transfers between devices: none -> 485 us  [swap(): lax.ppermute(values, axis, [(place, place ^ bit) for place in range(count)])]
    all_gather x12 -> x0, waiting for transfers between devices: 448 us -> none  [the longest x1 95 us: heads_layout(): lax.all_gather(feed_down, 'batch', axis=0, tiled=True)]
    reduce_scatter x11 -> x0, waiting for transfers between devices: 438 us -> none  [the longest x5 147 us: seq_sums(): lax.psum_scatter(shortened(members), 'seq', scatter_dimension=0, tiled=True)]
    unnamed x35 -> x0, waiting for transfers between devices: 427 us -> none
    another operation x9 -> x5, other arithmetic: 329 us -> 1.38 us  [the longest x1 1.32 us: local(): totals = jnp.cumsum(head_logs.reshape(2, heads, chunks, CHUNK), axis=-1)]
    dot_general x124 -> x12, matrix products: 366 us -> 88.5 us  [product(): return jnp.dot(left_side, right_side, preferred_element_type=F32)]
    all_gather x7 -> x0, blocking collectives: 97.2 us -> none  [the longest x1 30.6 us: heads_layout(): lax.all_gather(beta_weight, 'batch', axis=0, tiled=True)]
    pallas_call x0 -> x3, Pallas kernels: none -> 92.5 us  [the longest x1 46.8 us: run_backward(): pl.pallas_call(functools.partial(backward_body, heads), grid_spec=grid_sp...]
  transfers between devices with their start and end apart: 29 -> 93, of which waited for: 22 -> 35; matrix products, arithmetic and copies ran while one was open for 32% -> 33% of each run, Pallas kernels for 0% -> 4%
where the time goes in v1:
time: 1100 us
  waiting for transfers between devices  485 us (44%)
  matrix products  223 us (20%)
  local copies, waits for them, and re-layouts  140 us (13%)
  Pallas kernels  92.5 us (8%)
  other arithmetic  81.3 us (7%)
  starting transfers between devices  70.6 us (6%)
    ppermute x93, waiting for transfers between devices, swap(): lax.ppermute(values, axis, [(place, place ^ bit) for place in range(count)])  485 us
    dot_general x12, matrix products, product(): return jnp.dot(left_side, right_side, preferred_element_type=F32)  88.5 us
    unnamed x329, local copies, waits for them, and re-layouts  86.7 us
    dot_general x10, matrix products, product_nt(): lax.dot_general(left_side, right_side, (((1,), (1,)), ((), ())), preferre...  76.4 us
    ppermute x93, starting transfers between devices, swap(): lax.ppermute(values, axis, [(place, place ^ bit) for place in range(count)])  70.6 us
    dot_general x8, matrix products, product_tn(): lax.dot_general(left_side, right_side, (((0,), (0,)), ((), ())), preferre...  58.3 us
    pallas_call x1, Pallas kernels, run_backward(): pl.pallas_call(functools.partial(backward_body, heads), grid_spec=grid_sp...  46.8 us
    pallas_call x1, Pallas kernels, run_forward(): pl.pallas_call(functools.partial(forward_body, heads), grid_spec=grid_spe...  40.7 us
  transfers between devices with their start and end apart: 93, of which 35 were waited for; matrix products, arithmetic and copies ran while one was open for 33% of the time, Pallas kernels for 4%

profile of v1, /device:TPU:0, one launch (start us, length us, event | category | flops | bytes accessed | tf_op | source)
XLA Modules:
  0.0 1095.4 jit_solution(7291049013886753499)
XLA Ops:
  33.1 46.1 %collective-permute-done.9 = bf16[4,16,128]{2,1,0:T(8,128)(2,1)S(1)} collective-permute-done((bf16[4,16,128]{2,1,0:T(8,128)(2,1)S(1)}, bf16[4,16,128]{2,1,0:T(8,128)(2,1)S(1)}, u32[]{:S(2)}, u32[]{:S(2)}) %collective-permute-start.9) | collective-permute-done | bytes 16416 | tf_op jit(solution)/shard_map/ppermute | solution.py:470
  103.0 11.6 %collective-permute-done.12 = bf16[272,2048]{1,0:T(8,128)(2,1)} collective-permute-done((bf16[272,2048]{1,0:T(8,128)(2,1)S(1)}, bf16[272,2048]{1,0:T(8,128)(2,1)}, u32[]{:S(2)}, u32[]{:S(2)}) %collective-permute-start.12) | collective-permute-done | bytes 1114144 | tf_op jit(solution)/shard_map/ppermute | solution.py:470
  116.8 41.1 %collective-permute-done.13 = bf16[272,2048]{1,0:T(8,128)(2,1)S(1)} collective-permute-done((bf16[272,2048]{1,0:T(8,128)(2,1)S(1)}, bf16[272,2048]{1,0:T(8,128)(2,1)S(1)}, u32[]{:S(2)}, u32[]{:S(2)}) %collective-permute-start.13) | collective-permute-done | bytes 1114144 | tf_op jit(solution)/shard_map/ppermute | solution.py:470
  171.2 13.1 %collective-permute-done.15 = bf16[256,2048]{1,0:T(8,128)(2,1)} collective-permute-done((bf16[256,2048]{1,0:T(8,128)(2,1)}, bf16[256,2048]{1,0:T(8,128)(2,1)}, u32[]{:S(2)}, u32[]{:S(2)}) %collective-permute-start.15) | collective-permute-done | bytes 1048608 | tf_op jit(solution)/shard_map/ppermute | solution.py:470
  187.1 21.0 %collective-permute-done.14 = bf16[272,2048]{1,0:T(8,128)(2,1)S(1)} collective-permute-done((bf16[272,2048]{1,0:T(8,128)(2,1)}, bf16[272,2048]{1,0:T(8,128)(2,1)S(1)}, u32[]{:S(2)}, u32[]{:S(2)}) %collective-permute-start.14) | collective-permute-done | bytes 1114144 | tf_op jit(solution)/shard_map/ppermute | solution.py:470
  235.0 14.1 %convolution_convert_fusion.7 = bf16[2048,1024]{1,0:T(8,128)(2,1)} fusion(bf16[1024,2048]{1,0:T(8,128)(2,1)} %slice_dynamic-update-slice_fusion, f32[2048]{0:T(1024)S(1)} %reshape.308, f32[2048]{0:T(1024)S(1)} %add_rsqrt_fusion, bf16[2048,2048]{1,0:T(8,128)(2,1)} %constant_dynamic-update-slice_fusion), kind=kOutput, calls=%fused_computation.20 | convolution fusion | flops 8608808960 | bytes 16793600 | tf_op jit(solution)/shard_map/dot_general | solution.py:457
  249.2 10.4 convert_multiply_fusion
  269.5 40.7 %delta_forward.1 = (bf16[2,1024,512]{2,1,0:T(8,128)(2,1)S(1)}, bf16[2,1024,512]{2,1,0:T(8,128)(2,1)S(1)}, bf16[2,1024,512]{2,1,0:T(8,128)(2,1)S(1)}, bf16[8,4,12...) custom-call(s32[1]{0:T(128)} %bitcast.1.place, bf16[2,1024,1024]{2,1,0:T(8,128)(2,1)} %bitcast.189, ...), custom_call_target="tpu_custom_call" | custom-call | tf_op jit(solution)/shard_map/delta_forward/pallas_call | solution.py:347
  324.3 17.5 %collective-permute-done.38 = bf16[256,2048]{1,0:T(8,128)(2,1)S(1)} collective-permute-done((bf16[256,2048]{1,0:T(8,128)(2,1)}, bf16[256,2048]{1,0:T(8,128)(2,1)S(1)}, u32[]{:S(2)}, u32[]{:S(2)}) %collective-permute-start.38) | collective-permute-done | bytes 1048608 | tf_op jit(solution)/shard_map/ppermute | solution.py:470
  348.1 28.0 %collective-permute-done.30 = bf16[352,2048]{1,0:T(8,128)(2,1)S(1)} collective-permute-done((bf16[352,2048]{1,0:T(8,128)(2,1)}, bf16[352,2048]{1,0:T(8,128)(2,1)S(1)}, u32[]{:S(2)}, u32[]{:S(2)}) %collective-permute-start.30) | collective-permute-done | bytes 1441824 | tf_op jit(solution)/shard_map/ppermute | solution.py:470
  385.6 16.5 %collective-permute-done.26 = bf16[256,2048]{1,0:T(8,128)(2,1)S(1)} collective-permute-done((bf16[256,2048]{1,0:T(8,128)(2,1)S(1)}, bf16[256,2048]{1,0:T(8,128)(2,1)S(1)}, u32[]{:S(2)}, u32[]{:S(2)}) %collective-permute-start.26) | collective-permute-done | bytes 1048608 | tf_op jit(solution)/shard_map/ppermute | solution.py:470
  406.4 18.2 %collective-permute-done.45 = bf16[256,2048]{1,0:T(8,128)(2,1)S(1)} collective-permute-done((bf16[256,2048]{1,0:T(8,128)(2,1)S(1)}, bf16[256,2048]{1,0:T(8,128)(2,1)S(1)}, u32[]{:S(2)}, u32[]{:S(2)}) %collective-permute-start.45) | collective-permute-done | bytes 1048608 | tf_op jit(solution)/shard_map/ppermute | solution.py:470
  426.5 13.9 %collective-permute-done.36 = bf16[176,2048]{1,0:T(8,128)(2,1)S(1)} collective-permute-done((bf16[176,2048]{1,0:T(8,128)(2,1)}, bf16[176,2048]{1,0:T(8,128)(2,1)S(1)}, u32[]{:S(2)}, u32[]{:S(2)}) %collective-permute-start.36) | collective-permute-done | bytes 720928 | tf_op jit(solution)/shard_map/ppermute | solution.py:470
  456.6 14.5 %collective-permute-done.32 = bf16[256,2048]{1,0:T(8,128)(2,1)S(1)} collective-permute-done((bf16[256,2048]{1,0:T(8,128)(2,1)S(1)}, bf16[256,2048]{1,0:T(8,128)(2,1)S(1)}, u32[]{:S(2)}, u32[]{:S(2)}) %collective-permute-start.32) | collective-permute-done | bytes 1048608 | tf_op jit(solution)/shard_map/ppermute | solution.py:470
  521.9 10.9 fusion.16
  539.9 11.6 %multiply_convert_fusion.3 = (bf16[704,1024]{1,0:T(8,128)(2,1)}, bf16[704,1024]{1,0:T(8,128)(2,1)}, bf16[704,1024]{1,0:T(8,128)(2,1)}) fusion(f32[704,1024]{1,0:T(8,128)} %fusion.79, f32[704,1024]{1,0:T(8,128)} %fusion.29, bf16[1024,2048]{1,0:T(8,128)(2,1)} %copy-done.97, bf16[176,2048]{1,0:T(8,128)(2,1)S(1)} %copy-done.65, ...), kind=kOutput, calls=%fused_computation.40 | convolution fusion | flops 2975858688 | bytes 17170432 | tf_op jit(solution)/shard_map/dot_general | solution.py:457
  571.2 10.6 add_convert_fusion
  590.0 20.2 %collective-permute-done.53 = bf16[256,2048]{1,0:T(8,128)(2,1)S(1)} collective-permute-done((bf16[256,2048]{1,0:T(8,128)(2,1)S(1)}, bf16[256,2048]{1,0:T(8,128)(2,1)S(1)}, u32[]{:S(2)}, u32[]{:S(2)}) %collective-permute-start.53) | collective-permute-done | bytes 1048608 | tf_op jit(solution)/shard_map/ppermute | solution.py:470
  632.1 14.2 %collective-permute-done.54 = bf16[256,2048]{1,0:T(8,128)(2,1)S(1)} collective-permute-done((bf16[256,2048]{1,0:T(8,128)(2,1)S(1)}, bf16[256,2048]{1,0:T(8,128)(2,1)S(1)}, u32[]{:S(2)}, u32[]{:S(2)}) %collective-permute-start.54) | collective-permute-done | bytes 1048608 | tf_op jit(solution)/shard_map/ppermute | solution.py:470
  660.5 28.5 %collective-permute-done.92 = bf16[176,2048]{1,0:T(8,128)(2,1)S(1)} collective-permute-done((bf16[176,2048]{1,0:T(8,128)(2,1)S(1)}, bf16[176,2048]{1,0:T(8,128)(2,1)S(1)}, u32[]{:S(2)}, u32[]{:S(2)}) %collective-permute-start.92) | collective-permute-done | bytes 720928 | tf_op jit(solution)/shard_map/ppermute | solution.py:470
  690.5 12.9 %collective-permute-done.55 = bf16[256,2048]{1,0:T(8,128)(2,1)} collective-permute-done((bf16[256,2048]{1,0:T(8,128)(2,1)}, bf16[256,2048]{1,0:T(8,128)(2,1)}, u32[]{:S(2)}, u32[]{:S(2)}) %collective-permute-start.55) | collective-permute-done | bytes 1048608 | tf_op jit(solution)/shard_map/ppermute | solution.py:470
  705.0 11.9 %collective-permute-done.89 = bf16[352,2048]{1,0:T(8,128)(2,1)S(1)} collective-permute-done((bf16[352,2048]{1,0:T(8,128)(2,1)S(1)}, bf16[352,2048]{1,0:T(8,128)(2,1)S(1)}, u32[]{:S(2)}, u32[]{:S(2)}) %collective-permute-start.89) | collective-permute-done | bytes 1441824 | tf_op jit(solution)/shard_map/ppermute | solution.py:470
  754.8 46.8 %delta_backward.1 = (bf16[2,1024,1024]{2,1,0:T(8,128)(2,1)S(1)}, f32[2,1024,2]{2,1,0:T(8,128)S(1)}, f32[8,1024]{1,0:T(8,128)S(1)}) custom-call(s32[1]{0:T(128)} %bitcast.1.place, bf16[2,1024,1024]{2,1,0:T(8,128)(2,1)} %bitcast.190, bf16[2,1024,1024]{2,1,0:T(8,128)(2,1)} %bitcast.191, bf16[2,1024,512]{2,1,0:T(8,128)(2,1)S(1)} %get-tuple-element.52.d_outs, ...), custom_call_target="tpu_custom_call" | custom-call | tf_op jit(solution)/shard_map/delta_backward/pallas_call | solution.py:411
  801.7 14.0 %convolution_convert_fusion = bf16[1024,2048]{1,0:T(8,128)(2,1)S(1)} fusion(bf16[2048,1024]{1,0:T(8,128)(2,1)S(1)} %bitcast.182, f32[2048]{0:T(1024)S(1)} %copy-done.103, f32[2048]{0:T(1024)S(1)} %copy-done.109, bf16[2048,2048]{1,0:T(8,128)(2,1)} %constant_dynamic-update-slice_fusion), kind=kOutput, calls=%fused_computation.13 | convolution fusion | flops 8608808960 | bytes 16793600 | tf_op jit(solution)/shard_map/dot_general | solution.py:451
  863.7 12.3 %add_add_fusion.1 = f32[1024,2048]{1,0:T(8,128)S(1)} fusion(f32[1024,2048]{1,0:T(8,128)} %fusion.34, f32[1024,2048]{1,0:T(8,128)} %fusion.21, bf16[1024,2048]{1,0:T(8,128)(2,1)} %slice_dynamic-update-slice_fusion, bf16[2,1024,1024]{2,1,0:T(8,128)(2,1)} %copy-done.6), kind=kOutput, calls=%fused_computation.10 | convolution fusion | flops 4299161600 | bytes 31457280 | tf_op jit(solution)/shard_map/dot_general | solution.py:447
  876.0 19.1 %fusion.1 = (f32[2048]{0:T(1024)S(1)}, f32[2048]{0:T(1024)S(1)}, bf16[1024,2048]{1,0:T(8,128)(2,1)}, bf16[1024,2048]{1,0:T(8,128)(2,1)}) fusion(f32[2048,2048]{1,0:T(8,128)} %convert_multiply_fusion, f32[1024,2048]{1,0:T(8,128)S(1)} %add_add_fusion.1, f32[1024,2048]{1,0:T(8,128)} %fusion.33, f32[1024,2048]{1,0:T(8,128)} %fusion.19, ...), kind=kOutput, calls=%fused_computation.6 | convolution fusion | flops 4311740416 | bytes 56639488 | tf_op jit(solution)/shard_map/dot_general | solution.py:447
  946.0 26.0 %collective-permute-done.82 = bf16[272,2048]{1,0:T(8,128)(2,1)S(1)} collective-permute-done((bf16[272,2048]{1,0:T(8,128)(2,1)S(1)}, bf16[272,2048]{1,0:T(8,128)(2,1)S(1)}, u32[]{:S(2)}, u32[]{:S(2)}) %collective-permute-start.82) | collective-permute-done | bytes 1114144 | tf_op jit(solution)/shard_map/ppermute | solution.py:470
  974.4 13.8 %collective-permute-done.86 = bf16[256,2048]{1,0:T(8,128)(2,1)S(1)} collective-permute-done((bf16[256,2048]{1,0:T(8,128)(2,1)S(1)}, bf16[256,2048]{1,0:T(8,128)(2,1)S(1)}, u32[]{:S(2)}, u32[]{:S(2)}) %collective-permute-start.86) | collective-permute-done | bytes 1048608 | tf_op jit(solution)/shard_map/ppermute | solution.py:470
  1003.9 18.0 %collective-permute-done.74 = bf16[256,2048]{1,0:T(8,128)(2,1)} collective-permute-done((bf16[256,2048]{1,0:T(8,128)(2,1)}, bf16[256,2048]{1,0:T(8,128)(2,1)}, u32[]{:S(2)}, u32[]{:S(2)}) %collective-permute-start.74) | collective-permute-done | bytes 1048608 | tf_op jit(solution)/shard_map/ppermute | solution.py:470
  1027.3 13.7 %collective-permute-done.83 = bf16[272,2048]{1,0:T(8,128)(2,1)} collective-permute-done((bf16[272,2048]{1,0:T(8,128)(2,1)}, bf16[272,2048]{1,0:T(8,128)(2,1)}, u32[]{:S(2)}, u32[]{:S(2)}) %collective-permute-start.83) | collective-permute-done | bytes 1114144 | tf_op jit(solution)/shard_map/ppermute | solution.py:470
  1051.2 18.3 %collective-permute-done.71 = bf16[256,2048]{1,0:T(8,128)(2,1)} collective-permute-done((bf16[256,2048]{1,0:T(8,128)(2,1)}, bf16[256,2048]{1,0:T(8,128)(2,1)}, u32[]{:S(2)}, u32[]{:S(2)}) %collective-permute-start.71) | collective-permute-done | bytes 1048608 | tf_op jit(solution)/shard_map/ppermute | solution.py:470
  1072.6 16.2 %collective-permute-done.64 = bf16[256,2048]{1,0:T(8,128)(2,1)S(1)} collective-permute-done((bf16[256,2048]{1,0:T(8,128)(2,1)}, bf16[256,2048]{1,0:T(8,128)(2,1)S(1)}, u32[]{:S(2)}, u32[]{:S(2)}) %collective-permute-start.64) | collective-permute-done | bytes 1048608 | tf_op jit(solution)/shard_map/ppermute | solution.py:470
  (699 shorter events, 466.6 us)
Async XLA Ops:
  0.7 91.9 %collective-permute-start.1 = (bf16[256,2048]{1,0:T(8,128)(2,1)}, bf16[256,2048]{1,0:T(8,128)(2,1)}, u32[]{:S(2)}, u32[]{:S(2)}) collective-permute-start(bf16[256,2048]{1,0:T(8,128)(2,1)} %bitcast.192), channel_id=1, source_target_pairs={{0,16},{8,24},{16,0},{24,8},{1,17},{9,25},{17,1},{25,9},{2,18},{10... | collective-permute-start | bytes 3145736 | tf_op jit(solution)/shard_map/ppermute | solution.py:470
  3.7 91.8 %collective-permute-start = (bf16[256,2048]{1,0:T(8,128)(2,1)}, bf16[256,2048]{1,0:T(8,128)(2,1)}, u32[]{:S(2)}, u32[]{:S(2)}) collective-permute-start(bf16[256,2048]{1,0:T(8,128)(2,1)} %bitcast.193), channel_id=1, source_target_pairs={{0,8},{8,0},{16,24},{24,16},{1,9},{9,1},{17,25},{25,17},{2,10},{10... | collective-permute-start | bytes 3145736 | tf_op jit(solution)/shard_map/ppermute | solution.py:470
  3.7 91.8 %collective-permute-start.3 = (bf16[256,2048]{1,0:T(8,128)(2,1)}, bf16[256,2048]{1,0:T(8,128)(2,1)}, u32[]{:S(2)}, u32[]{:S(2)}) collective-permute-start(bf16[256,2048]{1,0:T(8,128)(2,1)} %bitcast.194), channel_id=1, source_target_pairs={{0,2},{1,3},{2,0},{3,1},{4,6},{5,7},{6,4},{7,5},{8,10},{9,11},{10,... | collective-permute-start | bytes 3145736 | tf_op jit(solution)/shard_map/ppermute | solution.py:470
  30.0 62.5 %collective-permute-start.16 = (bf16[256,2048]{1,0:T(8,128)(2,1)}, bf16[256,2048]{1,0:T(8,128)(2,1)}, u32[]{:S(2)}, u32[]{:S(2)}) collective-permute-start(bf16[256,2048]{1,0:T(8,128)(2,1)} %pad_maximum_fusion.17), channel_id=1, source_target_pairs={{0,4},{1,5},{2,6},{3,7},{4,0},{5,1},{6,2},{7,3},{8,12},{9,13},{10,... | collective-permute-start | bytes 3145736 | tf_op jit(solution)/shard_map/ppermute | solution.py:470
  92.5 65.3 %collective-permute-start.13 = (bf16[272,2048]{1,0:T(8,128)(2,1)S(1)}, bf16[272,2048]{1,0:T(8,128)(2,1)S(1)}, u32[]{:S(2)}, u32[]{:S(2)}) collective-permute-start(bf16[272,2048]{1,0:T(8,128)(2,1)S(1)} %pad_maximum_fusion.14), channel_id=1, source_target_pairs={{0,4},{1,5},{2,6},{3,7},{4,0},{5,1},{6,2},{7,3},{8,12},{9,13},{10,... | collective-permute-start | bytes 3342344 | tf_op jit(solution)/shard_map/ppermute | solution.py:470
  92.6 251.7 %collective-permute-start.35 = (bf16[176,2048]{1,0:T(8,128)(2,1)}, bf16[176,2048]{1,0:T(8,128)(2,1)}, u32[]{:S(2)}, u32[]{:S(2)}) collective-permute-start(bf16[176,2048]{1,0:T(8,128)(2,1)} %param.35), channel_id=1, source_target_pairs={{0,4},{1,5},{2,6},{3,7},{4,0},{5,1},{6,2},{7,3},{8,12},{9,13},{10,... | collective-permute-start | bytes 2162696 | tf_op jit(solution)/shard_map/ppermute | solution.py:470
  95.5 64.7 %collective-permute-start.2 = (bf16[256,2048]{1,0:T(8,128)(2,1)}, bf16[256,2048]{1,0:T(8,128)(2,1)}, u32[]{:S(2)}, u32[]{:S(2)}) collective-permute-start(bf16[256,2048]{1,0:T(8,128)(2,1)} %collective-permute-done.1), channel_id=1, source_target_pairs={{0,8},{8,0},{16,24},{24,16},{1,9},{9,1},{17,25},{25,17},{2,10},{10... | collective-permute-start | bytes 3145736 | tf_op jit(solution)/shard_map/ppermute | solution.py:470
  95.5 70.9 %collective-permute-start.4 = (bf16[256,2048]{1,0:T(8,128)(2,1)}, bf16[256,2048]{1,0:T(8,128)(2,1)}, u32[]{:S(2)}, u32[]{:S(2)}) collective-permute-start(bf16[256,2048]{1,0:T(8,128)(2,1)} %collective-permute-done.3), channel_id=1, source_target_pairs={{0,8},{8,0},{16,24},{24,16},{1,9},{9,1},{17,25},{25,17},{2,10},{10... | collective-permute-start | bytes 3145736 | tf_op jit(solution)/shard_map/ppermute | solution.py:470
  114.6 51.8 %collective-permute-start.5 = (bf16[256,2048]{1,0:T(8,128)(2,1)}, bf16[256,2048]{1,0:T(8,128)(2,1)}, u32[]{:S(2)}, u32[]{:S(2)}) collective-permute-start(bf16[256,2048]{1,0:T(8,128)(2,1)} %collective-permute-done.3), channel_id=1, source_target_pairs={{0,16},{8,24},{16,0},{24,8},{1,17},{9,25},{17,1},{25,9},{2,18},{10... | collective-permute-start | bytes 3145736 | tf_op jit(solution)/shard_map/ppermute | solution.py:470
  166.4 149.5 %collective-permute-start.29 = (bf16[352,2048]{1,0:T(8,128)(2,1)}, bf16[352,2048]{1,0:T(8,128)(2,1)}, u32[]{:S(2)}, u32[]{:S(2)}) collective-permute-start(bf16[352,2048]{1,0:T(8,128)(2,1)} %pad_maximum_fusion.11), channel_id=1, source_target_pairs={{0,4},{1,5},{2,6},{3,7},{4,0},{5,1},{6,2},{7,3},{8,12},{9,13},{10,... | collective-permute-start | bytes 4325384 | tf_op jit(solution)/shard_map/ppermute | solution.py:470
  166.4 55.3 %collective-permute-start.6 = (bf16[256,2048]{1,0:T(8,128)(2,1)}, bf16[256,2048]{1,0:T(8,128)(2,1)}, u32[]{:S(2)}, u32[]{:S(2)}) collective-permute-start(bf16[256,2048]{1,0:T(8,128)(2,1)} %collective-permute-done.5), channel_id=1, source_target_pairs={{0,8},{8,0},{16,24},{24,16},{1,9},{9,1},{17,25},{25,17},{2,10},{10... | collective-permute-start | bytes 3145736 | tf_op jit(solution)/shard_map/ppermute | solution.py:470
  184.3 132.2 %collective-permute-start.28 = (bf16[352,2048]{1,0:T(8,128)(2,1)}, bf16[352,2048]{1,0:T(8,128)(2,1)}, u32[]{:S(2)}, u32[]{:S(2)}) collective-permute-start(bf16[352,2048]{1,0:T(8,128)(2,1)} %pad_maximum_fusion.11), channel_id=1, source_target_pairs={{0,1},{1,0},{2,3},{3,2},{4,5},{5,4},{6,7},{7,6},{8,9},{9,8},{10,11... | collective-permute-start | bytes 4325384 | tf_op jit(solution)/shard_map/ppermute | solution.py:470
  224.1 98.8 %collective-permute-start.37 = (bf16[256,2048]{1,0:T(8,128)(2,1)}, bf16[256,2048]{1,0:T(8,128)(2,1)}, u32[]{:S(2)}, u32[]{:S(2)}) collective-permute-start(bf16[256,2048]{1,0:T(8,128)(2,1)} %bitcast.24), channel_id=1, source_target_pairs={{0,8},{8,0},{16,24},{24,16},{1,9},{9,1},{17,25},{25,17},{2,10},{10... | collective-permute-start | bytes 3145736 | tf_op jit(solution)/shard_map/ppermute | solution.py:470
  259.5 61.7 %collective-permute-start.43 = (bf16[256,2048]{1,0:T(8,128)(2,1)}, bf16[256,2048]{1,0:T(8,128)(2,1)S(1)}, u32[]{:S(2)}, u32[]{:S(2)}) collective-permute-start(bf16[256,2048]{1,0:T(8,128)(2,1)} %bitcast.24), channel_id=1, source_target_pairs={{0,2},{1,3},{2,0},{3,1},{4,6},{5,7},{6,4},{7,5},{8,10},{9,11},{10,... | collective-permute-start | bytes 3145736 | tf_op jit(solution)/shard_map/ppermute | solution.py:470
  322.9 118.5 %collective-permute-start.21 = (bf16[256,2048]{1,0:T(8,128)(2,1)S(1)}, bf16[256,2048]{1,0:T(8,128)(2,1)S(1)}, u32[]{:S(2)}, u32[]{:S(2)}) collective-permute-start(bf16[256,2048]{1,0:T(8,128)(2,1)S(1)} %get-tuple-element.199), channel_id=1, source_target_pairs={{0,8},{8,0},{16,24},{24,16},{1,9},{9,1},{17,25},{25,17},{2,10},{10... | collective-permute-start | bytes 3145736 | tf_op jit(solution)/shard_map/ppermute | solution.py:470
  346.7 79.7 %collective-permute-start.39 = (bf16[256,2048]{1,0:T(8,128)(2,1)S(1)}, bf16[256,2048]{1,0:T(8,128)(2,1)S(1)}, u32[]{:S(2)}, u32[]{:S(2)}) collective-permute-start(bf16[256,2048]{1,0:T(8,128)(2,1)S(1)} %collective-permute-done.38), channel_id=1, source_target_pairs={{0,8},{8,0},{16,24},{24,16},{1,9},{9,1},{17,25},{25,17},{2,10},{10... | collective-permute-start | bytes 3145736 | tf_op jit(solution)/shard_map/ppermute | solution.py:470
  347.4 55.9 %collective-permute-start.44 = (bf16[256,2048]{1,0:T(8,128)(2,1)S(1)}, bf16[256,2048]{1,0:T(8,128)(2,1)S(1)}, u32[]{:S(2)}, u32[]{:S(2)}) collective-permute-start(bf16[256,2048]{1,0:T(8,128)(2,1)S(1)} %collective-permute-done.43), channel_id=1, source_target_pairs={{0,8},{8,0},{16,24},{24,16},{1,9},{9,1},{17,25},{25,17},{2,10},{10... | collective-permute-start | bytes 3145736 | tf_op jit(solution)/shard_map/ppermute | solution.py:470
  509.0 77.6 %collective-permute-start.41 = (bf16[256,2048]{1,0:T(8,128)(2,1)}, bf16[256,2048]{1,0:T(8,128)(2,1)}, u32[]{:S(2)}, u32[]{:S(2)}) collective-permute-start(bf16[256,2048]{1,0:T(8,128)(2,1)} %get-tuple-element.196), channel_id=1, source_target_pairs={{0,8},{8,0},{16,24},{24,16},{1,9},{9,1},{17,25},{25,17},{2,10},{10... | collective-permute-start | bytes 3145736 | tf_op jit(solution)/shard_map/ppermute | solution.py:470
  509.2 113.4 %collective-permute-start.40 = (bf16[256,2048]{1,0:T(8,128)(2,1)}, bf16[256,2048]{1,0:T(8,128)(2,1)}, u32[]{:S(2)}, u32[]{:S(2)}) collective-permute-start(bf16[256,2048]{1,0:T(8,128)(2,1)} %get-tuple-element.195), channel_id=1, source_target_pairs={{0,8},{8,0},{16,24},{24,16},{1,9},{9,1},{17,25},{25,17},{2,10},{10... | collective-permute-start | bytes 3145736 | tf_op jit(solution)/shard_map/ppermute | solution.py:470
  558.4 55.4 %collective-permute-start.91 = (bf16[176,2048]{1,0:T(8,128)(2,1)}, bf16[176,2048]{1,0:T(8,128)(2,1)}, u32[]{:S(2)}, u32[]{:S(2)}) collective-permute-start(bf16[176,2048]{1,0:T(8,128)(2,1)} %get-tuple-element.204), channel_id=1, source_target_pairs={{0,1},{1,0},{2,3},{3,2},{4,5},{5,4},{6,7},{7,6},{8,9},{9,8},{10,11... | collective-permute-start | bytes 2162696 | tf_op jit(solution)/shard_map/ppermute | solution.py:470
  621.1 83.8 %collective-permute-start.87 = (bf16[352,2048]{1,0:T(8,128)(2,1)S(1)}, bf16[352,2048]{1,0:T(8,128)(2,1)S(1)}, u32[]{:S(2)}, u32[]{:S(2)}) collective-permute-start(bf16[352,2048]{1,0:T(8,128)(2,1)S(1)} %pad_maximum_fusion.12), channel_id=1, source_target_pairs={{0,1},{1,0},{2,3},{3,2},{4,5},{5,4},{6,7},{7,6},{8,9},{9,8},{10,11... | collective-permute-start | bytes 4325384 | tf_op jit(solution)/shard_map/ppermute | solution.py:470
  622.7 66.4 %collective-permute-start.92 = (bf16[176,2048]{1,0:T(8,128)(2,1)S(1)}, bf16[176,2048]{1,0:T(8,128)(2,1)S(1)}, u32[]{:S(2)}, u32[]{:S(2)}) collective-permute-start(bf16[176,2048]{1,0:T(8,128)(2,1)S(1)} %add_convert_fusion.33), channel_id=1, source_target_pairs={{0,4},{1,5},{2,6},{3,7},{4,0},{5,1},{6,2},{7,3},{8,12},{9,13},{10,... | collective-permute-start | bytes 2162696 | tf_op jit(solution)/shard_map/ppermute | solution.py:470
  631.7 85.2 %collective-permute-start.89 = (bf16[352,2048]{1,0:T(8,128)(2,1)S(1)}, bf16[352,2048]{1,0:T(8,128)(2,1)S(1)}, u32[]{:S(2)}, u32[]{:S(2)}) collective-permute-start(bf16[352,2048]{1,0:T(8,128)(2,1)S(1)} %add_convert_fusion.2), channel_id=1, source_target_pairs={{0,4},{1,5},{2,6},{3,7},{4,0},{5,1},{6,2},{7,3},{8,12},{9,13},{10,... | collective-permute-start | bytes 4325384 | tf_op jit(solution)/shard_map/ppermute | solution.py:470
  653.0 50.5 %collective-permute-start.55 = (bf16[256,2048]{1,0:T(8,128)(2,1)}, bf16[256,2048]{1,0:T(8,128)(2,1)}, u32[]{:S(2)}, u32[]{:S(2)}) collective-permute-start(bf16[256,2048]{1,0:T(8,128)(2,1)} %get-tuple-element.155), channel_id=1, source_target_pairs={{0,2},{1,3},{2,0},{3,1},{4,6},{5,7},{6,4},{7,5},{8,10},{9,11},{10,... | collective-permute-start | bytes 3145736 | tf_op jit(solution)/shard_map/ppermute | solution.py:470
  658.1 59.6 %collective-permute-start.66 = (bf16[256,2048]{1,0:T(8,128)(2,1)}, bf16[256,2048]{1,0:T(8,128)(2,1)}, u32[]{:S(2)}, u32[]{:S(2)}) collective-permute-start(bf16[256,2048]{1,0:T(8,128)(2,1)} %get-tuple-element.155), channel_id=1, source_target_pairs={{0,16},{8,24},{16,0},{24,8},{1,17},{9,25},{17,1},{25,9},{2,18},{10... | collective-permute-start | bytes 3145736 | tf_op jit(solution)/shard_map/ppermute | solution.py:470
  852.8 120.7 %collective-permute-start.84 = (bf16[256,2048]{1,0:T(8,128)(2,1)}, bf16[256,2048]{1,0:T(8,128)(2,1)}, u32[]{:S(2)}, u32[]{:S(2)}) collective-permute-start(bf16[256,2048]{1,0:T(8,128)(2,1)} %pad_maximum_fusion.18), channel_id=1, source_target_pairs={{0,1},{1,0},{2,3},{3,2},{4,5},{5,4},{6,7},{7,6},{8,9},{9,8},{10,11... | collective-permute-start | bytes 3145736 | tf_op jit(solution)/shard_map/ppermute | solution.py:470
  856.1 80.4 %collective-permute-start.85 = (bf16[256,2048]{1,0:T(8,128)(2,1)}, bf16[256,2048]{1,0:T(8,128)(2,1)}, u32[]{:S(2)}, u32[]{:S(2)}) collective-permute-start(bf16[256,2048]{1,0:T(8,128)(2,1)} %pad_maximum_fusion.19), channel_id=1, source_target_pairs={{0,1},{1,0},{2,3},{3,2},{4,5},{5,4},{6,7},{7,6},{8,9},{9,8},{10,11... | collective-permute-start | bytes 3145736 | tf_op jit(solution)/shard_map/ppermute | solution.py:470
  923.8 102.4 %collective-permute-start.81 = (bf16[272,2048]{1,0:T(8,128)(2,1)S(1)}, bf16[272,2048]{1,0:T(8,128)(2,1)S(1)}, u32[]{:S(2)}, u32[]{:S(2)}) collective-permute-start(bf16[272,2048]{1,0:T(8,128)(2,1)S(1)} %pad_maximum_fusion.15), channel_id=1, source_target_pairs={{0,1},{1,0},{2,3},{3,2},{4,5},{5,4},{6,7},{7,6},{8,9},{9,8},{10,11... | collective-permute-start | bytes 3342344 | tf_op jit(solution)/shard_map/ppermute | solution.py:470
  939.8 48.4 %collective-permute-start.86 = (bf16[256,2048]{1,0:T(8,128)(2,1)S(1)}, bf16[256,2048]{1,0:T(8,128)(2,1)S(1)}, u32[]{:S(2)}, u32[]{:S(2)}) collective-permute-start(bf16[256,2048]{1,0:T(8,128)(2,1)S(1)} %add_convert_fusion.6), channel_id=1, source_target_pairs={{0,4},{1,5},{2,6},{3,7},{4,0},{5,1},{6,2},{7,3},{8,12},{9,13},{10,... | collective-permute-start | bytes 3145736 | tf_op jit(solution)/shard_map/ppermute | solution.py:470
  990.7 50.4 %collective-permute-start.83 = (bf16[272,2048]{1,0:T(8,128)(2,1)}, bf16[272,2048]{1,0:T(8,128)(2,1)}, u32[]{:S(2)}, u32[]{:S(2)}) collective-permute-start(bf16[272,2048]{1,0:T(8,128)(2,1)} %add_convert_fusion.4), channel_id=1, source_target_pairs={{0,4},{1,5},{2,6},{3,7},{4,0},{5,1},{6,2},{7,3},{8,12},{9,13},{10,... | collective-permute-start | bytes 3342344 | tf_op jit(solution)/shard_map/ppermute | solution.py:470
  999.8 72.8 %collective-permute-start.58 = (bf16[256,2048]{1,0:T(8,128)(2,1)}, bf16[256,2048]{1,0:T(8,128)(2,1)}, u32[]{:S(2)}, u32[]{:S(2)}) collective-permute-start(bf16[256,2048]{1,0:T(8,128)(2,1)} %get-tuple-element.191), channel_id=1, source_target_pairs={{0,8},{8,0},{16,24},{24,16},{1,9},{9,1},{17,25},{25,17},{2,10},{10... | collective-permute-start | bytes 3145736 | tf_op jit(solution)/shard_map/ppermute | solution.py:470
  1021.9 50.8 %collective-permute-start.60 = (bf16[256,2048]{1,0:T(8,128)(2,1)}, bf16[256,2048]{1,0:T(8,128)(2,1)}, u32[]{:S(2)}, u32[]{:S(2)}) collective-permute-start(bf16[256,2048]{1,0:T(8,128)(2,1)} %add_convert_fusion.19), channel_id=1, source_target_pairs={{0,16},{8,24},{16,0},{24,8},{1,17},{9,25},{17,1},{25,9},{2,18},{10... | collective-permute-start | bytes 3145736 | tf_op jit(solution)/shard_map/ppermute | solution.py:470
  (196 other events, 4570.3 us)

commit v2 on v1

v2 whole, which is shorter than its diff:
```python
import functools

import jax
import jax.numpy as jnp
from jax import lax
from jax.experimental import pallas as pl
from jax.experimental.pallas import tpu as pltpu
from jax.sharding import Mesh, PartitionSpec as P

H = 16
DK = 128
DV = 256
CHUNK = 128
KERNEL = 4
HALO = 16
BETA_LANES = 128
BATCH = ("high", "team", "low")
ALL = ("seq", "high", "team", "low")
EPS_NORM = 1e-05
EPS_UNIT = 1e-06
F32 = jnp.float32
BF16 = jnp.bfloat16
VMEM_PARAMS = pltpu.CompilerParams(
    dimension_semantics=("arbitrary",), vmem_limit_bytes=52 * 1024 * 1024
)


def mm(a, b):
    return jnp.dot(a.astype(BF16), b.astype(BF16), preferred_element_type=F32)


def mm_nt(a, b):
    return lax.dot_general(
        a.astype(BF16), b.astype(BF16), (((1,), (1,)), ((), ())), preferred_element_type=F32
    )


def mm_tn(a, b):
    return lax.dot_general(
        a.astype(BF16), b.astype(BF16), (((0,), (0,)), ((), ())), preferred_element_type=F32
    )


def split_pair(a):
    high = a.astype(BF16)
    return high, (a - high.astype(F32)).astype(BF16)


def mm_fine(a, b):
    a_high, a_low = split_pair(a)
    b_high, b_low = split_pair(b)
    left = jnp.concatenate([a_high, a_low], axis=1)
    right = jnp.concatenate(
        [
            jnp.concatenate([b_high, b_low], axis=1),
            jnp.concatenate([b_high, jnp.zeros_like(b_low)], axis=1),
        ],
        axis=0,
    )
    both = jnp.dot(left, right, preferred_element_type=F32)
    wide = b.shape[1]
    return both[:, :wide] + both[:, wide:]


def sigmoid(v):
    return 1.0 / (1.0 + jnp.exp(-v))


def conv_cols(ext, seq, start, width, taps, rows):
    total = None
    for tap in range(KERNEL):
        term = taps[tap : tap + 1, start : start + width] * ext[
            seq, pl.ds(8 - (KERNEL - 1) + tap, rows), start : start + width
        ]
        total = term if total is None else total + term
    return total


def lower_masks(rows):
    row = lax.broadcasted_iota(jnp.int32, (rows, rows), 0)
    col = lax.broadcasted_iota(jnp.int32, (rows, rows), 1)
    return row, col


def inverse_many(couplings, row, col):
    rows = row.shape[0]
    eye = (row == col).astype(F32)
    pair = (row // 2 == col // 2)
    out = [eye - jnp.where(pair, a, 0.0) for a in couplings]
    size = 2
    while size < rows:
        mask = (row // (2 * size) == col // (2 * size)) & (row // size != col // size)
        inner = [mm_fine(jnp.where(mask, a, 0.0), t) for a, t in zip(couplings, out)]
        out = [t - mm_fine(t, i) for t, i in zip(out, inner)]
        size *= 2
    return out


def forward_body(
    heads, place, pre, strengths, cols, rows_g, taps, outs, fresh, starts, solved, ext, state
):
    chunk = pl.program_id(0)
    count = pre.shape[3]
    key_all = heads * DK

    @pl.when(chunk == 0)
    def _():
        ext[:, 0:8, :] = jnp.zeros((2, 8, ext.shape[2]), F32)
        state[...] = jnp.zeros(state.shape, F32)

    row, col = lower_masks(count)
    streams = [(seq, head) for seq in range(2) for head in range(heads)]
    for seq in range(2):
        ext[seq, 8 : 8 + count, :] = pre[0, seq, 0].astype(F32)
    queries, keys, values, ratios, couplings = [], [], [], [], []
    for seq, head in streams:
        q = conv_cols(ext, seq, head * DK, DK, taps, count)
        q = q * sigmoid(q)
        q = q * lax.rsqrt(jnp.sum(q * q, axis=1, keepdims=True) + EPS_UNIT)
        k = conv_cols(ext, seq, key_all + head * DK, DK, taps, count)
        k = k * sigmoid(k)
        k = k * lax.rsqrt(jnp.sum(k * k, axis=1, keepdims=True) + EPS_UNIT)
        v = conv_cols(ext, seq, 2 * key_all + head * DV, DV, taps, count)
        v = v * sigmoid(v)
        queries.append(q.astype(BF16))
        keys.append(k.astype(BF16))
        values.append(v.astype(BF16))
        g_col = cols[0, seq, 0, :, 3 * head : 3 * head + 1]
        g_row = rows_g[0, seq, 0, 0, head : head + 1, :]
        ratio = jnp.where(row >= col, jnp.exp(jnp.minimum(g_col - g_row, 0.0)), 0.0)
        ratios.append(ratio)
        beta = sigmoid(strengths[0, seq, 0, :, head : head + 1])
        couplings.append(jnp.where(row > col, beta * ratio * mm_nt(keys[-1], keys[-1]), 0.0))
    for seq in range(2):
        ext[seq, 0:8, :] = ext[seq, count : count + 8, :]
    inverses = inverse_many(couplings, row, col)
    for at, (seq, head) in enumerate(streams):
        q, k, v, ratio = queries[at], keys[at], values[at], ratios[at]
        beta = sigmoid(strengths[0, seq, 0, :, head : head + 1])
        grown = cols[0, seq, 0, :, 3 * head + 1 : 3 * head + 2]
        fade = cols[0, seq, 0, :, 3 * head + 2 : 3 * head + 3]
        held = state[at]
        held_low = held.astype(BF16)
        starts[0, at] = held_low
        inverse = inverses[at].astype(BF16)
        solved[0, at] = inverse
        right = beta * (v.astype(F32) - grown * mm(k, held_low))
        news = mm(inverse, right).astype(BF16)
        scores = ratio * mm_nt(q, k)
        out = mm(scores, news) + grown * mm(q, held_low)
        last = jnp.exp(rows_g[0, seq, 0, 0, head : head + 1, count - 1 : count])
        state[at] = last * held + mm_tn(fade * k.astype(F32), news)
        place_v = slice(head * DV, head * DV + DV)
        fresh[0, seq, 0, :, place_v] = news
        outs[0, seq, 0, :, place_v] = out.astype(BF16)


def backward_body(
    heads,
    place,
    pre,
    halo,
    d_outs,
    d_gate,
    strengths,
    cols,
    rows_g,
    taps,
    fresh,
    starts,
    solved,
    d_all,
    d_taps,
    ext,
    d_ext,
    d_state,
):
    step = pl.program_id(0)
    chunk = pl.num_programs(0) - 1 - step
    count = pre.shape[3]
    key_all = heads * DK

    @pl.when(step == 0)
    def _():
        d_ext[:, count : count + 8, :] = jnp.zeros((2, 8, d_ext.shape[2]), F32)
        d_state[...] = jnp.zeros(d_state.shape, F32)
        d_taps[...] = jnp.zeros(d_taps.shape, F32)

    row, col = lower_masks(count)
    streams = [(seq, head) for seq in range(2) for head in range(heads)]
    keep = jnp.where(chunk > 0, 1.0, 0.0)
    for seq in range(2):
        ext[seq, 0:8, :] = keep * halo[0, seq, 0].astype(F32)[HALO - 8 : HALO, :]
        ext[seq, 8 : 8 + count, :] = pre[0, seq, 0].astype(F32)
    d_betas = []
    for at, (seq, head) in enumerate(streams):
        beta = sigmoid(strengths[0, seq, 0, :, head : head + 1])
        g_col = cols[0, seq, 0, :, 3 * head : 3 * head + 1]
        grown = cols[0, seq, 0, :, 3 * head + 1 : 3 * head + 2]
        fade = cols[0, seq, 0, :, 3 * head + 2 : 3 * head + 3]
        g_row = rows_g[0, seq, 0, 0, head : head + 1, :]
        last = jnp.exp(g_row[:, count - 1 : count])

        q_conv = conv_cols(ext, seq, head * DK, DK, taps, count)
        q_sig = sigmoid(q_conv)
        q_act = q_conv * q_sig
        q_scale = lax.rsqrt(jnp.sum(q_act * q_act, axis=1, keepdims=True) + EPS_UNIT)
        q_unit = q_act * q_scale
        k_conv = conv_cols(ext, seq, key_all + head * DK, DK, taps, count)
        k_sig = sigmoid(k_conv)
        k_act = k_conv * k_sig
        k_scale = lax.rsqrt(jnp.sum(k_act * k_act, axis=1, keepdims=True) + EPS_UNIT)
        k_unit = k_act * k_scale
        v_conv = conv_cols(ext, seq, 2 * key_all + head * DV, DV, taps, count)
        v_sig = sigmoid(v_conv)
        q, k = q_unit.astype(BF16), k_unit.astype(BF16)
        v = (v_conv * v_sig).astype(BF16).astype(F32)
        k_full = k.astype(F32)

        place_v = slice(head * DV, head * DV + DV)
        d_out = d_outs[0, seq, 0, :, place_v]
        news = fresh[0, seq, 0, :, place_v]
        held = starts[0, at]
        inverse = solved[0, at]
        d_held = d_state[at]
        d_held_low = d_held.astype(BF16)
        ratio = jnp.where(row >= col, jnp.exp(jnp.minimum(g_col - g_row, 0.0)), 0.0)
        scores = ratio * mm_nt(q, k)
        d_news = mm_tn(scores, d_out) + mm(fade * k_full, d_held_low)
        d_right = mm_tn(inverse, d_news)
        d_right_low = d_right.astype(BF16)
        d_couple = jnp.where(row > col, -ratio * mm_nt(d_right_low, news), 0.0)
        key_key = mm_nt(k, k)
        d_kk = beta * d_couple
        d_scores = ratio * mm_nt(d_out, news)
        out_held = mm_nt(d_out, held)
        right_held = mm_nt(d_right_low, held)
        news_held = mm_nt(news, d_held_low)
        d_q = mm(d_scores, k) + grown * out_held
        d_k = (
            mm_tn(d_scores, q)
            + mm(d_kk, k)
            + mm_tn(d_kk, k)
            + fade * news_held
            - (beta * grown) * right_held
        )
        d_v = beta * d_right
        d_betas.append(
            jnp.sum(d_right * v, axis=1, keepdims=True)
            - grown * jnp.sum(right_held * k_full, axis=1, keepdims=True)
            + jnp.sum(d_couple * key_key, axis=1, keepdims=True)
        )
        d_state[at] = (
            last * d_held
            + mm_tn(grown * q.astype(F32), d_out)
            - mm_tn((beta * grown) * k_full, d_right_low)
        )
        d_qa = q_scale * (d_q - q_unit * jnp.sum(q_unit * d_q, axis=1, keepdims=True))
        d_ka = k_scale * (d_k - k_unit * jnp.sum(k_unit * d_k, axis=1, keepdims=True))
        d_ext[seq, 0:count, head * DK : head * DK + DK] = d_qa * (
            q_sig * (1.0 + q_conv * (1.0 - q_sig))
        )
        d_ext[seq, 0:count, key_all + head * DK : key_all + head * DK + DK] = d_ka * (
            k_sig * (1.0 + k_conv * (1.0 - k_sig))
        )
        d_ext[
            seq, 0:count, 2 * key_all + head * DV : 2 * key_all + head * DV + DV
        ] = d_v * (v_sig * (1.0 + v_conv * (1.0 - v_sig)))
    for seq in range(2):
        lane = lax.broadcasted_iota(jnp.int32, (count, BETA_LANES), 1)
        d_beta = jnp.zeros((count, BETA_LANES), F32)
        for head in range(heads):
            beta = sigmoid(strengths[0, seq, 0, :, head : head + 1])
            d_beta = jnp.where(
                lane == head, d_betas[seq * heads + head] * beta * (1.0 - beta), d_beta
            )
        wide = ext.shape[2]
        d_all[0, seq, 0, :, wide : wide + BETA_LANES] = d_beta.astype(BF16)
        d_all[0, seq, 0, :, wide + BETA_LANES :] = d_gate[0, seq, 0]
        for start in range(0, wide, 128):
            span = slice(start, start + 128)
            total = None
            near = d_ext[seq, 0:count, span]
            for tap in range(KERNEL):
                term = taps[tap : tap + 1, span] * d_ext[seq, pl.ds(KERNEL - 1 - tap, count), span]
                total = term if total is None else total + term
                moved = ext[seq, pl.ds(8 - (KERNEL - 1) + tap, count), span]
                d_taps[tap : tap + 1, span] += jnp.sum(near * moved, axis=0, keepdims=True)
            d_all[0, seq, 0, :, span] = total.astype(BF16)
        d_ext[seq, count : count + 8, :] = d_ext[seq, 0:8, :]


def chunk_block(chunk, place, per_piece):
    piece = jnp.bitwise_xor(chunk // per_piece, place[0])
    return piece % 2, piece // 2, chunk % per_piece


def chunk_specs(turn, per_piece):
    def by_rows(width):
        def index(step, at):
            half, piece, within = chunk_block(turn(step), at, per_piece)
            return (half, 0, piece, within, 0)

        return pl.BlockSpec((1, 2, 1, CHUNK, width), index)

    def by_chunk(heads):
        def index(step, at):
            half, piece, within = chunk_block(turn(step), at, per_piece)
            return (half, 0, piece, within, 0, 0)

        return pl.BlockSpec((1, 2, 1, 1, heads, CHUNK), index)

    return by_rows, by_chunk


def run_forward(place, pre, strengths, cols, rows_g, taps):
    halves, _, pieces, piece_rows, wide = pre.shape
    heads = rows_g.shape[-2]
    per_piece = piece_rows // CHUNK
    chunks = halves * pieces * per_piece
    by_rows, by_chunk = chunk_specs(lambda step: step, per_piece)
    grid_spec = pltpu.PrefetchScalarGridSpec(
        num_scalar_prefetch=1,
        grid=(chunks,),
        in_specs=[
            by_rows(wide),
            by_rows(BETA_LANES),
            by_rows(3 * heads),
            by_chunk(heads),
            pl.BlockSpec((8, wide), lambda c, at: (0, 0)),
        ],
        out_specs=[
            by_rows(heads * DV),
            by_rows(heads * DV),
            pl.BlockSpec((1, 2 * heads, DK, DV), lambda c, at: (c, 0, 0, 0)),
            pl.BlockSpec((1, 2 * heads, CHUNK, CHUNK), lambda c, at: (c, 0, 0, 0)),
        ],
        scratch_shapes=[
            pltpu.VMEM((2, CHUNK + 8, wide), F32),
            pltpu.VMEM((2 * heads, DK, DV), F32),
        ],
    )
    rows_out = jax.ShapeDtypeStruct(pre.shape[:-1] + (heads * DV,), BF16)
    return pl.pallas_call(
        functools.partial(forward_body, heads),
        grid_spec=grid_spec,
        out_shape=[
            rows_out,
            rows_out,
            jax.ShapeDtypeStruct((chunks, 2 * heads, DK, DV), BF16),
            jax.ShapeDtypeStruct((chunks, 2 * heads, CHUNK, CHUNK), BF16),
        ],
        compiler_params=VMEM_PARAMS,
        name="delta_forward",
    )(place, pre, strengths, cols, rows_g, taps)


def run_backward(
    place, pre, d_outs, d_gate, strengths, cols, rows_g, taps, fresh, starts, solved
):
    halves, _, pieces, piece_rows, wide = pre.shape
    heads = d_outs.shape[-1] // DV
    per_piece = piece_rows // CHUNK
    chunks = halves * pieces * per_piece
    per_halo = CHUNK // HALO
    wide_out = wide + BETA_LANES + heads * DV

    def turned(step):
        return chunks - 1 - step

    by_rows, by_chunk = chunk_specs(turned, per_piece)

    def halo_place(step, at):
        half, piece, within = chunk_block(jnp.maximum(turned(step) - 1, 0), at, per_piece)
        return (half, 0, piece, within * per_halo + per_halo - 1, 0)

    grid_spec = pltpu.PrefetchScalarGridSpec(
        num_scalar_prefetch=1,
        grid=(chunks,),
        in_specs=[
            by_rows(wide),
            pl.BlockSpec((1, 2, 1, HALO, wide), halo_place),
            by_rows(heads * DV),
            by_rows(heads * DV),
            by_rows(BETA_LANES),
            by_rows(3 * heads),
            by_chunk(heads),
            pl.BlockSpec((8, wide), lambda c, at: (0, 0)),
            by_rows(heads * DV),
            pl.BlockSpec((1, 2 * heads, DK, DV), lambda c, at: (turned(c), 0, 0, 0)),
            pl.BlockSpec((1, 2 * heads, CHUNK, CHUNK), lambda c, at: (turned(c), 0, 0, 0)),
        ],
        out_specs=[by_rows(wide_out), pl.BlockSpec((8, wide), lambda c, at: (0, 0))],
        scratch_shapes=[
            pltpu.VMEM((2, CHUNK + 8, wide), F32),
            pltpu.VMEM((2, CHUNK + 8, wide), F32),
            pltpu.VMEM((2 * heads, DK, DV), F32),
        ],
    )
    return pl.pallas_call(
        functools.partial(backward_body, heads),
        grid_spec=grid_spec,
        out_shape=[
            jax.ShapeDtypeStruct(pre.shape[:-1] + (wide_out,), BF16),
            jax.ShapeDtypeStruct((8, wide), F32),
        ],
        compiler_params=VMEM_PARAMS,
        name="delta_backward",
    )(place, pre, pre, d_outs, d_gate, strengths, cols, rows_g, taps, fresh, starts, solved)


def norm_body(half, other, scale, gain, out):
    step = pl.program_id(0)

    @pl.when(step < pl.num_programs(0) // 2)
    def _():
        out[...] = (half[...].astype(F32) * scale[...] * gain[...]).astype(BF16)

    @pl.when(step >= pl.num_programs(0) // 2)
    def _():
        out[...] = (other[...].astype(F32) * scale[...] * gain[...]).astype(BF16)


def run_norm(half, other, scale, gain):
    length, model = half.shape
    tile = 256
    steps = length // tile
    return pl.pallas_call(
        norm_body,
        grid=(2 * steps,),
        in_specs=[
            pl.BlockSpec((tile, model), lambda i: (jnp.minimum(i, steps - 1), 0)),
            pl.BlockSpec((tile, model), lambda i: (jnp.maximum(i - steps, 0), 0)),
            pl.BlockSpec((tile, 1), lambda i: (i, 0)),
            pl.BlockSpec((1, model), lambda i: (0, 0)),
        ],
        out_specs=pl.BlockSpec((tile, model), lambda i: (i, 0)),
        out_shape=jax.ShapeDtypeStruct((2 * length, model), BF16),
        compiler_params=VMEM_PARAMS,
        name="norm_rows",
    )(half, other, scale, gain)


def place_rows(pieces, places, out, gain=None):
    for piece, start, size, target in places:
        rows = pieces[piece][start : start + size, :]
        if gain is not None:
            rows = (rows.astype(F32) * gain[...]).astype(BF16)
        out[target : target + size, :] = rows


def project_body(count, places, narrow, half, other, gain, scale, *refs):
    pieces, weights, outs = refs[:count], refs[count], refs[count + 1 :]
    step, steps = pl.program_id(0), pl.num_programs(0) // 2

    @pl.when(step == 0)
    def _():
        place_rows(pieces, places, weights, gain)

    for chosen, tokens in ((step < steps, half), (step >= steps, other)):

        @pl.when(chosen)
        def _():
            sums = mm_nt(tokens[...], weights[...]) * scale[...]
            outs[0][...] = sums[:, :narrow].astype(BF16)
            if len(outs) > 1:
                outs[1][...] = sums[:, narrow:]


def whole_block(shape):
    return pl.BlockSpec(shape, lambda i: (0, 0), pipeline_mode=pl.Buffered(1))


def run_project(halves, pieces, places, gain, scale, wide, narrow):
    length, model = halves[0].shape
    tile = 256
    steps = length // tile
    out_shape = [jax.ShapeDtypeStruct((wide, model), BF16)]
    out_shape.append(jax.ShapeDtypeStruct((2 * length, narrow), BF16))
    if wide > narrow:
        out_shape.append(jax.ShapeDtypeStruct((2 * length, wide - narrow), F32))
    return pl.pallas_call(
        functools.partial(project_body, len(pieces), places, narrow),
        grid=(2 * steps,),
        in_specs=[
            pl.BlockSpec((tile, model), lambda i: (jnp.minimum(i, steps - 1), 0)),
            pl.BlockSpec((tile, model), lambda i: (jnp.maximum(i - steps, 0), 0)),
            whole_block((1, model)),
            pl.BlockSpec((tile, 1), lambda i: (i, 0)),
        ]
        + [whole_block(piece.shape) for piece in pieces],
        out_specs=[pl.BlockSpec((wide, model), lambda i: (0, 0))]
        + [pl.BlockSpec((tile, one.shape[1]), lambda i: (i, 0)) for one in out_shape[1:]],
        out_shape=out_shape,
        compiler_params=VMEM_PARAMS,
        name="project_rows",
    )(*halves, gain, scale, *pieces)


def hidden_body(count, feed_places, down_places, first, second, *refs):
    pieces, (feed_rows, down_rows, back_first, back_second) = refs[:count], refs[count:]
    step, steps = pl.program_id(0), pl.num_programs(0) // 2

    @pl.when(step == 0)
    def _():
        place_rows(pieces, feed_places, feed_rows)
        place_rows(pieces, down_places, down_rows)

    for chosen, grads, back in (
        (step < steps, first, back_first),
        (step >= steps, second, back_second),
    ):

        @pl.when(chosen)
        def _():
            back[...] = mm_nt(down_rows[...], grads[...]).astype(BF16)


def run_hidden(grads, pieces, feed_places, down_places, units):
    length, model = grads[0].shape
    tile = 256
    steps = length // tile
    return pl.pallas_call(
        functools.partial(hidden_body, len(pieces), feed_places, down_places),
        grid=(2 * steps,),
        in_specs=[
            pl.BlockSpec((tile, model), lambda i: (jnp.minimum(i, steps - 1), 0)),
            pl.BlockSpec((tile, model), lambda i: (jnp.maximum(i - steps, 0), 0)),
        ]
        + [whole_block(piece.shape) for piece in pieces],
        out_specs=[
            pl.BlockSpec((2 * units, model), lambda i: (0, 0)),
            pl.BlockSpec((units, model), lambda i: (0, 0)),
            pl.BlockSpec((units, tile), lambda i: (0, jnp.minimum(i, steps - 1))),
            pl.BlockSpec((units, tile), lambda i: (0, jnp.maximum(i - steps, 0))),
        ],
        out_shape=[
            jax.ShapeDtypeStruct((2 * units, model), BF16),
            jax.ShapeDtypeStruct((units, model), BF16),
            jax.ShapeDtypeStruct((units, length), BF16),
            jax.ShapeDtypeStruct((units, length), BF16),
        ],
        compiler_params=VMEM_PARAMS,
        name="hidden_cotangents",
    )(*grads, *pieces)


def feed_body(feed, weights, back, hidden, d_both, d_feed):
    units = back.shape[0]
    rows = feed[...]
    gate = mm_nt(weights[:units, :], rows)
    up = mm_nt(weights[units:, :], rows)
    sig = sigmoid(gate)
    smooth = gate * sig
    d_hidden = back[...].astype(F32)
    hidden[...] = (smooth * up).astype(BF16)
    d_gate = (d_hidden * up * (sig * (1.0 + gate * (1.0 - sig)))).astype(BF16)
    d_up = (d_hidden * smooth).astype(BF16)
    d_both[:units, :] = d_gate
    d_both[units:, :] = d_up
    d_feed[...] = (
        mm_tn(d_gate, weights[:units, :]) + mm_tn(d_up, weights[units:, :])
    ).astype(BF16)


def run_feed(feed, weights, back):
    length, model = feed.shape
    units = back.shape[0]
    tile = 256
    return pl.pallas_call(
        feed_body,
        grid=(length // tile,),
        in_specs=[
            pl.BlockSpec((tile, model), lambda i: (i, 0)),
            pl.BlockSpec((2 * units, model), lambda i: (0, 0)),
            pl.BlockSpec((units, tile), lambda i: (0, i)),
        ],
        out_specs=[
            pl.BlockSpec((units, tile), lambda i: (0, i)),
            pl.BlockSpec((2 * units, tile), lambda i: (0, i)),
            pl.BlockSpec((tile, model), lambda i: (i, 0)),
        ],
        out_shape=[
            jax.ShapeDtypeStruct((units, length), BF16),
            jax.ShapeDtypeStruct((2 * units, length), BF16),
            jax.ShapeDtypeStruct((length, model), BF16),
        ],
        compiler_params=VMEM_PARAMS,
        name="feed_forward",
    )(feed, weights, back)


def outer_body(first, second, right_first, right_second, out):
    out[...] = (
        mm(first[...], right_first[...]) + mm(second[...], right_second[...])
    ).astype(BF16)


def run_outer(lefts, rights):
    wide, length = lefts[0].shape
    model = rights[0].shape[1]
    tile = 176 if wide % 176 == 0 else wide
    left = pl.BlockSpec((tile, length), lambda i: (i, 0))
    right = pl.BlockSpec((length, model), lambda i: (0, 0))
    return pl.pallas_call(
        outer_body,
        grid=(wide // tile,),
        in_specs=[left, left, right, right],
        out_specs=pl.BlockSpec((tile, model), lambda i: (i, 0)),
        out_shape=jax.ShapeDtypeStruct((wide, model), BF16),
        compiler_params=VMEM_PARAMS,
        name="outer_sums",
    )(*lefts, *rights)


def back_body(d_rows, weights, normed, out, gain):
    @pl.when(pl.program_id(0) == 0)
    def _():
        gain[...] = jnp.zeros(gain.shape, F32)

    sums = mm(d_rows[...], weights[...])
    out[...] = sums.astype(BF16)
    gain[0:1, :] += jnp.sum(sums * normed[...].astype(F32), axis=0, keepdims=True)


def run_back(d_rows, weights, normed, half):
    length, wide = d_rows.shape[0] // 2, d_rows.shape[1]
    model = weights.shape[1]
    tile = 256
    start = half * (length // tile)
    return pl.pallas_call(
        back_body,
        grid=(length // tile,),
        in_specs=[
            pl.BlockSpec((tile, wide), lambda i: (start + i, 0)),
            pl.BlockSpec((wide, model), lambda i: (0, 0)),
            pl.BlockSpec((tile, model), lambda i: (start + i, 0)),
        ],
        out_specs=[
            pl.BlockSpec((tile, model), lambda i: (i, 0)),
            pl.BlockSpec((8, model), lambda i: (0, 0)),
        ],
        out_shape=[
            jax.ShapeDtypeStruct((length, model), BF16),
            jax.ShapeDtypeStruct((8, model), F32),
        ],
        compiler_params=VMEM_PARAMS,
        name="back_rows",
    )(d_rows, weights, normed)


def weigh_body(parts, d_rows, normed, taps, out):
    count, key_part, value_part = parts
    step = pl.program_id(0)
    piece = 2 * key_part + value_part + 16
    sums = mm_tn(d_rows[...], normed[...]).astype(BF16)
    tile = sums.shape[0]
    key_steps = count * key_part // tile
    value_steps = count * value_part // tile

    def store(part, first_step, offset):
        for at in range(tile // part):
            target = (step - first_step) * (tile // part) + at
            start = pl.multiple_of(target * piece + offset, 16)
            out[pl.ds(start, part), :] = sums[at * part : (at + 1) * part, :]

    @pl.when(step < key_steps)
    def _():
        store(key_part, 0, 0)

    @pl.when((step >= key_steps) & (step < 2 * key_steps))
    def _():
        store(key_part, key_steps, key_part)

    @pl.when((step >= 2 * key_steps) & (step < 2 * key_steps + value_steps))
    def _():
        store(value_part, 2 * key_steps, 2 * key_part)

    @pl.when(step == 2 * key_steps + value_steps)
    def _():
        out[count * piece : count * piece + tile, :] = sums
        for at in range(count):
            start = at * piece + piece - 16
            out[start : start + 16, :] = taps[at * 16 : at * 16 + 16, :]


def run_weigh(d_rows, normed, taps, parts):
    count, key_part, value_part = parts
    length = d_rows.shape[0]
    model = normed.shape[1]
    tile = 128
    wide = count * (2 * key_part + value_part)
    rows = wide + 16 * count + tile
    return pl.pallas_call(
        functools.partial(weigh_body, parts),
        grid=(wide // tile + 1,),
        in_specs=[
            pl.BlockSpec((length, tile), lambda i: (0, i)),
            whole_block((length, model)),
            whole_block(taps.shape),
        ],
        out_specs=pl.BlockSpec((rows, model), lambda i: (0, 0)),
        out_shape=jax.ShapeDtypeStruct((rows, model), BF16),
        compiler_params=VMEM_PARAMS,
        name="weight_sums",
    )(d_rows, normed, taps)


def mixer_back_body(
    heads,
    part,
    branch_own,
    branch_other,
    out_rows,
    head_outs,
    gate_own,
    gate_other,
    mixed_own,
    mixed_other,
    normed,
    gain,
    d_outs,
    d_gate,
    d_gain,
    terms,
    out_sums,
    gate_sums,
):
    step, steps = pl.program_id(0), pl.num_programs(0) // 2

    @pl.when(step == 0)
    def _():
        d_gain[...] = jnp.zeros(d_gain.shape, F32)
        out_sums[...] = jnp.zeros(out_sums.shape, F32)
        gate_sums[...] = jnp.zeros(gate_sums.shape, F32)

    for chosen, branch, gate, mixed in (
        (step < steps, branch_own, gate_own, mixed_own),
        (step >= steps, branch_other, gate_other, mixed_other),
    ):

        @pl.when(chosen)
        def _():
            d_mixed = mm_nt(branch[...], out_rows[...])
            out_sums[...] += mm_tn(mixed[...], branch[...])
            total = None
            for head in range(heads):
                span = slice(head * DV, head * DV + DV)
                out = head_outs[:, span].astype(F32)
                grad = d_mixed[:, span]
                g = gate[:, span].astype(F32)
                sig = sigmoid(g)
                scale = lax.rsqrt(jnp.mean(out * out, axis=1, keepdims=True) + EPS_NORM)
                unit = out * scale
                cot = grad * (g * sig)
                term = jnp.sum(cot * unit, axis=0, keepdims=True)
                total = term if total is None else total + term
                scaled = cot * gain[0:1, :]
                d_outs[:, span] = (
                    scale * (scaled - unit * jnp.mean(unit * scaled, axis=1, keepdims=True))
                ).astype(BF16)
                d_gate[:, span] = (
                    grad * unit * gain[0:1, :] * (sig * (1.0 + g * (1.0 - sig)))
                ).astype(BF16)
            d_gain[0:1, :] += total
            gate_sums[...] += mm_tn(d_gate[...], normed[...])

    @pl.when(step == 2 * steps - 1)
    def _():
        for at in range(out_sums.shape[0] // part):
            span = slice(at * part, (at + 1) * part)
            start = 2 * at * part
            terms[start : start + part, :] = gate_sums[span, :].astype(BF16)
            terms[start + part : start + 2 * part, :] = out_sums[span, :].astype(BF16)


def run_mixer_back(branches, out_rows, head_outs, gates, mixed, normed, gain, part):
    length, model = branches[0].shape
    wide = out_rows.shape[0]
    tile = 512
    steps = length // tile
    rows = pl.BlockSpec((tile, wide), lambda i: (i, 0))
    first = pl.BlockSpec((tile, wide), lambda i: (jnp.minimum(i, steps - 1), 0))
    second = pl.BlockSpec((tile, wide), lambda i: (jnp.maximum(i - steps, 0), 0))
    sums = pl.BlockSpec((2 * wide, model), lambda i: (0, 0))
    return pl.pallas_call(
        functools.partial(mixer_back_body, wide // DV, part),
        grid=(2 * steps,),
        in_specs=[
            pl.BlockSpec((tile, model), lambda i: (jnp.minimum(i, steps - 1), 0)),
            pl.BlockSpec((tile, model), lambda i: (jnp.maximum(i - steps, 0), 0)),
            whole_block((wide, model)),
            rows,
            first,
            second,
            first,
            second,
            pl.BlockSpec((tile, model), lambda i: (i, 0)),
            pl.BlockSpec((1, DV), lambda i: (0, 0)),
        ],
        out_specs=[rows, rows, pl.BlockSpec((8, DV), lambda i: (0, 0)), sums],
        out_shape=[
            jax.ShapeDtypeStruct((2 * length, wide), BF16),
            jax.ShapeDtypeStruct((2 * length, wide), BF16),
            jax.ShapeDtypeStruct((8, DV), F32),
            jax.ShapeDtypeStruct((2 * wide, model), BF16),
        ],
        scratch_shapes=[pltpu.VMEM((wide, model), F32), pltpu.VMEM((wide, model), F32)],
        compiler_params=VMEM_PARAMS,
        name="mixer_backward",
    )(*branches, out_rows, head_outs, *gates, *mixed, normed, gain)


def branch_body(count, gate_places, out_places, heads, tokens, gain, scale, head_outs, head_gain, *refs):
    pieces, (gate_rows, out_rows, gate, mixed, branch) = refs[:count], refs[count:]

    @pl.when(pl.program_id(0) == 0)
    def _():
        place_rows(pieces, gate_places, gate_rows, gain)
        place_rows(pieces, out_places, out_rows)

    gate_pre = mm_nt(tokens[...], gate_rows[...]) * scale[...]
    gate[...] = gate_pre.astype(BF16)
    for head in range(heads):
        span = slice(head * DV, head * DV + DV)
        out = head_outs[:, span].astype(F32)
        factor = lax.rsqrt(jnp.mean(out * out, axis=1, keepdims=True) + EPS_NORM)
        g = gate_pre[:, span]
        mixed[:, span] = (out * factor * head_gain[0:1, :] * (g * sigmoid(g))).astype(BF16)
    branch[...] = mm(mixed[...], out_rows[...]).astype(BF16)


def run_branch(half, tokens, pieces, gate_places, out_places, gain, scale, head_outs, head_gain):
    length, model = tokens.shape
    wide = head_outs.shape[1]
    tile = 256
    start = half * (length // tile)
    rows = pl.BlockSpec((tile, wide), lambda i: (i, 0))
    weights = pl.BlockSpec((wide, model), lambda i: (0, 0))
    return pl.pallas_call(
        functools.partial(branch_body, len(pieces), gate_places, out_places, wide // DV),
        grid=(length // tile,),
        in_specs=[
            pl.BlockSpec((tile, model), lambda i: (i, 0)),
            whole_block((1, model)),
            pl.BlockSpec((tile, 1), lambda i: (start + i, 0)),
            pl.BlockSpec((tile, wide), lambda i: (start + i, 0)),
            pl.BlockSpec((1, DV), lambda i: (0, 0)),
        ]
        + [whole_block(piece.shape) for piece in pieces],
        out_specs=[
            weights,
            weights,
            rows,
            rows,
            pl.BlockSpec((tile, model), lambda i: (i, 0)),
        ],
        out_shape=[
            jax.ShapeDtypeStruct((wide, model), BF16),
            jax.ShapeDtypeStruct((wide, model), BF16),
            jax.ShapeDtypeStruct((length, wide), BF16),
            jax.ShapeDtypeStruct((length, wide), BF16),
            jax.ShapeDtypeStruct((length, model), BF16),
        ],
        compiler_params=VMEM_PARAMS,
        name="branch_rows",
    )(tokens, gain, scale, head_outs, head_gain, *pieces)


def finish_body(count, outputs, *refs):
    given, outs = refs[:count], refs[count:]
    for (segments, turned), out in zip(outputs, outs):
        slabs = []
        for size, sources in segments:
            total = None
            for which, start in sources:
                term = given[which][start : start + size, :].astype(F32)
                total = term if total is None else total + term
            slabs.append(total)
        slab = slabs[0] if len(slabs) == 1 else jnp.concatenate(slabs, axis=0)
        if turned:
            rows = slab.shape[0]
            spare = -rows % 128
            if spare:
                slab = jnp.concatenate([slab, jnp.zeros((spare, slab.shape[1]), F32)], axis=0)
            out[...] = slab.T[:, :rows]
        else:
            out[...] = slab


def run_finish(given, outputs):
    model = given[0].shape[1]
    tile = 256
    out_specs, out_shape = [], []
    for segments, turned in outputs:
        rows = sum(size for size, _ in segments)
        if turned:
            out_specs.append(pl.BlockSpec((tile, rows), lambda i: (i, 0)))
            out_shape.append(jax.ShapeDtypeStruct((model, rows), F32))
        else:
            out_specs.append(pl.BlockSpec((rows, tile), lambda i: (0, i)))
            out_shape.append(jax.ShapeDtypeStruct((rows, model), F32))
    return pl.pallas_call(
        functools.partial(finish_body, len(given), outputs),
        grid=(model // tile,),
        in_specs=[pl.BlockSpec((piece.shape[0], tile), lambda i: (0, i)) for piece in given],
        out_specs=out_specs,
        out_shape=out_shape,
        compiler_params=VMEM_PARAMS,
        name="finish_sums",
    )(*given)


def product(left_side, right_side):
    return jnp.dot(left_side, right_side, preferred_element_type=F32)


def product_tn(left_side, right_side):
    return lax.dot_general(
        left_side, right_side, (((0,), (0,)), ((), ())), preferred_element_type=F32
    )


def product_nt(left_side, right_side):
    return lax.dot_general(
        left_side, right_side, (((1,), (1,)), ((), ())), preferred_element_type=F32
    )


def rms_scale(values, gain_vals):
    return (
        values * lax.rsqrt(jnp.mean(values * values, axis=-1, keepdims=True) + EPS_NORM) * gain_vals
    )


def swap(values, axis, bit):
    count = lax.axis_size(axis)
    return lax.ppermute(values, axis, [(place, place ^ bit) for place in range(count)])


def bits_of(count):
    found = []
    bit = 1
    while bit < count:
        found.append(bit)
        bit *= 2
    return found


def after(values, *earlier):
    return lax.optimization_barrier((values, *earlier))[0]


def add_low(left_side, right_side):
    return (left_side.astype(F32) + right_side.astype(F32)).astype(BF16)


def along_x(first):
    count = lax.axis_size("seq") // 2
    pieces = {0: first}
    for offset in sorted(range(1, count), key=lambda o: (-(o & -o), o)):
        low = offset & -offset
        pieces[offset] = swap(pieces[offset ^ low], "seq", 2 * low)
    return [pieces[offset] for offset in range(count)]


def fold_rows(part_own, part_other):
    return fold_came(part_own, swap(part_other, "seq", 1))


def fold_came(part_own, came):
    count = lax.axis_size("seq") // 2
    rows = part_own.shape[0] // (2 * count)
    folded = []
    for start in (count, 0):
        pieces = {}
        for at in reversed(range(count)):
            span = slice((start + at) * rows, (start + at + 1) * rows)
            pieces[at] = add_low(part_own[span], came[span])
        folded.append(pieces)
    return folded


def send_along(pieces):
    return {at: swap(piece, "seq", 2 * at) for at, piece in pieces.items() if at}


def add_along(pieces, came):
    return sum(
        [piece.astype(F32) for piece in came.values()], pieces[0].astype(F32)
    ).astype(BF16)


def cut(values, at, size):
    return values[at * size : (at + 1) * size]


def send_bits(pieces, axis, chosen):
    at = 1 if axis == "low" else 0
    return {
        offset: swap(pieces[offset], axis, offset[at]) for offset in chosen if offset[at]
    }


def add_bits(pieces, came, hold=()):
    pieces = dict(pieces)
    for offset, piece in came.items():
        pieces.pop(offset)
        target = (offset[0], 0)
        kept = after(pieces[target], *hold) if hold else pieces[target]
        total = kept.astype(F32) + piece.astype(F32)
        pieces[target] = total if target == (0, 0) else total.astype(BF16)
    return pieces


def sum_pieces(pieces, near, far):
    return sum(
        [piece.astype(F32) for piece in (*near.values(), *far.values())],
        pieces[0, 0].astype(F32),
    )


def spread_stage(values, axis, bits=None):
    for bit in bits_of(lax.axis_size(axis)) if bits is None else bits:
        came = swap(values, axis, bit)
        values = jnp.where(
            (lax.axis_index(axis) & bit) == 0,
            jnp.concatenate([values, came], axis=0),
            jnp.concatenate([came, values], axis=0),
        )
    return values


def sum_stage(values, axis, dim, bits=None):
    for bit in reversed(bits_of(lax.axis_size(axis)) if bits is None else bits):
        lower, upper = jnp.split(values, 2, axis=dim)
        is_upper = (lax.axis_index(axis) & bit) != 0
        kept = jnp.where(is_upper, upper, lower)
        values = kept + swap(jnp.where(is_upper, lower, upper), axis, bit)
    return values


def local(
    tokens,
    decays,
    out_grad,
    mixer_gain,
    query_weight,
    key_weight,
    value_weight,
    beta_weight,
    outgate_weight,
    query_conv,
    key_conv,
    value_conv,
    head_gain,
    output_weight,
    feed_gain,
    feed_gate,
    feed_up,
    feed_down,
):
    seq_count = lax.axis_size("seq")
    high_count = lax.axis_size("high")
    low_count = lax.axis_size("low")
    seq_pos = lax.axis_index("seq")
    low_pos = lax.axis_index("low")
    devices = seq_count * high_count * 2 * low_count
    heads = high_count
    source = tokens[0]
    grad_own = out_grad[0]
    rows, model = source.shape
    length = rows * seq_count
    pieces_x = seq_count // 2
    key_part = query_weight.shape[1]
    value_part = value_weight.shape[1]
    feed_part = feed_gate.shape[1]
    gain_part = mixer_gain.shape[0]
    head_part = head_gain.shape[0]
    offsets = [(high, low) for high in range(high_count) for low in range(low_count)]
    count = len(offsets)
    far_offsets = [o for o in offsets if o[0] and not o[1]]
    near_offsets = [o for o in offsets if not o[0] and o[1]]
    cross_offsets = [o for o in offsets if o[0] and o[1]]

    groups = []

    def settle(*values):
        places = [(got, offset) for got in groups for offset in got]
        values, pieces = lax.optimization_barrier(
            (values, [got[offset] for got, offset in places])
        )
        for (got, offset), piece in zip(places, pieces):
            got[offset] = piece
        return values

    def fetch(got, chosen):
        if not got[0, 0].shape[0]:
            return
        for high, low in sorted(chosen, key=lambda o: (o[0], -(o[1] & -o[1]), o[1])):
            if low == 0:
                axis, bit, start = "high", high & -high, (high ^ (high & -high), 0)
            else:
                axis, bit, start = "low", low & -low, (high, low ^ (low & -low))
            got[high, low] = swap(got[start], axis, bit)

    def joined(got, start, size):
        return [got[offset][start : start + size] for offset in offsets]

    source_f = source.astype(F32)
    scale_own = lax.rsqrt(jnp.mean(source_f * source_f, axis=-1, keepdims=True) + EPS_NORM)
    small = jnp.concatenate([mixer_gain, feed_gain, beta_weight.T.reshape(-1), head_gain], axis=0)
    small_size = small.shape[0]
    small = jnp.pad(small, (0, -small_size % 2048)).reshape(1, -1, 128)
    small = spread_stage(small, "high")
    small = spread_stage(small, "low")
    small = spread_stage(small, "team")
    logs = jnp.concatenate([jnp.log(decays[0]), scale_own.reshape(1, rows)], axis=0)
    logs = jnp.pad(logs, ((0, -logs.shape[0] % 8), (0, 0)))
    logs = jnp.stack([logs, swap(logs, "team", 1)], axis=0)[:, None]
    taps_own = jnp.concatenate([query_conv, key_conv, value_conv], axis=1)
    taps_wide = taps_own.shape[1]
    taps_rows = jnp.pad(taps_own, ((0, 16 - KERNEL), (0, model - taps_wide)))
    head_got = {(0, 0): jnp.concatenate([query_weight.T, key_weight.T], axis=0)}
    value_got = {(0, 0): jnp.concatenate([value_weight.T, taps_rows], axis=0)}
    groups += [head_got]
    source_x = along_x(source)
    small, logs, source_kept, grad_kept = settle(small, logs, source, grad_own)

    source_team = swap(source_kept, "team", 1)
    fetch(head_got, far_offsets)
    fetch(head_got, near_offsets)
    groups += [value_got]
    small = spread_stage(small, "seq", (1,))
    small = spread_stage(after(small, source_x[-1]), "seq", bits_of(seq_count)[1:])
    for bit in bits_of(seq_count)[1:]:
        logs = jnp.concatenate([logs, swap(after(logs, source_x[-1]), "seq", bit)], axis=1)
    logs = jnp.stack([logs, swap(logs, "seq", 1)], axis=0)
    small, logs, source_x, source_team = settle(small, logs, source_x, source_team)

    team_x = along_x(source_team)
    fetch(value_got, far_offsets)
    fetch(head_got, cross_offsets)
    fetch(value_got, near_offsets)
    gate_got = {(0, 0): outgate_weight.T}
    out_got = {(0, 0): output_weight}
    groups += [gate_got, out_got]
    small_all = small.reshape((seq_count, 2, low_count, high_count, -1)).transpose(0, 3, 1, 2, 4)
    small_all = small_all.reshape(devices, -1)
    gain_f = small_all[:, :gain_part].reshape(-1).astype(F32)
    feed_gain_f = small_all[:, gain_part : 2 * gain_part].reshape(-1).astype(F32)
    beta_rows = (
        small_all[:, 2 * gain_part : 2 * gain_part + H * gain_part]
        .reshape(devices, H, gain_part)
        .transpose(1, 0, 2)
        .reshape(H, model)
    )
    head_gain_all = small_all[:, small_size - head_part : small_size].reshape(-1)
    gain_blocks = head_gain_all.reshape(low_count, DV // low_count)
    gain_row = jnp.concatenate(
        [
            lax.dynamic_index_in_dim(gain_blocks, at ^ low_pos, 0, False)
            for at in range(low_count)
        ],
        axis=0,
    ).astype(F32)[None]
    head_places = [
        seq_pos * (2 * heads) + 2 * (lax.axis_index("high") ^ head) + lax.axis_index("team")
        for head in range(heads)
    ]
    beta_own = jnp.stack(
        [lax.dynamic_index_in_dim(beta_rows, place, 0, False) for place in head_places], axis=0
    )

    head_logs = jnp.stack(
        [lax.dynamic_index_in_dim(logs, place, 3, False) for place in head_places], axis=3
    )
    outer = (2, 2, pieces_x)
    scale_all = logs[:, :, :, H].reshape(2 * length, 1)
    per_piece = rows // CHUNK
    totals = jnp.cumsum(head_logs.reshape(outer + (heads, per_piece, CHUNK)), axis=-1)
    rows_g = totals.transpose(0, 1, 2, 4, 3, 5)

    def as_cols(values):
        return values.transpose(0, 1, 2, 4, 5, 3).reshape(outer + (rows, heads))

    totals_cols = as_cols(totals)
    fade_cols = as_cols(jnp.exp(totals[..., -1:] - totals))

    half_tokens = jnp.concatenate(list(source_x) + list(team_x), axis=0)
    (
        half_tokens,
        grad_kept,
        gain_f,
        feed_gain_f,
        beta_own,
        gain_row,
        scale_all,
        rows_g,
        cols,
        beta_block,
    ) = settle(
        half_tokens,
        grad_kept,
        gain_f,
        feed_gain_f,
        beta_own,
        gain_row,
        scale_all,
        rows_g,
        jnp.stack([totals_cols, jnp.exp(totals_cols), fade_cols], axis=-1).reshape(
            outer + (rows, 3 * heads)
        ),
        jnp.pad(beta_own, ((0, BETA_LANES - heads), (0, 0))),
    )

    other_tokens = swap(half_tokens, "seq", 1)
    fetch(value_got, cross_offsets)
    fetch(gate_got, far_offsets)

    ends = [feed_part * part // 11 // 16 * 16 for part in (3, 4, 6, 9)] + [feed_part]
    starts_at = [0] + ends[:-1]
    units = [end - start for start, end in zip(starts_at, ends)]
    first_count = ends[2]
    shares = []
    for start, end in zip(starts_at, ends):
        span = slice(start, end)
        shares.append(
            jnp.concatenate([feed_gate[:, span].T, feed_up[:, span].T, feed_down[span]], axis=0)
        )
    fine_gots = [{(0, 0): share} for share in shares]
    coarse_ranges = ((0,), (1, 2), (3,), (4,))
    coarse_gots = [
        {(0, 0): jnp.concatenate([shares[at] for at in ranges], axis=0)}
        for ranges in coarse_ranges
    ]
    feed_gots = fine_gots + coarse_gots
    near_or_own = [o for o in offsets if not o[0]]

    def fetch_fine(index, chosen):
        if units[index]:
            fetch(fine_gots[index], chosen)

    def fetch_near(index):
        if coarse_gots[index][0, 0].shape[0]:
            fetch(coarse_gots[index], near_offsets)

    half_tokens, other_tokens, grad_kept = settle(half_tokens, other_tokens, grad_kept)
    both_tokens = [half_tokens, other_tokens]

    fetch(gate_got, near_offsets)
    fetch(out_got, near_offsets)
    fetch(out_got, far_offsets)
    key_here = count * key_part
    mix_wide = 2 * key_here + count * value_part
    mix_places = []
    for at in range(count):
        mix_places += [
            (at, 0, key_part, at * key_part),
            (at, key_part, key_part, key_here + at * key_part),
            (count + at, 0, value_part, 2 * key_here + at * value_part),
        ]
    mix_places.append((2 * count, 0, BETA_LANES, mix_wide))
    mix_given = [got[offset] for got in (head_got, value_got) for offset in offsets] + [beta_block]
    taps_all = [
        value_got[offset][value_part : value_part + KERNEL, :taps_wide] for offset in offsets
    ]
    taps = jnp.concatenate(
        [piece[:, :key_part] for piece in taps_all]
        + [piece[:, key_part : 2 * key_part] for piece in taps_all]
        + [piece[:, 2 * key_part :] for piece in taps_all],
        axis=1,
    ).astype(F32)
    taps = jnp.pad(taps, ((0, 8 - KERNEL), (0, 0)))
    feed_here = count * feed_part
    mix_rows, pre, beta_pre = run_project(
        both_tokens, mix_given, mix_places, gain_f[None], scale_all, mix_wide + BETA_LANES, mix_wide
    )
    groups[:] = [gate_got, out_got] + feed_gots
    both_tokens, pre, beta_pre, taps, grad_kept = settle(
        both_tokens, pre, beta_pre, taps, grad_kept
    )

    fetch(gate_got, cross_offsets)
    fetch(out_got, cross_offsets)
    fetch_fine(0, far_offsets)
    grad_x = along_x(grad_kept)
    grad_team = swap(grad_kept, "team", 1)
    pre = pre.reshape(outer + (rows, -1))
    beta_pre = beta_pre.reshape(outer + (rows, -1))
    place = jnp.full((1,), seq_pos, jnp.int32)
    head_outs, fresh, starts, solved = run_forward(place, pre, beta_pre, cols, rows_g, taps)
    groups[:] = [gate_got, out_got] + feed_gots
    both_tokens, head_outs, grad_x, grad_team = settle(both_tokens, head_outs, grad_x, grad_team)

    grad_half_rows = rows // 32 * 16

    def part_rows(pieces, start, stop):
        return [piece[start:stop] for piece in pieces]

    fetch_fine(0, cross_offsets)
    fetch_fine(1, far_offsets)
    grad_team_low = along_x(grad_team[:grad_half_rows])
    gate_wide = count * value_part
    head_outs = head_outs.reshape(2 * length, -1)
    gate_rows, out_rows, gate_other, mixed_other, branch_other = run_branch(
        1,
        both_tokens[1],
        [got[offset] for got in (gate_got, out_got) for offset in offsets],
        [(at, 0, value_part, at * value_part) for at in range(count)],
        [(count + at, 0, value_part, at * value_part) for at in range(count)],
        gain_f[None],
        scale_all,
        head_outs,
        gain_row,
    )
    groups[:] = feed_gots
    (
        both_tokens,
        grad_team,
        grad_team_low,
        gate_rows,
        out_rows,
        gate_other,
        mixed_other,
        branch_other,
    ) = settle(
        both_tokens,
        grad_team,
        grad_team_low,
        gate_rows,
        out_rows,
        gate_other,
        mixed_other,
        branch_other,
    )
    fetch_fine(1, cross_offsets)
    fetch_near(0)
    fetch_fine(2, far_offsets)
    grad_team_high = along_x(grad_team[grad_half_rows:])
    came_all = swap(branch_other, "seq", 1)
    whole = [(0, 0, gate_wide, 0)]
    _, _, gate_own, mixed_own, branch_own = run_branch(
        0,
        both_tokens[0],
        [gate_rows, out_rows],
        whole,
        [(1, 0, gate_wide, 0)],
        jnp.ones_like(gain_f)[None],
        scale_all,
        head_outs,
        gain_row,
    )
    came_all, grad_team_high, gate_own, mixed_own, branch_own = settle(
        came_all, grad_team_high, gate_own, mixed_own, branch_own
    )
    theirs, mine = fold_came(branch_own, came_all)
    grad_team_x = [
        jnp.concatenate([low, high], axis=0) for low, high in zip(grad_team_low, grad_team_high)
    ]
    fetch_fine(2, cross_offsets)
    fetch_near(1)
    fetch_fine(3, far_offsets)
    came = send_along(theirs)
    normed = run_norm(*after(tuple(both_tokens), *theirs.values()), scale_all, gain_f[None])
    theirs, mine, came, normed = settle(theirs, mine, came, normed)

    theirs = add_along(theirs, came)
    came = send_along(mine)
    came_team = swap(theirs, "team", 1)
    fetch_fine(3, cross_offsets)
    fetch_near(2)
    fetch_fine(4, far_offsets)
    grad_half = jnp.concatenate(list(grad_x) + list(grad_team_x), axis=0)
    mine, came, came_team, grad_half = settle(mine, came, came_team, grad_half)
    middle = source_f + add_along(mine, came).astype(F32) + came_team.astype(F32)

    feed_in = rms_scale(middle, feed_gain_f).astype(BF16)
    feed_x = along_x(feed_in)
    feed_team = swap(feed_in, "team", 1)
    fetch_fine(4, cross_offsets)
    fetch_near(3)
    grad_other = swap(grad_half, "seq", 1)
    all_rows = jnp.concatenate([mix_rows, gate_rows], axis=0)
    feed_x, feed_team, grad_half, grad_other, all_rows = settle(
        feed_x, feed_team, grad_half, grad_other, all_rows
    )
    seq_grads = [grad_half, grad_other]

    feed_team_x = along_x(feed_team)

    feed_places, down_places, feed_given = [], [], []
    for at, offset in enumerate(offsets):
        if offset[0]:
            spots = [(fine_gots[index][offset], 0, index) for index in range(len(units))]
        else:
            spots = []
            for got, ranges in zip(coarse_gots, coarse_ranges):
                start = 0
                for index in ranges:
                    spots.append((got.get(offset), start, index))
                    start += 3 * units[index]
        for piece, start, index in spots:
            size = units[index]
            if not size:
                continue
            which = next((n for n, given in enumerate(feed_given) if given is piece), None)
            if which is None:
                which = len(feed_given)
                feed_given.append(piece)
            target = starts_at[index] * count + at * size
            for kind in range(3):
                one = (which, start + kind * size, size)
                if kind < 2:
                    feed_places.append((*one, kind * feed_here + target))
                else:
                    down_places.append((*one, target))
    feed_rows, down_rows, *d_hiddens = run_hidden(
        seq_grads, feed_given, feed_places, down_places, feed_here
    )
    feed_half = jnp.concatenate(list(feed_x) + list(feed_team_x), axis=0)
    groups[:] = []
    feed_half, feed_rows, down_rows, d_hiddens = settle(feed_half, feed_rows, down_rows, d_hiddens)

    seq_feed = [feed_half, swap(feed_half, "seq", 1)]
    hidden_own, d_both_own, feed_own = run_feed(seq_feed[0], feed_rows, d_hiddens[0])
    hidden_other, d_both_other, feed_other = run_feed(seq_feed[1], feed_rows, d_hiddens[1])
    hiddens, d_boths = [hidden_own, hidden_other], [d_both_own, d_both_other]
    theirs, mine = fold_rows(feed_own, feed_other)
    kept = after((tuple(hiddens), tuple(d_boths)), *theirs.values())
    came = send_along(theirs)
    feed_low = run_outer(kept[1], seq_feed)
    theirs, mine, came, feed_low, hiddens = settle(theirs, mine, came, feed_low, list(kept[0]))

    theirs = add_along(theirs, came)
    came = send_along(mine)
    came_team = swap(theirs, "team", 1)
    down_low = run_outer(hiddens, seq_grads)
    rest = slice(3, None)

    def feed_pack(at, chosen):
        rows_of = []
        for values, base in ((feed_low, 0), (feed_low, feed_here), (down_low, 0)):
            for size, start in list(zip(units, starts_at))[chosen]:
                begin = base + start * count + at * size
                rows_of.append(values[begin : begin + size])
        return jnp.concatenate(rows_of, axis=0)

    far_all = [o for o in offsets if o[0]]
    near_all = [o for o in offsets if not o[0]]
    first_sent = {
        o: feed_pack(at, slice(0, 3)) for at, o in enumerate(offsets) if all(o)
    }
    mine, came, came_team, first_sent, feed_low, down_low = settle(
        mine, came, came_team, first_sent, feed_low, down_low
    )
    d_feed_in = add_along(mine, came).astype(F32) + came_team.astype(F32)

    feed_pull = jax.vjp(rms_scale, middle, feed_gain_f)[1]
    d_mid_norm, feed_gain_term = feed_pull(d_feed_in)
    d_middle = grad_own.astype(F32) + d_mid_norm
    d_branch = d_middle.astype(BF16)
    branch_x = along_x(d_branch)
    branch_team = swap(d_branch, "team", 1)
    first_came = send_bits(first_sent, "low", list(first_sent))
    first_pieces = {
        o: first_sent[o] if o in first_sent else feed_pack(at, slice(0, 3))
        for at, o in enumerate(offsets)
    }
    rest_pieces = {o: feed_pack(at, rest) for at, o in enumerate(offsets)}
    groups[:] = [first_pieces, rest_pieces]
    branch_x, branch_team, first_came, hiddens = settle(
        branch_x, branch_team, first_came, hiddens
    )

    branch_team_x = along_x(branch_team)
    first_pieces = add_bits(first_pieces, first_came)
    first_half = 3 * first_count // 2 // 16 * 16
    first_far = {
        o: swap(piece[:first_half], "high", o[0]) for o, piece in first_pieces.items() if o[0]
    }
    rest_came = send_bits(rest_pieces, "low", far_all)
    down_own, down_other = [product_tn(hidden, down_rows).astype(BF16) for hidden in hiddens]
    down_theirs, down_mine = fold_rows(down_own, down_other)
    branch_half = jnp.concatenate(list(branch_x) + list(branch_team_x), axis=0)
    groups[:] = [first_pieces, rest_pieces]
    branch_half, rest_came, down_theirs, down_mine, first_far = settle(
        branch_half, rest_came, down_theirs, down_mine, first_far
    )

    down_came = send_along(down_theirs)
    next_far = {
        o: swap(piece[first_half:], "high", o[0]) for o, piece in first_pieces.items() if o[0]
    }
    rest_near = send_bits(rest_pieces, "low", near_all)
    seq_branch = [branch_half, swap(branch_half, "seq", 1)]
    d_outs, d_gate_pre, head_gain_term, mixer_terms = run_mixer_back(
        seq_branch,
        out_rows,
        head_outs,
        [gate_own, gate_other],
        [mixed_own, mixed_other],
        normed,
        gain_row,
        value_part,
    )
    def gate_pack(at):
        return cut(mixer_terms, at, 2 * value_part)

    groups[:] = [rest_pieces, first_pieces]
    d_outs, down_theirs, down_mine, down_came, next_far, rest_near, mixer_terms = (
        settle(
            d_outs,
            down_theirs,
            down_mine,
            down_came,
            next_far,
            rest_near,
            mixer_terms,
        )
    )
    gate_first = {o: gate_pack(at) for at, o in enumerate(offsets) if all(o)}
    rest_pieces = add_bits(rest_pieces, rest_came)

    head_terms = head_gain_term[0].reshape(low_count, DV // low_count)
    head_terms = jnp.concatenate(
        [
            lax.dynamic_index_in_dim(head_terms, at ^ low_pos, 0, False)
            for at in range(low_count)
        ],
        axis=0,
    ).reshape(devices, head_part)
    head_terms = jnp.pad(head_terms, ((0, 0), (0, gain_part - head_part))).reshape(1, model)
    small_base = jnp.concatenate(
        [
            jnp.zeros((H + 1, model), F32),
            feed_gain_term[None],
            head_terms,
            jnp.zeros((5, model), F32),
        ],
        axis=0,
    )

    rest_far = send_bits(rest_pieces, "high", list(rest_pieces))
    gate_came = send_bits(gate_first, "low", list(gate_first))
    first_near = send_bits(first_pieces, "low", near_all)
    down_theirs = add_along(down_theirs, down_came)
    down_came = send_along(down_mine)
    down_team = swap(down_theirs, "team", 1)
    wide_shape = outer + (rows, -1)
    d_all, d_taps = run_backward(
        place,
        pre,
        d_outs.reshape(wide_shape),
        d_gate_pre.reshape(wide_shape),
        beta_pre,
        cols,
        rows_g,
        taps,
        fresh,
        starts,
        solved,
    )
    groups[:] = []
    small_base, mixer_terms, d_all, d_taps, down_mine, down_came, down_team, gate_came, rest_far, first_near = settle(
        small_base, mixer_terms, d_all, d_taps, down_mine, down_came, down_team, gate_came, rest_far, first_near
    )
    d_all = d_all.reshape(2 * length, -1)

    gate_later = {o: gate_pack(at) for at, o in enumerate(offsets) if not all(o)}
    gate_near = send_bits(gate_later, "low", near_all)
    gate_pieces = add_bits({**gate_first, **gate_later}, gate_came)
    gate_far = {
        o: swap(piece[:value_part], "high", o[0]) for o, piece in gate_pieces.items() if o[0]
    }
    d_all = after(d_all, *[piece for o, piece in gate_pieces.items() if o[0]])
    def taps_of(start, part):
        return d_taps[:KERNEL, start : start + count * part].reshape(KERNEL, count, part)

    taps_rows = jnp.concatenate(
        [
            taps_of(0, key_part),
            taps_of(key_here, key_part),
            taps_of(2 * key_here, value_part),
        ],
        axis=2,
    ).transpose(1, 0, 2)
    taps_rows = jnp.pad(taps_rows, ((0, 0), (0, 16 - KERNEL), (0, model - taps_wide)))
    taps_rows = taps_rows.reshape(count * 16, model).astype(BF16)
    mix_low = run_weigh(d_all, normed, taps_rows, (count, key_part, value_part))
    piece_rows = 2 * key_part + value_part + 16
    beta_term = mix_low[count * piece_rows : count * piece_rows + heads].astype(F32)

    def mix_pack(at):
        return cut(mix_low, at, piece_rows)

    groups[:] = [gate_pieces]
    d_all, gate_far, gate_near, mix_low, d_taps, down_mine, down_came, down_team = settle(
        d_all, gate_far, gate_near, mix_low, d_taps, down_mine, down_came, down_team
    )
    mix_sent = {o: mix_pack(at) for at, o in enumerate(offsets) if all(o)}

    def part_of(pieces, start, stop):
        return {o: piece[start:stop] for o, piece in pieces.items()}

    out_pieces = {o: piece[value_part:] for o, piece in gate_pieces.items() if o[0]}
    out_half = value_part // 32 * 16
    mix_half = (2 * key_part + value_part + 16) // 32 * 16
    out_far = send_bits(part_of(out_pieces, 0, out_half), "high", list(out_pieces))
    mix_came = send_bits(part_of(mix_sent, 0, mix_half), "low", list(mix_sent))
    normed_other, gain_other = run_back(d_all, all_rows, normed, 1)
    d_all, normed_other, gain_other, out_far, mix_came, out_pieces, mix_sent = settle(
        d_all, normed_other, gain_other, out_far, mix_came, out_pieces, mix_sent
    )
    out_next = send_bits(part_of(out_pieces, out_half, None), "high", list(out_pieces))
    mix_next = send_bits(part_of(mix_sent, mix_half, None), "low", list(mix_sent))
    came_other = swap(normed_other, "seq", 1)
    normed_own, gain_own = run_back(d_all, all_rows, normed, 0)
    groups[:] = [gate_pieces, first_pieces, rest_pieces]
    (
        normed_own,
        gain_own,
        came_other,
        out_next,
        mix_next,
        gain_other,
        down_mine,
        down_came,
        down_team,
        beta_term,
        mix_low,
    ) = settle(
        normed_own,
        gain_own,
        came_other,
        out_next,
        mix_next,
        gain_other,
        down_mine,
        down_came,
        down_team,
        beta_term,
        mix_low,
    )
    mix_came = {o: jnp.concatenate([mix_came[o], mix_next[o]], axis=0) for o in mix_came}
    theirs, _ = fold_came(normed_own, came_other)
    mixer_gain_term = (gain_own[0] + gain_other[0]) / (gain_f * gain_f)
    row_ids = lax.broadcasted_iota(jnp.int32, (H + 8, model), 0)
    small_rows = jnp.where(row_ids == H, mixer_gain_term[None], small_base)
    for head in range(heads):
        small_rows = jnp.where(row_ids == head_places[head], beta_term[head][None], small_rows)
    blocks = model // (low_count * gain_part)
    small_terms = small_rows.reshape(H + 8, blocks, -1).transpose(1, 0, 2)
    small_terms = small_terms.reshape(pieces_x, 2, high_count, 2, H + 8, -1)
    groups[:] = []
    theirs_sent = {at: piece for at, piece in theirs.items() if at}
    theirs_sent, normed_own, came_other, small_terms, mix_came, mix_sent, mix_low = settle(
        theirs_sent, normed_own, came_other, small_terms, mix_came, mix_sent, mix_low
    )

    mix_pieces = {
        o: mix_sent[o] if o in mix_sent else mix_pack(at) for at, o in enumerate(offsets)
    }
    mix_pieces = add_bits(mix_pieces, mix_came)
    groups[:] = [mix_pieces, gate_pieces, first_pieces, rest_pieces]
    theirs, mine = fold_came(normed_own, came_other)
    theirs.update(theirs_sent)
    came = send_along(theirs)
    mix_far = {
        o: swap(piece[: 2 * key_part], "high", o[0]) for o, piece in mix_pieces.items() if o[0]
    }
    mix_near = send_bits(mix_pieces, "low", near_all)
    small_terms = sum_stage(small_terms, "team", 3)
    small_terms = sum_stage(small_terms, "seq", 1, (1,))
    small_terms = sum_stage(small_terms, "high", 2)
    theirs, mine, came, small_terms, mix_far, mix_near, first_near, rest_near, rest_far = settle(
        theirs, mine, came, small_terms, mix_far, mix_near, first_near, rest_near, rest_far
    )

    theirs = add_along(theirs, came)
    came_team = swap(theirs, "team", 1)
    small_terms = sum_stage(small_terms, "seq", 0, bits_of(seq_count)[1:])
    came = send_along({at: after(piece, small_terms) for at, piece in mine.items()})
    for bit in bits_of(low_count):
        small_terms = small_terms + swap(small_terms, "low", bit)
    value_far = {
        o: swap(piece[2 * key_part :], "high", o[0]) for o, piece in mix_pieces.items() if o[0]
    }
    given = []

    def known(piece):
        for at, other in enumerate(given):
            if other is piece:
                return at
        given.append(piece)
        return len(given) - 1

    def segment(size, start, pieces, parts=()):
        sources = [(known(piece), start) for piece in pieces]
        for begin, more in parts:
            sources += [(known(piece), start - begin) for piece in more]
        return size, sources

    def spans(start, size, cut_at):
        if start < cut_at < start + size:
            return [(start, cut_at - start), (cut_at, start + size - cut_at)]
        return [(start, size)]

    mix_all = [mix_pieces[0, 0], *mix_near.values()]
    gate_all = [gate_pieces[0, 0], *gate_near.values()]
    first_all = [first_pieces[0, 0], *first_near.values()]
    rest_all = [rest_pieces[0, 0], *rest_near.values(), *rest_far.values()]
    rest_count = feed_part - first_count
    outputs = [
        ([segment(key_part, 0, mix_all + list(mix_far.values()))], False),
        ([segment(key_part, key_part, mix_all + list(mix_far.values()))], False),
        ([segment(value_part, 0, gate_all + list(gate_far.values()))], True),
        (
            [
                segment(
                    size,
                    start,
                    gate_all,
                    [
                        (value_part, out_far.values())
                        if start < value_part + out_half
                        else (value_part + out_half, out_next.values())
                    ],
                )
                for start, size in spans(value_part, value_part, value_part + out_half)
            ],
            False,
        ),
    ]
    for kind in range(3):
        segments = [
            segment(
                size,
                start,
                first_all,
                [(0, first_far.values()) if start < first_half else (first_half, next_far.values())],
            )
            for start, size in spans(kind * first_count, first_count, first_half)
        ]
        segments.append(segment(rest_count, kind * rest_count, rest_all))
        outputs.append((segments, False))
    finished = run_finish(given, outputs)
    mine, came, came_team, value_far, small_terms, finished = settle(
        mine, came, came_team, value_far, small_terms, finished
    )
    small_rows = small_terms.reshape(H + 8, low_count, gain_part)
    small_rows = sum(
        jnp.where(low_pos == at, small_rows[:, at], 0.0) for at in range(low_count)
    )
    beta_sum = small_rows[:H].T
    d_source = add_along(mine, came).astype(F32) + came_team.astype(F32)
    unit = source_f * scale_own
    d_norm = scale_own * (d_source - unit * jnp.mean(unit * d_source, axis=-1, keepdims=True))
    tokens_grad = (d_middle + d_norm).astype(BF16)[None]
    block_out = middle + add_along(down_mine, down_came).astype(F32) + down_team.astype(F32)
    block_out = block_out.astype(BF16)[None]

    value_sum = sum(
        [piece[2 * key_part :].astype(F32) for piece in mix_near.values()],
        mix_pieces[0, 0][2 * key_part :].astype(F32),
    )
    value_sum = sum([piece.astype(F32) for piece in value_far.values()], value_sum)
    taps_sum = value_sum[value_part : value_part + KERNEL, :taps_wide]

    return (
        block_out,
        tokens_grad,
        small_rows[H],
        finished[0].T,
        finished[1].T,
        value_sum[:value_part].T,
        beta_sum,
        finished[2],
        taps_sum[:, :key_part],
        taps_sum[:, key_part : 2 * key_part],
        taps_sum[:, 2 * key_part :],
        small_rows[H + 2, :head_part],
        finished[3],
        small_rows[H + 1],
        finished[4].T,
        finished[5].T,
        finished[6],
    )


def solution(mesh):
    in_specs = (
        P(BATCH, "seq", None),
        P(BATCH, None, "seq"),
        P(BATCH, "seq", None),
        P(ALL),
        P(None, ALL),
        P(None, ALL),
        P(None, ALL),
        P(ALL, None),
        P(None, ALL),
        P(None, ALL),
        P(None, ALL),
        P(None, ALL),
        P(ALL),
        P(ALL, None),
        P(ALL),
        P(None, ALL),
        P(None, ALL),
        P(ALL, None),
    )
    out_specs = (
        P(BATCH, "seq", None),
        P(BATCH, "seq", None),
        P(ALL),
        P(None, ALL),
        P(None, ALL),
        P(None, ALL),
        P(ALL, None),
        P(None, ALL),
        P(None, ALL),
        P(None, ALL),
        P(None, ALL),
        P(ALL),
        P(ALL, None),
        P(ALL),
        P(None, ALL),
        P(None, ALL),
        P(ALL, None),
    )
    seq_count, batch_count = mesh.shape["seq"], mesh.shape["batch"]
    team = seq_count * batch_count // H
    split = mesh.devices.reshape(seq_count, batch_count // (2 * team), 2, team)
    mesh = Mesh(split, ("seq", "high", "team", "low"))
    return jax.shard_map(local, mesh=mesh, in_specs=in_specs, out_specs=out_specs, check_vma=False)
```

time: 1100 us -> 783 us (0.71)
  waiting for transfers between devices: 485 us -> 233 us
  matrix products: 223 us -> 7.42 us
  Pallas kernels: 92.5 us -> 301 us
  local copies, waits for them, and re-layouts: 140 us -> 75 us
  starting transfers between devices: 70.6 us -> 91 us
  other arithmetic: 81.3 us -> 68.5 us
    ppermute x93 -> x89, waiting for transfers between devices: 485 us -> 233 us  [swap(): lax.ppermute(values, axis, [(place, place ^ bit) for place in range(count)])]
    pallas_call x1 -> x14, Pallas kernels: 5.01 us -> 213 us  [the longest x2 39.2 us: run_feed(): pl.pallas_call(feed_body, grid=(length // tile,), in_specs=[pl.BlockSpec(...]
    dot_general x22 -> x0, matrix products: 165 us -> none  [the longest x12 88.5 us: product(): return jnp.dot(left_side, right_side, preferred_element_type=F32)]
    unnamed x329 -> x184, local copies, waits for them, and re-layouts: 86.7 us -> 32.3 us
    dot_general x8 -> x2, matrix products: 58.3 us -> 7.42 us  [product_tn(): lax.dot_general(left_side, right_side, (((0,), (0,)), ((), ())), preferre...]
    ppermute x93 -> x89, starting transfers between devices: 70.6 us -> 91 us  [swap(): lax.ppermute(values, axis, [(place, place ^ bit) for place in range(count)])]
    slice x29 -> x20, local copies, waits for them, and re-layouts: 23.2 us -> 7.52 us  [the longest x4 2.38 us: part_of(): return {o: piece[start:stop] for o, piece in pieces.items()}]
    convert_element_type x12 -> x5, other arithmetic: 24.4 us -> 17 us  [add_low(): return (left_side.astype(F32) + right_side.astype(F32)).astype(BF16)]
  transfers between devices with their start and end apart: 93 -> 89, of which waited for: 35 -> 39; matrix products, arithmetic and copies ran while one was open for 33% -> 13% of each run, Pallas kernels for 4% -> 36%
where the time goes in v2:
time: 783 us; the launch traced here: 778 us
  Pallas kernels  301 us (38%)
  waiting for transfers between devices  233 us (30%)
  starting transfers between devices  91 us (12%)
  local copies, waits for them, and re-layouts  75 us (10%)
  other arithmetic  68.5 us (9%)
    ppermute x89, waiting for transfers between devices, swap(): lax.ppermute(values, axis, [(place, place ^ bit) for place in range(count)])  233 us
    ppermute x89, starting transfers between devices, swap(): lax.ppermute(values, axis, [(place, place ^ bit) for place in range(count)])  91 us
    pallas_call x1, Pallas kernels, run_backward(): pl.pallas_call(functools.partial(backward_body, heads), grid_spec=grid_sp...  49.8 us
    pallas_call x2, Pallas kernels, run_feed(): pl.pallas_call(feed_body, grid=(length // tile,), in_specs=[pl.BlockSpec(...  39.2 us
    pallas_call x1, Pallas kernels, run_forward(): pl.pallas_call(functools.partial(forward_body, heads), grid_spec=grid_spe...  38.4 us
    unnamed x184, local copies, waits for them, and re-layouts  32.3 us
    pallas_call x2, Pallas kernels, run_outer(): pl.pallas_call(outer_body, grid=(wide // tile,), in_specs=[left, left, ri...  29.5 us
    pallas_call x2, Pallas kernels, run_back(): pl.pallas_call(back_body, grid=(length // tile,), in_specs=[pl.BlockSpec(...  26.3 us
  transfers between devices with their start and end apart: 89, of which 39 were waited for; matrix products, arithmetic and copies ran while one was open for 13% of the time, Pallas kernels for 36%

profile of v2, /device:TPU:0, one launch (start us, length us, event | category | flops | bytes accessed | tf_op | source)
XLA Modules:
  0.0 778.4 jit_solution(6324692451925766211)
XLA Ops:
  31.1 5.1 collective-permute-done.5
  42.8 15.1 %collective-permute-done.10.refs_2_ = bf16[128,2048]{1,0:T(8,128)(2,1)S(1)} collective-permute-done((bf16[128,2048]{1,0:T(8,128)(2,1)S(1)}, bf16[128,2048]{1,0:T(8,128)(2,1)S(1)}, u32[]{:S(2)}, u32[]{:S(2)}) %collective-permute-start.10) | collective-permute-done | bytes 524320 | tf_op jit(solution)/shard_map/ppermute | solution.py:938
  74.9 10.2 %collective-permute-done.12 = bf16[256,2048]{1,0:T(8,128)(2,1)} collective-permute-done((bf16[256,2048]{1,0:T(8,128)(2,1)}, bf16[256,2048]{1,0:T(8,128)(2,1)}, u32[]{:S(2)}, u32[]{:S(2)}) %collective-permute-start.12) | collective-permute-done | bytes 1048608 | tf_op jit(solution)/shard_map/ppermute | solution.py:938
  97.2 19.5 %collective-permute-done.18.refs_2_ = bf16[128,2048]{1,0:T(8,128)(2,1)S(1)} collective-permute-done((bf16[128,2048]{1,0:T(8,128)(2,1)S(1)}, bf16[128,2048]{1,0:T(8,128)(2,1)S(1)}, u32[]{:S(2)}, u32[]{:S(2)}) %collective-permute-start.18) | collective-permute-done | bytes 524320 | tf_op jit(solution)/shard_map/ppermute | solution.py:938
  123.6 18.7 %project_rows.1 = (bf16[1152,2048]{1,0:T(8,128)(2,1)}, bf16[2048,1024]{1,0:T(8,128)(2,1)}, f32[2048,128]{1,0:T(8,128)}) custom-call(bf16[1024,2048]{1,0:T(8,128)(2,1)} %pad_maximum_fusion.1.half.tokens, bf16[1024,2048]{1,0:T(8,128)(2,1)} %collective-permute-done.16.other.tokens, f32[1,2048]{1,0:T(1,128)S(1)} %bitcast.130, f32[2048,1]{1,0:T(8,128)} %copy.123.scale, ...), custom_call_target="tpu_custom_call" | custom-call | tf_op jit(solution)/shard_map/project_rows/pallas_call | solution.py:482
  153.5 38.4 %delta_forward.1 = (bf16[2,2,2,256,512]{4,3,2,1,0:T(8,128)(2,1)}, bf16[2,2,2,256,512]{4,3,2,1,0:T(8,128)(2,1)}, bf16[8,4,128,256]{3,2,1,0:T(8,128)(2,1)}, bf16[8,4,128,128]{3,2,1,0:T(8,128)(2,1)S(1)}) custom-call(s32[1]{0:T(128)} %bitcast.32.place, bf16[2,2,2,256,1024]{4,3,2,1,0:T(8,128)(2,1)} %bitcast.138, f32[2,2,2,256,128]{4,3,2,1,0:T(8,128)} %bitcast.124, ...), custom_call_target="tpu_custom_call" | custom-call | tf_op jit(solution)/shard_map/delta_forward/pallas_call | solution.py:344
  199.9 11.0 %branch_rows.2 = (bf16[512,2048]{1,0:T(8,128)(2,1)}, bf16[512,2048]{1,0:T(8,128)(2,1)}, bf16[1024,512]{1,0:T(8,128)(2,1)}, bf16[1024,512]{1,0:T(8,128)(2,1)}, bf16[1024,2048]{1,0:T(8,128)(2,1)}) custom-call(bf16[1024,2048]{1,0:T(8,128)(2,1)} %collective-permute-done.16.other.tokens, f32[1,2048]{1,0:T(1,128)S(1)} %bitcast.131, f32[2048,1]{1,0:T(8,128)} %copy.123.scale, ...), custom_call_target="tpu_custom_call" | custom-call | tf_op jit(solution)/shard_map/branch_rows/pallas_call | solution.py:840
  214.9 11.5 %branch_rows.3 = (bf16[512,2048]{1,0:T(8,128)(2,1)}, bf16[512,2048]{1,0:T(8,128)(2,1)}, bf16[1024,512]{1,0:T(8,128)(2,1)S(1)}, bf16[1024,512]{1,0:T(8,128)(2,1)}, bf16[1024,2048]{1,0:T(8,128)(2,1)}) custom-call(bf16[1024,2048]{1,0:T(8,128)(2,1)} %pad_maximum_fusion.1.half.tokens, f32[1,2048]{1,0:T(1,128)S(1)} %broadcast_in_dim_broadcast_in_dim.3.gain, ...), custom_call_target="tpu_custom_call" | custom-call | tf_op jit(solution)/shard_map/branch_rows/pallas_call | solution.py:840
  242.9 9.7 %norm_rows.1.normed = bf16[2048,2048]{1,0:T(8,128)(2,1)} custom-call(bf16[1024,2048]{1,0:T(8,128)(2,1)} %pad_maximum_fusion.1.half.tokens, bf16[1024,2048]{1,0:T(8,128)(2,1)} %collective-permute-done.16.other.tokens, f32[2048,1]{1,0:T(8,128)S(1)} %copy-done, f32[1,2048]{1,0:T(1,128)S(1)} %bitcast.132), custom_call_target="tpu_custom_call" | custom-call | tf_op jit(solution)/shard_map/norm_rows/pallas_call | solution.py:428
  252.6 10.6 %collective-permute-done.36.refs_15_ = bf16[96,2048]{1,0:T(8,128)(2,1)S(1)} collective-permute-done((bf16[96,2048]{1,0:T(8,128)(2,1)S(1)}, bf16[96,2048]{1,0:T(8,128)(2,1)S(1)}, u32[]{:S(2)}, u32[]{:S(2)}) %collective-permute-start.36) | collective-permute-done | bytes 393248 | tf_op jit(solution)/shard_map/ppermute | solution.py:938
  278.7 20.4 %collective-permute-done.42.refs_12_ = bf16[96,2048]{1,0:T(8,128)(2,1)S(1)} collective-permute-done((bf16[96,2048]{1,0:T(8,128)(2,1)S(1)}, bf16[96,2048]{1,0:T(8,128)(2,1)S(1)}, u32[]{:S(2)}, u32[]{:S(2)}) %collective-permute-start.42) | collective-permute-done | bytes 393248 | tf_op jit(solution)/shard_map/ppermute | solution.py:938
  306.8 7.0 pad_maximum_fusion.weights
  316.9 7.3 collective-permute-done.48.refs_7_
  329.9 16.7 %hidden_cotangents.1 = (bf16[1408,2048]{1,0:T(8,128)(2,1)}, bf16[704,2048]{1,0:T(8,128)(2,1)}, bf16[704,1024]{1,0:T(8,128)(2,1)}, bf16[704,1024]{1,0:T(8,128)(2,1)}) custom-call(bf16[1024,2048]{1,0:T(8,128)(2,1)} %constant_dynamic-update-slice_fusion.8.first.right_first, bf16[1024,2048]{1,0:T(8,128)(2,1)} %collective-permute-done.46.second.right_second, ...), custom_call_target="tpu_custom_call" | custom-call | tf_op jit(solution)/shard_map/hidden_cotangents/pallas_call | solution.py:523
  346.6 6.5 collective-permute-done.49
  355.2 7.3 collective-permute-done.50.feed.right_second
  362.5 19.8 %feed_forward.3 = (bf16[704,1024]{1,0:T(8,128)(2,1)S(1)}, bf16[1408,1024]{1,0:T(8,128)(2,1)}, bf16[1024,2048]{1,0:T(8,128)(2,1)}) custom-call(bf16[1024,2048]{1,0:T(8,128)(2,1)} %collective-permute-done.50.feed.right_second, bf16[1408,2048]{1,0:T(8,128)(2,1)} %get-tuple-element.597.weights, bf16[704,1024]{1,0:T(8,128)(2,1)} %get-tuple-element.600.back), custom_call_target="tpu_custom_call" | custom-call | tf_op jit(solution)/shard_map/feed_forward/pallas_call | solution.py:570
  383.5 19.4 %feed_forward.2 = (bf16[704,1024]{1,0:T(8,128)(2,1)S(1)}, bf16[1408,1024]{1,0:T(8,128)(2,1)}, bf16[1024,2048]{1,0:T(8,128)(2,1)}) custom-call(bf16[1024,2048]{1,0:T(8,128)(2,1)} %copy-done.8, bf16[1408,2048]{1,0:T(8,128)(2,1)} %get-tuple-element.597.weights, bf16[704,1024]{1,0:T(8,128)(2,1)} %get-tuple-element.598.back), custom_call_target="tpu_custom_call" | custom-call | tf_op jit(solution)/shard_map/feed_forward/pallas_call | solution.py:570
  408.6 18.1 %outer_sums.2 = bf16[1408,2048]{1,0:T(8,128)(2,1)} custom-call(bf16[1408,1024]{1,0:T(8,128)(2,1)} %get-tuple-element.606.first, bf16[1408,1024]{1,0:T(8,128)(2,1)} %get-tuple-element.607.second, bf16[1024,2048]{1,0:T(8,128)(2,1)} %copy-done.8, bf16[1024,2048]{1,0:T(8,128)(2,1)} %collective-permute-done.50.feed.right_second), custom_call_target="tpu_custom_call" | custom-call | tf_op jit(solution)/shard_map/outer_sums/pallas_call | solution.py:605
  426.7 6.1 collective-permute-done.52
  442.9 11.4 %outer_sums.3 = bf16[704,2048]{1,0:T(8,128)(2,1)} custom-call(bf16[704,1024]{1,0:T(8,128)(2,1)S(1)} %get-tuple-element.627.first, bf16[704,1024]{1,0:T(8,128)(2,1)} %copy-done.2, bf16[1024,2048]{1,0:T(8,128)(2,1)} %constant_dynamic-update-slice_fusion.8.first.right_first, bf16[1024,2048]{1,0:T(8,128)(2,1)} %collective-permute-done.46.second.right_second), custom_call_target="tpu_custom_call" | custom-call | tf_op jit(solution)/shard_map/outer_sums/pallas_call | solution.py:605
  457.0 7.5 collective-permute-done.54
  480.2 13.2 %collective-permute-done.55 = bf16[256,2048]{1,0:T(8,128)(2,1)S(1)} collective-permute-done((bf16[256,2048]{1,0:T(8,128)(2,1)S(1)}, bf16[256,2048]{1,0:T(8,128)(2,1)S(1)}, u32[]{:S(2)}, u32[]{:S(2)}) %collective-permute-start.55) | collective-permute-done | bytes 1048608 | tf_op jit(solution)/shard_map/ppermute | solution.py:938
  510.6 17.5 %collective-permute-done.58 = bf16[256,2048]{1,0:T(8,128)(2,1)S(1)} collective-permute-done((bf16[256,2048]{1,0:T(8,128)(2,1)S(1)}, bf16[256,2048]{1,0:T(8,128)(2,1)S(1)}, u32[]{:S(2)}, u32[]{:S(2)}) %collective-permute-start.58) | collective-permute-done | bytes 1048608 | tf_op jit(solution)/shard_map/ppermute | solution.py:938
  540.1 23.0 %mixer_backward.1 = (bf16[2048,512]{1,0:T(8,128)(2,1)}, bf16[2048,512]{1,0:T(8,128)(2,1)}, f32[8,256]{1,0:T(8,128)S(1)}, bf16[1024,2048]{1,0:T(8,128)(2,1)}) custom-call(bf16[1024,2048]{1,0:T(8,128)(2,1)} %copy-done.12, bf16[1024,2048]{1,0:T(8,128)(2,1)} %collective-permute-done.62.branch_other, bf16[512,2048]{1,0:T(8,128)(2,1)} %get-tuple-element.492.refs_1_.out_rows, ...), custom_call_target="tpu_custom_call" | custom-call | tf_op jit(solution)/shard_map/mixer_backward/pallas_call | solution.py:786
  575.9 49.8 %delta_backward.1 = (bf16[2,2,2,256,1664]{4,3,2,1,0:T(8,128)(2,1)}, f32[8,1024]{1,0:T(8,128)S(1)}) custom-call(s32[1]{0:T(128)} %bitcast.32.place, bf16[2,2,2,256,1024]{4,3,2,1,0:T(8,128)(2,1)} %bitcast.139, bf16[2,2,2,256,1024]{4,3,2,1,0:T(8,128)(2,1)} %bitcast.140, bf16[2,2,2,256,512]{4,3,2,1,0:T(8,128)(2,1)} %bitcast.154, ...), custom_call_target="tpu_custom_call" | custom-call | tf_op jit(solution)/shard_map/delta_backward/pallas_call | solution.py:400
  631.0 18.1 %weight_sums.1 = bf16[1216,2048]{1,0:T(8,128)(2,1)} custom-call(bf16[2048,1664]{1,0:T(8,128)(2,1)} %bitcast.135, bf16[2048,2048]{1,0:T(8,128)(2,1)} %norm_rows.1.normed, bf16[64,2048]{1,0:T(8,128)(2,1)S(1)} %bitcast.129), custom_call_target="tpu_custom_call" | custom-call | tf_op jit(solution)/shard_map/weight_sums/pallas_call | solution.py:694
  657.2 13.1 %back_rows.2 = (bf16[1024,2048]{1,0:T(8,128)(2,1)}, f32[8,2048]{1,0:T(8,128)S(1)}) custom-call(bf16[2048,1664]{1,0:T(8,128)(2,1)} %bitcast.136, bf16[1664,2048]{1,0:T(8,128)(2,1)} %pad_maximum_fusion.weights, bf16[2048,2048]{1,0:T(8,128)(2,1)} %norm_rows.1.normed), custom_call_target="tpu_custom_call" | custom-call | tf_op jit(solution)/shard_map/back_rows/pallas_call | solution.py:631
  675.6 13.2 %back_rows.3 = (bf16[1024,2048]{1,0:T(8,128)(2,1)}, f32[8,2048]{1,0:T(8,128)S(1)}) custom-call(bf16[2048,1664]{1,0:T(8,128)(2,1)} %bitcast.137, bf16[1664,2048]{1,0:T(8,128)(2,1)} %pad_maximum_fusion.weights, bf16[2048,2048]{1,0:T(8,128)(2,1)} %norm_rows.1.normed), custom_call_target="tpu_custom_call" | custom-call | tf_op jit(solution)/shard_map/back_rows/pallas_call | solution.py:631
  706.3 18.0 %collective-permute-done.81 = f32[2,1,1,1,24,128]{5,4,3,2,1,0:T(8,128)S(1)} collective-permute-done((f32[2,1,1,1,24,128]{5,4,3,2,1,0:T(8,128)S(1)}, f32[2,1,1,1,24,128]{5,4,3,2,1,0:T(8,128)S(1)}, u32[]{:S(2)}, u32[]{:S(2)}) %collective-permute-start.81) | collective-permute-done | bytes 24608 | tf_op jit(solution)/shard_map/ppermute | solution.py:938
  738.2 9.1 %finish_sums.1 = (f32[64,2048]{1,0:T(8,128)}, f32[64,2048]{1,0:T(8,128)}, f32[2048,128]{1,0:T(8,128)}, f32[128,2048]{1,0:T(8,128)}, f32[176,2048]{1,0:T(8,128)},...) custom-call(bf16[272,2048]{1,0:T(8,128)(2,1)} %get-tuple-element.758.refs_0_, bf16[272,2048]{1,0:T(8,128)(2,1)} %copy-done.23, ...), custom_call_target="tpu_custom_call" | custom-call | tf_op jit(solution)/shard_map/finish_sums/pallas_call | solution.py:903
  747.3 15.7 %collective-permute-done.87 = bf16[144,2048]{1,0:T(8,128)(2,1)S(1)} collective-permute-done((bf16[144,2048]{1,0:T(8,128)(2,1)S(1)}, bf16[144,2048]{1,0:T(8,128)(2,1)S(1)}, u32[]{:S(2)}, u32[]{:S(2)}) %collective-permute-start.87) | collective-permute-done | bytes 589856 | tf_op jit(solution)/shard_map/ppermute | solution.py:938
  (519 shorter events, 287.7 us)
Async XLA Ops:
  26.1 34.0 %collective-permute-start.9 = (bf16[256,2048]{1,0:T(8,128)(2,1)S(1)}, bf16[256,2048]{1,0:T(8,128)(2,1)}, u32[]{:S(2)}, u32[]{:S(2)}) collective-permute-start(bf16[256,2048]{1,0:T(8,128)(2,1)S(1)} %bitcast.142), channel_id=1, source_target_pairs={{0,2},{2,0},{1,3},{3,1},{4,6},{6,4},{5,7},{7,5},{8,10},{10,8},{9,1... | collective-permute-start | bytes 3145736 | tf_op jit(solution)/shard_map/ppermute | solution.py:938
  29.3 28.7 %collective-permute-start.10 = (bf16[128,2048]{1,0:T(8,128)(2,1)S(1)}, bf16[128,2048]{1,0:T(8,128)(2,1)S(1)}, u32[]{:S(2)}, u32[]{:S(2)}) collective-permute-start(bf16[128,2048]{1,0:T(8,128)(2,1)S(1)} %pad_maximum_fusion.8.refs_0_), channel_id=1, source_target_pairs={{0,4},{4,0},{1,5},{5,1},{2,6},{6,2},{3,7},{7,3},{8,12},{12,8},{9,1... | collective-permute-start | bytes 1572872 | tf_op jit(solution)/shard_map/ppermute | solution.py:938
  29.6 28.4 %collective-permute-start.11 = (bf16[128,2048]{1,0:T(8,128)(2,1)S(1)}, bf16[128,2048]{1,0:T(8,128)(2,1)S(1)}, u32[]{:S(2)}, u32[]{:S(2)}) collective-permute-start(bf16[128,2048]{1,0:T(8,128)(2,1)S(1)} %pad_maximum_fusion.8.refs_0_), channel_id=1, source_target_pairs={{0,1},{1,0},{2,3},{3,2},{4,5},{5,4},{6,7},{7,6},{8,9},{9,8},{10,11... | collective-permute-start | bytes 1572872 | tf_op jit(solution)/shard_map/ppermute | solution.py:938
  60.3 28.4 %collective-permute-start.14 = (bf16[144,2048]{1,0:T(8,128)(2,1)}, bf16[144,2048]{1,0:T(8,128)(2,1)}, u32[]{:S(2)}, u32[]{:S(2)}) collective-permute-start(bf16[144,2048]{1,0:T(8,128)(2,1)} %pad_maximum_fusion.5.refs_4_), channel_id=1, source_target_pairs={{0,4},{4,0},{1,5},{5,1},{2,6},{6,2},{3,7},{7,3},{8,12},{12,8},{9,1... | collective-permute-start | bytes 1769480 | tf_op jit(solution)/shard_map/ppermute | solution.py:938
  88.7 28.0 %collective-permute-start.16 = (bf16[1024,2048]{1,0:T(8,128)(2,1)}, bf16[1024,2048]{1,0:T(8,128)(2,1)}, u32[]{:S(2)}, u32[]{:S(2)}) collective-permute-start(bf16[1024,2048]{1,0:T(8,128)(2,1)} %pad_maximum_fusion.1.half.tokens), channel_id=1, source_target_pairs={{0,8},{8,0},{16,24},{24,16},{1,9},{9,1},{17,25},{25,17},{2,10},{10... | collective-permute-start | bytes 12582920 | tf_op jit(solution)/shard_map/ppermute | solution.py:938
  116.7 28.2 %collective-permute-start.20 = (bf16[128,2048]{1,0:T(8,128)(2,1)}, bf16[128,2048]{1,0:T(8,128)(2,1)}, u32[]{:S(2)}, u32[]{:S(2)}) collective-permute-start(bf16[128,2048]{1,0:T(8,128)(2,1)} %refs_4_), channel_id=1, source_target_pairs={{0,1},{1,0},{2,3},{3,2},{4,5},{5,4},{6,7},{7,6},{8,9},{9,8},{10,11... | collective-permute-start | bytes 1572872 | tf_op jit(solution)/shard_map/ppermute | solution.py:938
  144.9 48.1 %collective-permute-start.22 = (bf16[256,2048]{1,0:T(8,128)(2,1)}, bf16[256,2048]{1,0:T(8,128)(2,1)}, u32[]{:S(2)}, u32[]{:S(2)}) collective-permute-start(bf16[256,2048]{1,0:T(8,128)(2,1)} %bitcast.151), channel_id=1, source_target_pairs={{0,16},{8,24},{16,0},{24,8},{1,17},{9,25},{17,1},{25,9},{2,18},{10... | collective-permute-start | bytes 3145736 | tf_op jit(solution)/shard_map/ppermute | solution.py:938
  145.7 47.3 %collective-permute-start.23 = (bf16[256,2048]{1,0:T(8,128)(2,1)}, bf16[256,2048]{1,0:T(8,128)(2,1)}, u32[]{:S(2)}, u32[]{:S(2)}) collective-permute-start(bf16[256,2048]{1,0:T(8,128)(2,1)} %bitcast.152), channel_id=1, source_target_pairs={{0,2},{2,0},{1,3},{3,1},{4,6},{6,4},{5,7},{7,5},{8,10},{10,8},{9,1... | collective-permute-start | bytes 3145736 | tf_op jit(solution)/shard_map/ppermute | solution.py:938
  148.4 44.5 %collective-permute-start.26 = (bf16[144,2048]{1,0:T(8,128)(2,1)}, bf16[144,2048]{1,0:T(8,128)(2,1)}, u32[]{:S(2)}, u32[]{:S(2)}) collective-permute-start(bf16[144,2048]{1,0:T(8,128)(2,1)} %get-tuple-element.574.refs_0_), channel_id=1, source_target_pairs={{0,4},{4,0},{1,5},{5,1},{2,6},{6,2},{3,7},{7,3},{8,12},{12,8},{9,1... | collective-permute-start | bytes 1769480 | tf_op jit(solution)/shard_map/ppermute | solution.py:938
  148.7 44.3 %collective-permute-start.24 = (bf16[128,2048]{1,0:T(8,128)(2,1)S(1)}, bf16[128,2048]{1,0:T(8,128)(2,1)}, u32[]{:S(2)}, u32[]{:S(2)}) collective-permute-start(bf16[128,2048]{1,0:T(8,128)(2,1)S(1)} %collective-permute-done.18.refs_2_), channel_id=1, source_target_pairs={{0,1},{1,0},{2,3},{3,2},{4,5},{5,4},{6,7},{7,6},{8,9},{9,8},{10,11... | collective-permute-start | bytes 1572872 | tf_op jit(solution)/shard_map/ppermute | solution.py:938
  150.0 43.0 %collective-permute-start.25 = (bf16[128,2048]{1,0:T(8,128)(2,1)}, bf16[128,2048]{1,0:T(8,128)(2,1)}, u32[]{:S(2)}, u32[]{:S(2)}) collective-permute-start(bf16[128,2048]{1,0:T(8,128)(2,1)} %collective-permute-done.21.refs_6_), channel_id=1, source_target_pairs={{0,1},{1,0},{2,3},{3,2},{4,5},{5,4},{6,7},{7,6},{8,9},{9,8},{10,11... | collective-permute-start | bytes 1572872 | tf_op jit(solution)/shard_map/ppermute | solution.py:938
  238.2 29.1 %collective-permute-start.35 = (bf16[256,2048]{1,0:T(8,128)(2,1)}, bf16[256,2048]{1,0:T(8,128)(2,1)S(1)}, u32[]{:S(2)}, u32[]{:S(2)}) collective-permute-start(bf16[256,2048]{1,0:T(8,128)(2,1)} %get-tuple-element.871), channel_id=1, source_target_pairs={{0,16},{8,24},{16,0},{24,8},{1,17},{9,25},{17,1},{25,9},{2,18},{10... | collective-permute-start | bytes 3145736 | tf_op jit(solution)/shard_map/ppermute | solution.py:938
  239.7 27.6 %collective-permute-start.37 = (bf16[144,2048]{1,0:T(8,128)(2,1)S(1)}, bf16[144,2048]{1,0:T(8,128)(2,1)S(1)}, u32[]{:S(2)}, u32[]{:S(2)}) collective-permute-start(bf16[144,2048]{1,0:T(8,128)(2,1)S(1)} %copy-done.26), channel_id=1, source_target_pairs={{0,4},{4,0},{1,5},{5,1},{2,6},{6,2},{3,7},{7,3},{8,12},{12,8},{9,1... | collective-permute-start | bytes 1769480 | tf_op jit(solution)/shard_map/ppermute | solution.py:938
  239.7 27.6 %collective-permute-start.38 = (bf16[144,2048]{1,0:T(8,128)(2,1)S(1)}, bf16[144,2048]{1,0:T(8,128)(2,1)S(1)}, u32[]{:S(2)}, u32[]{:S(2)}) collective-permute-start(bf16[144,2048]{1,0:T(8,128)(2,1)S(1)} %copy-done.39), channel_id=1, source_target_pairs={{0,1},{1,0},{2,3},{3,2},{4,5},{5,4},{6,7},{7,6},{8,9},{9,8},{10,11... | collective-permute-start | bytes 1769480 | tf_op jit(solution)/shard_map/ppermute | solution.py:938
  267.7 33.6 %collective-permute-start.40 = (bf16[256,2048]{1,0:T(8,128)(2,1)S(1)}, bf16[256,2048]{1,0:T(8,128)(2,1)S(1)}, u32[]{:S(2)}, u32[]{:S(2)}) collective-permute-start(bf16[256,2048]{1,0:T(8,128)(2,1)S(1)} %add_convert_fusion.23), channel_id=1, source_target_pairs={{0,2},{2,0},{1,3},{3,1},{4,6},{6,4},{5,7},{7,5},{8,10},{10,8},{9,1... | collective-permute-start | bytes 3145736 | tf_op jit(solution)/shard_map/ppermute | solution.py:938
  267.8 33.5 %collective-permute-start.39 = (bf16[256,2048]{1,0:T(8,128)(2,1)S(1)}, bf16[256,2048]{1,0:T(8,128)(2,1)S(1)}, u32[]{:S(2)}, u32[]{:S(2)}) collective-permute-start(bf16[256,2048]{1,0:T(8,128)(2,1)S(1)} %copy-done.33), channel_id=1, source_target_pairs={{0,16},{8,24},{16,0},{24,8},{1,17},{9,25},{17,1},{25,9},{2,18},{10... | collective-permute-start | bytes 3145736 | tf_op jit(solution)/shard_map/ppermute | solution.py:938
  271.7 27.4 %collective-permute-start.41 = (bf16[144,2048]{1,0:T(8,128)(2,1)S(1)}, bf16[144,2048]{1,0:T(8,128)(2,1)S(1)}, u32[]{:S(2)}, u32[]{:S(2)}) collective-permute-start(bf16[144,2048]{1,0:T(8,128)(2,1)S(1)} %collective-permute-done.37.refs_11_), channel_id=1, source_target_pairs={{0,1},{1,0},{2,3},{3,2},{4,5},{5,4},{6,7},{7,6},{8,9},{9,8},{10,11... | collective-permute-start | bytes 1769480 | tf_op jit(solution)/shard_map/ppermute | solution.py:938
  301.3 27.1 %collective-permute-start.46 = (bf16[1024,2048]{1,0:T(8,128)(2,1)}, bf16[1024,2048]{1,0:T(8,128)(2,1)}, u32[]{:S(2)}, u32[]{:S(2)}) collective-permute-start(bf16[1024,2048]{1,0:T(8,128)(2,1)} %constant_dynamic-update-slice_fusion.8.first.right_first), channel_id=1, source_target_pairs={{0,8},{8,0},{16,24},{24,16},{1,9},{9,1},{17,25},{25,17},{2,10},{10... | collective-permute-start | bytes 12582920 | tf_op jit(solution)/shard_map/ppermute | solution.py:938
  503.7 29.0 %collective-permute-start.61 = (bf16[144,2048]{1,0:T(8,128)(2,1)S(1)}, bf16[144,2048]{1,0:T(8,128)(2,1)S(1)}, u32[]{:S(2)}, u32[]{:S(2)}) collective-permute-start(bf16[144,2048]{1,0:T(8,128)(2,1)S(1)} %slice.715), channel_id=1, source_target_pairs={{0,4},{4,0},{1,5},{5,1},{2,6},{6,2},{3,7},{7,3},{8,12},{12,8},{9,1... | collective-permute-start | bytes 1769480 | tf_op jit(solution)/shard_map/ppermute | solution.py:938
  505.3 27.4 %collective-permute-start.59 = (bf16[240,2048]{1,0:T(8,128)(2,1)S(1)}, bf16[240,2048]{1,0:T(8,128)(2,1)S(1)}, u32[]{:S(2)}, u32[]{:S(2)}) collective-permute-start(bf16[240,2048]{1,0:T(8,128)(2,1)S(1)} %get-tuple-element.626), channel_id=1, source_target_pairs={{0,1},{1,0},{2,3},{3,2},{4,5},{5,4},{6,7},{7,6},{8,9},{9,8},{10,11... | collective-permute-start | bytes 2949128 | tf_op jit(solution)/shard_map/ppermute | solution.py:938
  532.8 31.9 %collective-permute-start.63 = (bf16[256,2048]{1,0:T(8,128)(2,1)S(1)}, bf16[256,2048]{1,0:T(8,128)(2,1)S(1)}, u32[]{:S(2)}, u32[]{:S(2)}) collective-permute-start(bf16[256,2048]{1,0:T(8,128)(2,1)S(1)} %get-tuple-element.646), channel_id=1, source_target_pairs={{0,16},{8,24},{16,0},{24,8},{1,17},{9,25},{17,1},{25,9},{2,18},{10... | collective-permute-start | bytes 3145736 | tf_op jit(solution)/shard_map/ppermute | solution.py:938
  534.3 30.4 %collective-permute-start.65 = (bf16[240,2048]{1,0:T(8,128)(2,1)}, bf16[240,2048]{1,0:T(8,128)(2,1)S(1)}, u32[]{:S(2)}, u32[]{:S(2)}) collective-permute-start(bf16[240,2048]{1,0:T(8,128)(2,1)} %get-tuple-element.650), channel_id=1, source_target_pairs={{0,1},{1,0},{2,3},{3,2},{4,5},{5,4},{6,7},{7,6},{8,9},{9,8},{10,11... | collective-permute-start | bytes 2949128 | tf_op jit(solution)/shard_map/ppermute | solution.py:938
  536.7 28.0 %collective-permute-start.64 = (bf16[144,2048]{1,0:T(8,128)(2,1)}, bf16[144,2048]{1,0:T(8,128)(2,1)S(1)}, u32[]{:S(2)}, u32[]{:S(2)}) collective-permute-start(bf16[144,2048]{1,0:T(8,128)(2,1)} %slice.649), channel_id=1, source_target_pairs={{0,4},{4,0},{1,5},{5,1},{2,6},{6,2},{3,7},{7,3},{8,12},{12,8},{9,1... | collective-permute-start | bytes 1769480 | tf_op jit(solution)/shard_map/ppermute | solution.py:938
  566.1 59.7 %collective-permute-start.67 = (bf16[256,2048]{1,0:T(8,128)(2,1)}, bf16[256,2048]{1,0:T(8,128)(2,1)}, u32[]{:S(2)}, u32[]{:S(2)}) collective-permute-start(bf16[256,2048]{1,0:T(8,128)(2,1)} %add_convert_fusion.11), channel_id=1, source_target_pairs={{0,2},{2,0},{1,3},{3,1},{4,6},{6,4},{5,7},{7,5},{8,10},{10,8},{9,1... | collective-permute-start | bytes 3145736 | tf_op jit(solution)/shard_map/ppermute | solution.py:938
  568.5 57.3 %collective-permute-start.68 = (bf16[256,2048]{1,0:T(8,128)(2,1)}, bf16[256,2048]{1,0:T(8,128)(2,1)}, u32[]{:S(2)}, u32[]{:S(2)}) collective-permute-start(bf16[256,2048]{1,0:T(8,128)(2,1)} %slice.650), channel_id=1, source_target_pairs={{0,1},{1,0},{2,3},{3,2},{4,5},{5,4},{6,7},{7,6},{8,9},{9,8},{10,11... | collective-permute-start | bytes 3145736 | tf_op jit(solution)/shard_map/ppermute | solution.py:938
  569.0 56.8 %collective-permute-start.70 = (bf16[288,2048]{1,0:T(8,128)(2,1)}, bf16[288,2048]{1,0:T(8,128)(2,1)S(1)}, u32[]{:S(2)}, u32[]{:S(2)}) collective-permute-start(bf16[288,2048]{1,0:T(8,128)(2,1)} %get-tuple-element.670), channel_id=1, source_target_pairs={{0,1},{1,0},{2,3},{3,2},{4,5},{5,4},{6,7},{7,6},{8,9},{9,8},{10,11... | collective-permute-start | bytes 3538952 | tf_op jit(solution)/shard_map/ppermute | solution.py:938
  570.5 55.3 %collective-permute-start.66 = (bf16[256,2048]{1,0:T(8,128)(2,1)}, bf16[256,2048]{1,0:T(8,128)(2,1)}, u32[]{:S(2)}, u32[]{:S(2)}) collective-permute-start(bf16[256,2048]{1,0:T(8,128)(2,1)} %get-tuple-element.665), channel_id=1, source_target_pairs={{0,16},{8,24},{16,0},{24,8},{1,17},{9,25},{17,1},{25,9},{2,18},{10... | collective-permute-start | bytes 3145736 | tf_op jit(solution)/shard_map/ppermute | solution.py:938
  572.9 52.9 %collective-permute-start.69 = (bf16[240,2048]{1,0:T(8,128)(2,1)}, bf16[240,2048]{1,0:T(8,128)(2,1)S(1)}, u32[]{:S(2)}, u32[]{:S(2)}) collective-permute-start(bf16[240,2048]{1,0:T(8,128)(2,1)} %add_convert_fusion.28), channel_id=1, source_target_pairs={{0,4},{4,0},{1,5},{5,1},{2,6},{6,2},{3,7},{7,3},{8,12},{12,8},{9,1... | collective-permute-start | bytes 2949128 | tf_op jit(solution)/shard_map/ppermute | solution.py:938
  696.8 27.6 %collective-permute-start.82 = (bf16[128,2048]{1,0:T(8,128)(2,1)S(1)}, bf16[128,2048]{1,0:T(8,128)(2,1)S(1)}, u32[]{:S(2)}, u32[]{:S(2)}) collective-permute-start(bf16[128,2048]{1,0:T(8,128)(2,1)S(1)} %slice.721), channel_id=1, source_target_pairs={{0,4},{4,0},{1,5},{5,1},{2,6},{6,2},{3,7},{7,3},{8,12},{12,8},{9,1... | collective-permute-start | bytes 1572872 | tf_op jit(solution)/shard_map/ppermute | solution.py:938
  727.4 37.4 %collective-permute-start.86 = (bf16[256,2048]{1,0:T(8,128)(2,1)}, bf16[256,2048]{1,0:T(8,128)(2,1)}, u32[]{:S(2)}, u32[]{:S(2)}) collective-permute-start(bf16[256,2048]{1,0:T(8,128)(2,1)} %add_convert_fusion.3), channel_id=1, source_target_pairs={{0,2},{2,0},{1,3},{3,1},{4,6},{6,4},{5,7},{7,5},{8,10},{10,8},{9,1... | collective-permute-start | bytes 3145736 | tf_op jit(solution)/shard_map/ppermute | solution.py:938
  728.5 36.3 %collective-permute-start.85 = (bf16[256,2048]{1,0:T(8,128)(2,1)}, bf16[256,2048]{1,0:T(8,128)(2,1)}, u32[]{:S(2)}, u32[]{:S(2)}) collective-permute-start(bf16[256,2048]{1,0:T(8,128)(2,1)} %get-tuple-element.726), channel_id=1, source_target_pairs={{0,16},{8,24},{16,0},{24,8},{1,17},{9,25},{17,1},{25,9},{2,18},{10... | collective-permute-start | bytes 3145736 | tf_op jit(solution)/shard_map/ppermute | solution.py:938
  730.8 32.2 %collective-permute-start.87 = (bf16[144,2048]{1,0:T(8,128)(2,1)S(1)}, bf16[144,2048]{1,0:T(8,128)(2,1)S(1)}, u32[]{:S(2)}, u32[]{:S(2)}) collective-permute-start(bf16[144,2048]{1,0:T(8,128)(2,1)S(1)} %slice.681), channel_id=1, source_target_pairs={{0,4},{4,0},{1,5},{5,1},{2,6},{6,2},{3,7},{7,3},{8,12},{12,8},{9,1... | collective-permute-start | bytes 1769480 | tf_op jit(solution)/shard_map/ppermute | solution.py:938
  (135 other events, 2092.4 us)

commit v3 on v2

--- a/solution.py
+++ b/solution.py
@@ -981,6 +981,15 @@
     return folded
 
 
+def fold_first(part_own, came):
+    theirs = fold_came(part_own, came)[0]
+    sent = {at: piece for at, piece in theirs.items() if at}
+    part_own, came, sent = lax.optimization_barrier((part_own, came, sent))
+    theirs, mine = fold_came(part_own, came)
+    theirs.update(sent)
+    return theirs, mine
+
+
 def send_along(pieces):
     return {at: swap(piece, "seq", 2 * at) for at, piece in pieces.items() if at}
 
@@ -1218,10 +1227,11 @@
     fetch(value_got, cross_offsets)
     fetch(gate_got, far_offsets)
 
-    ends = [feed_part * part // 11 // 16 * 16 for part in (3, 4, 6, 9)] + [feed_part]
+    ends = [feed_part * part // 11 // 16 * 16 for part in (4, 5, 6, 9)] + [feed_part]
     starts_at = [0] + ends[:-1]
     units = [end - start for start, end in zip(starts_at, ends)]
     first_count = ends[2]
+    rest_count = feed_part - first_count
     shares = []
     for start, end in zip(starts_at, ends):
         span = slice(start, end)
@@ -1335,7 +1345,7 @@
         branch_other,
     )
     fetch_fine(1, cross_offsets)
-    fetch_near(0)
+    fetch_near(1)
     fetch_fine(2, far_offsets)
     grad_team_high = along_x(grad_team[grad_half_rows:])
     came_all = swap(branch_other, "seq", 1)
@@ -1354,12 +1364,12 @@
     came_all, grad_team_high, gate_own, mixed_own, branch_own = settle(
         came_all, grad_team_high, gate_own, mixed_own, branch_own
     )
-    theirs, mine = fold_came(branch_own, came_all)
+    theirs, mine = fold_first(branch_own, came_all)
     grad_team_x = [
         jnp.concatenate([low, high], axis=0) for low, high in zip(grad_team_low, grad_team_high)
     ]
     fetch_fine(2, cross_offsets)
-    fetch_near(1)
+    fetch_near(0)
     fetch_fine(3, far_offsets)
     came = send_along(theirs)
     normed = run_norm(*after(tuple(both_tokens), *theirs.values()), scale_all, gain_f[None])
@@ -1408,7 +1418,8 @@
             if which is None:
                 which = len(feed_given)
                 feed_given.append(piece)
-            target = starts_at[index] * count + at * size
+            set_start, set_count = (0, first_count) if index < 3 else (first_count, rest_count)
+            target = set_start * count + at * set_count + starts_at[index] - set_start
             for kind in range(3):
                 one = (which, start + kind * size, size)
                 if kind < 2:
@@ -1426,7 +1437,7 @@
     hidden_own, d_both_own, feed_own = run_feed(seq_feed[0], feed_rows, d_hiddens[0])
     hidden_other, d_both_other, feed_other = run_feed(seq_feed[1], feed_rows, d_hiddens[1])
     hiddens, d_boths = [hidden_own, hidden_other], [d_both_own, d_both_other]
-    theirs, mine = fold_rows(feed_own, feed_other)
+    theirs, mine = fold_first(feed_own, swap(feed_other, "seq", 1))
     kept = after((tuple(hiddens), tuple(d_boths)), *theirs.values())
     came = send_along(theirs)
     feed_low = run_outer(kept[1], seq_feed)
@@ -1436,20 +1447,22 @@
     came = send_along(mine)
     came_team = swap(theirs, "team", 1)
     down_low = run_outer(hiddens, seq_grads)
-    rest = slice(3, None)
-
-    def feed_pack(at, chosen):
-        rows_of = []
-        for values, base in ((feed_low, 0), (feed_low, feed_here), (down_low, 0)):
-            for size, start in list(zip(units, starts_at))[chosen]:
-                begin = base + start * count + at * size
-                rows_of.append(values[begin : begin + size])
-        return jnp.concatenate(rows_of, axis=0)
+
+    def feed_pack(at, start, size):
+        begin = start * count + at * size
+        return jnp.concatenate(
+            [
+                feed_low[begin : begin + size],
+                feed_low[feed_here + begin : feed_here + begin + size],
+                down_low[begin : begin + size],
+            ],
+            axis=0,
+        )
 
     far_all = [o for o in offsets if o[0]]
     near_all = [o for o in offsets if not o[0]]
     first_sent = {
-        o: feed_pack(at, slice(0, 3)) for at, o in enumerate(offsets) if all(o)
+        o: feed_pack(at, 0, first_count) for at, o in enumerate(offsets) if all(o)
     }
     mine, came, came_team, first_sent, feed_low, down_low = settle(
         mine, came, came_team, first_sent, feed_low, down_low
@@ -1464,10 +1477,10 @@
     branch_team = swap(d_branch, "team", 1)
     first_came = send_bits(first_sent, "low", list(first_sent))
     first_pieces = {
-        o: first_sent[o] if o in first_sent else feed_pack(at, slice(0, 3))
+        o: first_sent[o] if o in first_sent else feed_pack(at, 0, first_count)
         for at, o in enumerate(offsets)
     }
-    rest_pieces = {o: feed_pack(at, rest) for at, o in enumerate(offsets)}
+    rest_pieces = {o: feed_pack(at, first_count, rest_count) for at, o in enumerate(offsets)}
     groups[:] = [first_pieces, rest_pieces]
     branch_x, branch_team, first_came, hiddens = settle(
         branch_x, branch_team, first_came, hiddens
@@ -1710,7 +1723,6 @@
     gate_all = [gate_pieces[0, 0], *gate_near.values()]
     first_all = [first_pieces[0, 0], *first_near.values()]
     rest_all = [rest_pieces[0, 0], *rest_near.values(), *rest_far.values()]
-    rest_count = feed_part - first_count
     outputs = [
         ([segment(key_part, 0, mix_all + list(mix_far.values()))], False),
         ([segment(key_part, key_part, mix_all + list(mix_far.values()))], False),

time: 783 us -> 769 us (0.982)
  local copies, waits for them, and re-layouts: 75 us -> 51.6 us
  other arithmetic: 68.5 us -> 83.7 us
    unnamed x184 -> x148, local copies, waits for them, and re-layouts: 32.3 us -> 14.9 us
    convert_element_type x5 -> x7, other arithmetic: 17 us -> 19.5 us  [add_low(): return (left_side.astype(F32) + right_side.astype(F32)).astype(BF16)]
  transfers between devices with their start and end apart: 89 -> 89, of which waited for: 39 -> 42; matrix products, arithmetic and copies ran while one was open for 13% -> 12% of each run, Pallas kernels for 36% -> 37%
where the time goes in v3:
time: 769 us; the launch traced here: 764 us
  Pallas kernels  301 us (39%)
  waiting for transfers between devices  229 us (30%)
  starting transfers between devices  89.1 us (12%)
  other arithmetic  83.7 us (11%)
  local copies, waits for them, and re-layouts  51.6 us (7%)
    ppermute x89, waiting for transfers between devices, swap(): lax.ppermute(values, axis, [(place, place ^ bit) for place in range(count)])  229 us
    ppermute x89, starting transfers between devices, swap(): lax.ppermute(values, axis, [(place, place ^ bit) for place in range(count)])  89.1 us
    pallas_call x1, Pallas kernels, run_backward(): pl.pallas_call(functools.partial(backward_body, heads), grid_spec=grid_sp...  50 us
    pallas_call x2, Pallas kernels, run_feed(): pl.pallas_call(feed_body, grid=(length // tile,), in_specs=[pl.BlockSpec(...  38.7 us
    pallas_call x1, Pallas kernels, run_forward(): pl.pallas_call(functools.partial(forward_body, heads), grid_spec=grid_spe...  38.4 us
    pallas_call x2, Pallas kernels, run_outer(): pl.pallas_call(outer_body, grid=(wide // tile,), in_specs=[left, left, ri...  29.5 us
    pallas_call x2, Pallas kernels, run_back(): pl.pallas_call(back_body, grid=(length // tile,), in_specs=[pl.BlockSpec(...  26.2 us
    pallas_call x1, Pallas kernels, run_mixer_back(): pl.pallas_call(functools.partial(mixer_back_body, wide // DV, part), grid...  23 us
  transfers between devices with their start and end apart: 89, of which 42 were waited for; matrix products, arithmetic and copies ran while one was open for 12% of the time, Pallas kernels for 37%

profile of v3, /device:TPU:0, one launch (start us, length us, event | category | flops | bytes accessed | tf_op | source)
XLA Modules:
  0.0 764.4 jit_solution(6409781959385515692)
XLA Ops:
  27.8 8.5 %collective-permute-done.5 = bf16[256,2048]{1,0:T(8,128)(2,1)} collective-permute-done((bf16[256,2048]{1,0:T(8,128)(2,1)}, bf16[256,2048]{1,0:T(8,128)(2,1)}, u32[]{:S(2)}, u32[]{:S(2)}) %collective-permute-start.5) | collective-permute-done | bytes 1048608 | tf_op jit(solution)/shard_map/ppermute | solution.py:938
  42.8 12.6 %collective-permute-done.10.refs_2_ = bf16[128,2048]{1,0:T(8,128)(2,1)S(1)} collective-permute-done((bf16[128,2048]{1,0:T(8,128)(2,1)S(1)}, bf16[128,2048]{1,0:T(8,128)(2,1)S(1)}, u32[]{:S(2)}, u32[]{:S(2)}) %collective-permute-start.10) | collective-permute-done | bytes 524320 | tf_op jit(solution)/shard_map/ppermute | solution.py:938
  71.2 11.3 %collective-permute-done.12 = bf16[256,2048]{1,0:T(8,128)(2,1)} collective-permute-done((bf16[256,2048]{1,0:T(8,128)(2,1)}, bf16[256,2048]{1,0:T(8,128)(2,1)}, u32[]{:S(2)}, u32[]{:S(2)}) %collective-permute-start.12) | collective-permute-done | bytes 1048608 | tf_op jit(solution)/shard_map/ppermute | solution.py:938
  93.4 19.0 %collective-permute-done.18.refs_2_ = bf16[128,2048]{1,0:T(8,128)(2,1)S(1)} collective-permute-done((bf16[128,2048]{1,0:T(8,128)(2,1)S(1)}, bf16[128,2048]{1,0:T(8,128)(2,1)S(1)}, u32[]{:S(2)}, u32[]{:S(2)}) %collective-permute-start.18) | collective-permute-done | bytes 524320 | tf_op jit(solution)/shard_map/ppermute | solution.py:938
  117.1 18.7 %project_rows.1 = (bf16[1152,2048]{1,0:T(8,128)(2,1)}, bf16[2048,1024]{1,0:T(8,128)(2,1)}, f32[2048,128]{1,0:T(8,128)}) custom-call(bf16[1024,2048]{1,0:T(8,128)(2,1)} %pad_maximum_fusion.1.half.tokens, bf16[1024,2048]{1,0:T(8,128)(2,1)} %collective-permute-done.16.other.tokens, f32[1,2048]{1,0:T(1,128)S(1)} %bitcast.130, f32[2048,1]{1,0:T(8,128)} %copy.123.scale, ...), custom_call_target="tpu_custom_call" | custom-call | tf_op jit(solution)/shard_map/project_rows/pallas_call | solution.py:482
  145.7 38.4 %delta_forward.1 = (bf16[2,2,2,256,512]{4,3,2,1,0:T(8,128)(2,1)}, bf16[2,2,2,256,512]{4,3,2,1,0:T(8,128)(2,1)}, bf16[8,4,128,256]{3,2,1,0:T(8,128)(2,1)}, bf16[8,4,128,128]{3,2,1,0:T(8,128)(2,1)S(1)}) custom-call(s32[1]{0:T(128)} %bitcast.32.place, bf16[2,2,2,256,1024]{4,3,2,1,0:T(8,128)(2,1)} %bitcast.138, f32[2,2,2,256,128]{4,3,2,1,0:T(8,128)} %bitcast.124, ...), custom_call_target="tpu_custom_call" | custom-call | tf_op jit(solution)/shard_map/delta_forward/pallas_call | solution.py:344
  191.2 11.0 %branch_rows.2 = (bf16[512,2048]{1,0:T(8,128)(2,1)}, bf16[512,2048]{1,0:T(8,128)(2,1)}, bf16[1024,512]{1,0:T(8,128)(2,1)}, bf16[1024,512]{1,0:T(8,128)(2,1)}, bf16[1024,2048]{1,0:T(8,128)(2,1)}) custom-call(bf16[1024,2048]{1,0:T(8,128)(2,1)} %collective-permute-done.16.other.tokens, f32[1,2048]{1,0:T(1,128)S(1)} %bitcast.131, f32[2048,1]{1,0:T(8,128)} %copy.123.scale, ...), custom_call_target="tpu_custom_call" | custom-call | tf_op jit(solution)/shard_map/branch_rows/pallas_call | solution.py:840
  209.1 11.6 %branch_rows.3 = (bf16[512,2048]{1,0:T(8,128)(2,1)}, bf16[512,2048]{1,0:T(8,128)(2,1)}, bf16[1024,512]{1,0:T(8,128)(2,1)S(1)}, bf16[1024,512]{1,0:T(8,128)(2,1)}, bf16[1024,2048]{1,0:T(8,128)(2,1)}) custom-call(bf16[1024,2048]{1,0:T(8,128)(2,1)} %pad_maximum_fusion.1.half.tokens, f32[1,2048]{1,0:T(1,128)S(1)} %broadcast_in_dim_broadcast_in_dim.3.gain, ...), custom_call_target="tpu_custom_call" | custom-call | tf_op jit(solution)/shard_map/branch_rows/pallas_call | solution.py:840
  231.8 9.7 %norm_rows.1.normed = bf16[2048,2048]{1,0:T(8,128)(2,1)} custom-call(bf16[1024,2048]{1,0:T(8,128)(2,1)} %pad_maximum_fusion.1.half.tokens, bf16[1024,2048]{1,0:T(8,128)(2,1)} %collective-permute-done.16.other.tokens, f32[2048,1]{1,0:T(8,128)S(1)} %copy-done, f32[1,2048]{1,0:T(1,128)S(1)} %bitcast.132), custom_call_target="tpu_custom_call" | custom-call | tf_op jit(solution)/shard_map/norm_rows/pallas_call | solution.py:428
  241.5 5.9 collective-permute-done.36.refs_15_
  266.4 19.4 %collective-permute-done.42.refs_12_ = bf16[96,2048]{1,0:T(8,128)(2,1)} collective-permute-done((bf16[96,2048]{1,0:T(8,128)(2,1)S(1)}, bf16[96,2048]{1,0:T(8,128)(2,1)}, u32[]{:S(2)}, u32[]{:S(2)}) %collective-permute-start.42) | collective-permute-done | bytes 393248 | tf_op jit(solution)/shard_map/ppermute | solution.py:938
  294.9 7.1 pad_maximum_fusion.weights
  305.1 7.0 collective-permute-done.48.refs_7_
  317.8 16.7 %hidden_cotangents.1 = (bf16[1408,2048]{1,0:T(8,128)(2,1)}, bf16[704,2048]{1,0:T(8,128)(2,1)}, bf16[704,1024]{1,0:T(8,128)(2,1)}, bf16[704,1024]{1,0:T(8,128)(2,1)}) custom-call(bf16[1024,2048]{1,0:T(8,128)(2,1)} %constant_dynamic-update-slice_fusion.8.first.right_first, bf16[1024,2048]{1,0:T(8,128)(2,1)} %collective-permute-done.46.second.right_second, ...), custom_call_target="tpu_custom_call" | custom-call | tf_op jit(solution)/shard_map/hidden_cotangents/pallas_call | solution.py:523
  334.4 7.2 collective-permute-done.49
  341.6 6.7 pad_maximum_fusion.2.feed.right_first
  348.4 7.3 collective-permute-done.50.feed.right_second
  355.7 19.4 %feed_forward.3 = (bf16[704,1024]{1,0:T(8,128)(2,1)S(1)}, bf16[1408,1024]{1,0:T(8,128)(2,1)}, bf16[1024,2048]{1,0:T(8,128)(2,1)}) custom-call(bf16[1024,2048]{1,0:T(8,128)(2,1)} %collective-permute-done.50.feed.right_second, bf16[1408,2048]{1,0:T(8,128)(2,1)} %get-tuple-element.606.weights, bf16[704,1024]{1,0:T(8,128)(2,1)} %get-tuple-element.609.back), custom_call_target="tpu_custom_call" | custom-call | tf_op jit(solution)/shard_map/feed_forward/pallas_call | solution.py:570
  376.3 19.4 %feed_forward.2 = (bf16[704,1024]{1,0:T(8,128)(2,1)S(1)}, bf16[1408,1024]{1,0:T(8,128)(2,1)}, bf16[1024,2048]{1,0:T(8,128)(2,1)}) custom-call(bf16[1024,2048]{1,0:T(8,128)(2,1)} %copy-done.7, bf16[1408,2048]{1,0:T(8,128)(2,1)} %get-tuple-element.606.weights, bf16[704,1024]{1,0:T(8,128)(2,1)} %get-tuple-element.607.back), custom_call_target="tpu_custom_call" | custom-call | tf_op jit(solution)/shard_map/feed_forward/pallas_call | solution.py:570
  402.3 18.1 %outer_sums.2 = bf16[1408,2048]{1,0:T(8,128)(2,1)} custom-call(bf16[1408,1024]{1,0:T(8,128)(2,1)} %get-tuple-element.618.first, bf16[1408,1024]{1,0:T(8,128)(2,1)} %get-tuple-element.619.second, bf16[1024,2048]{1,0:T(8,128)(2,1)} %copy-done.7, bf16[1024,2048]{1,0:T(8,128)(2,1)} %collective-permute-done.50.feed.right_second), custom_call_target="tpu_custom_call" | custom-call | tf_op jit(solution)/shard_map/outer_sums/pallas_call | solution.py:605
  425.4 11.4 %outer_sums.3 = bf16[704,2048]{1,0:T(8,128)(2,1)} custom-call(bf16[704,1024]{1,0:T(8,128)(2,1)S(1)} %get-tuple-element.639.first, bf16[704,1024]{1,0:T(8,128)(2,1)} %copy-done.2, bf16[1024,2048]{1,0:T(8,128)(2,1)} %constant_dynamic-update-slice_fusion.8.first.right_first, bf16[1024,2048]{1,0:T(8,128)(2,1)} %collective-permute-done.46.second.right_second), custom_call_target="tpu_custom_call" | custom-call | tf_op jit(solution)/shard_map/outer_sums/pallas_call | solution.py:605
  437.8 11.1 %collective-permute-done.54 = bf16[256,2048]{1,0:T(8,128)(2,1)S(1)} collective-permute-done((bf16[256,2048]{1,0:T(8,128)(2,1)}, bf16[256,2048]{1,0:T(8,128)(2,1)S(1)}, u32[]{:S(2)}, u32[]{:S(2)}) %collective-permute-start.54) | collective-permute-done | bytes 1048608 | tf_op jit(solution)/shard_map/ppermute | solution.py:938
  467.4 15.1 %collective-permute-done.55 = bf16[256,2048]{1,0:T(8,128)(2,1)S(1)} collective-permute-done((bf16[256,2048]{1,0:T(8,128)(2,1)S(1)}, bf16[256,2048]{1,0:T(8,128)(2,1)S(1)}, u32[]{:S(2)}, u32[]{:S(2)}) %collective-permute-start.55) | collective-permute-done | bytes 1048608 | tf_op jit(solution)/shard_map/ppermute | solution.py:938
  499.1 17.2 %collective-permute-done.58 = bf16[256,2048]{1,0:T(8,128)(2,1)S(1)} collective-permute-done((bf16[256,2048]{1,0:T(8,128)(2,1)S(1)}, bf16[256,2048]{1,0:T(8,128)(2,1)S(1)}, u32[]{:S(2)}, u32[]{:S(2)}) %collective-permute-start.58) | collective-permute-done | bytes 1048608 | tf_op jit(solution)/shard_map/ppermute | solution.py:938
  528.9 23.0 %mixer_backward.1 = (bf16[2048,512]{1,0:T(8,128)(2,1)}, bf16[2048,512]{1,0:T(8,128)(2,1)}, f32[8,256]{1,0:T(8,128)S(1)}, bf16[1024,2048]{1,0:T(8,128)(2,1)}) custom-call(bf16[1024,2048]{1,0:T(8,128)(2,1)} %copy-done.8, bf16[1024,2048]{1,0:T(8,128)(2,1)} %collective-permute-done.62.branch_other, bf16[512,2048]{1,0:T(8,128)(2,1)} %get-tuple-element.498.refs_1_.out_rows, ...), custom_call_target="tpu_custom_call" | custom-call | tf_op jit(solution)/shard_map/mixer_backward/pallas_call | solution.py:786
  564.7 50.0 %delta_backward.1 = (bf16[2,2,2,256,1664]{4,3,2,1,0:T(8,128)(2,1)}, f32[8,1024]{1,0:T(8,128)S(1)}) custom-call(s32[1]{0:T(128)} %bitcast.32.place, bf16[2,2,2,256,1024]{4,3,2,1,0:T(8,128)(2,1)} %bitcast.139, bf16[2,2,2,256,1024]{4,3,2,1,0:T(8,128)(2,1)} %bitcast.140, bf16[2,2,2,256,512]{4,3,2,1,0:T(8,128)(2,1)} %bitcast.151, ...), custom_call_target="tpu_custom_call" | custom-call | tf_op jit(solution)/shard_map/delta_backward/pallas_call | solution.py:400
  619.4 18.2 %weight_sums.1 = bf16[1216,2048]{1,0:T(8,128)(2,1)} custom-call(bf16[2048,1664]{1,0:T(8,128)(2,1)} %bitcast.135, bf16[2048,2048]{1,0:T(8,128)(2,1)} %norm_rows.1.normed, bf16[64,2048]{1,0:T(8,128)(2,1)S(1)} %bitcast.129), custom_call_target="tpu_custom_call" | custom-call | tf_op jit(solution)/shard_map/weight_sums/pallas_call | solution.py:694
  646.0 13.1 %back_rows.2 = (bf16[1024,2048]{1,0:T(8,128)(2,1)}, f32[8,2048]{1,0:T(8,128)S(1)}) custom-call(bf16[2048,1664]{1,0:T(8,128)(2,1)} %bitcast.136, bf16[1664,2048]{1,0:T(8,128)(2,1)} %pad_maximum_fusion.weights, bf16[2048,2048]{1,0:T(8,128)(2,1)} %norm_rows.1.normed), custom_call_target="tpu_custom_call" | custom-call | tf_op jit(solution)/shard_map/back_rows/pallas_call | solution.py:631
  664.2 13.1 %back_rows.3 = (bf16[1024,2048]{1,0:T(8,128)(2,1)}, f32[8,2048]{1,0:T(8,128)S(1)}) custom-call(bf16[2048,1664]{1,0:T(8,128)(2,1)} %bitcast.137, bf16[1664,2048]{1,0:T(8,128)(2,1)} %pad_maximum_fusion.weights, bf16[2048,2048]{1,0:T(8,128)(2,1)} %norm_rows.1.normed), custom_call_target="tpu_custom_call" | custom-call | tf_op jit(solution)/shard_map/back_rows/pallas_call | solution.py:631
  694.4 18.4 %collective-permute-done.81 = f32[2,1,1,1,24,128]{5,4,3,2,1,0:T(8,128)S(1)} collective-permute-done((f32[2,1,1,1,24,128]{5,4,3,2,1,0:T(8,128)S(1)}, f32[2,1,1,1,24,128]{5,4,3,2,1,0:T(8,128)S(1)}, u32[]{:S(2)}, u32[]{:S(2)}) %collective-permute-start.81) | collective-permute-done | bytes 24608 | tf_op jit(solution)/shard_map/ppermute | solution.py:938
  726.2 9.1 %finish_sums.1 = (f32[64,2048]{1,0:T(8,128)}, f32[64,2048]{1,0:T(8,128)}, f32[2048,128]{1,0:T(8,128)}, f32[128,2048]{1,0:T(8,128)}, f32[176,2048]{1,0:T(8,128)},...) custom-call(bf16[272,2048]{1,0:T(8,128)(2,1)} %get-tuple-element.770.refs_0_, bf16[272,2048]{1,0:T(8,128)(2,1)} %copy-done.20, ...), custom_call_target="tpu_custom_call" | custom-call | tf_op jit(solution)/shard_map/finish_sums/pallas_call | solution.py:903
  735.4 16.0 %collective-permute-done.87 = bf16[144,2048]{1,0:T(8,128)(2,1)S(1)} collective-permute-done((bf16[144,2048]{1,0:T(8,128)(2,1)S(1)}, bf16[144,2048]{1,0:T(8,128)(2,1)S(1)}, u32[]{:S(2)}, u32[]{:S(2)}) %collective-permute-start.87) | collective-permute-done | bytes 589856 | tf_op jit(solution)/shard_map/ppermute | solution.py:938
  (504 shorter events, 271.2 us)
Async XLA Ops:
  23.4 34.2 %collective-permute-start.9 = (bf16[256,2048]{1,0:T(8,128)(2,1)}, bf16[256,2048]{1,0:T(8,128)(2,1)}, u32[]{:S(2)}, u32[]{:S(2)}) collective-permute-start(bf16[256,2048]{1,0:T(8,128)(2,1)} %bitcast), channel_id=1, source_target_pairs={{0,2},{2,0},{1,3},{3,1},{4,6},{6,4},{5,7},{7,5},{8,10},{10,8},{9,1... | collective-permute-start | bytes 3145736 | tf_op jit(solution)/shard_map/ppermute | solution.py:938
  25.9 29.5 %collective-permute-start.10 = (bf16[128,2048]{1,0:T(8,128)(2,1)S(1)}, bf16[128,2048]{1,0:T(8,128)(2,1)S(1)}, u32[]{:S(2)}, u32[]{:S(2)}) collective-permute-start(bf16[128,2048]{1,0:T(8,128)(2,1)S(1)} %pad_maximum_fusion.16.refs_0_), channel_id=1, source_target_pairs={{0,4},{4,0},{1,5},{5,1},{2,6},{6,2},{3,7},{7,3},{8,12},{12,8},{9,1... | collective-permute-start | bytes 1572872 | tf_op jit(solution)/shard_map/ppermute | solution.py:938
  26.3 29.1 %collective-permute-start.11 = (bf16[128,2048]{1,0:T(8,128)(2,1)S(1)}, bf16[128,2048]{1,0:T(8,128)(2,1)S(1)}, u32[]{:S(2)}, u32[]{:S(2)}) collective-permute-start(bf16[128,2048]{1,0:T(8,128)(2,1)S(1)} %pad_maximum_fusion.16.refs_0_), channel_id=1, source_target_pairs={{0,1},{1,0},{2,3},{3,2},{4,5},{5,4},{6,7},{7,6},{8,9},{9,8},{10,11... | collective-permute-start | bytes 1572872 | tf_op jit(solution)/shard_map/ppermute | solution.py:938
  57.8 28.5 %collective-permute-start.14 = (bf16[144,2048]{1,0:T(8,128)(2,1)S(1)}, bf16[144,2048]{1,0:T(8,128)(2,1)}, u32[]{:S(2)}, u32[]{:S(2)}) collective-permute-start(bf16[144,2048]{1,0:T(8,128)(2,1)S(1)} %pad_maximum_fusion.14.refs_4_), channel_id=1, source_target_pairs={{0,4},{4,0},{1,5},{5,1},{2,6},{6,2},{3,7},{7,3},{8,12},{12,8},{9,1... | collective-permute-start | bytes 1769480 | tf_op jit(solution)/shard_map/ppermute | solution.py:938
  59.2 27.1 %collective-permute-start.15 = (bf16[144,2048]{1,0:T(8,128)(2,1)S(1)}, bf16[144,2048]{1,0:T(8,128)(2,1)}, u32[]{:S(2)}, u32[]{:S(2)}) collective-permute-start(bf16[144,2048]{1,0:T(8,128)(2,1)S(1)} %pad_maximum_fusion.14.refs_4_), channel_id=1, source_target_pairs={{0,1},{1,0},{2,3},{3,2},{4,5},{5,4},{6,7},{7,6},{8,9},{9,8},{10,11... | collective-permute-start | bytes 1769480 | tf_op jit(solution)/shard_map/ppermute | solution.py:938
  139.1 46.0 %collective-permute-start.22 = (bf16[256,2048]{1,0:T(8,128)(2,1)}, bf16[256,2048]{1,0:T(8,128)(2,1)}, u32[]{:S(2)}, u32[]{:S(2)}) collective-permute-start(bf16[256,2048]{1,0:T(8,128)(2,1)} %bitcast.148), channel_id=1, source_target_pairs={{0,16},{8,24},{16,0},{24,8},{1,17},{9,25},{17,1},{25,9},{2,18},{10... | collective-permute-start | bytes 3145736 | tf_op jit(solution)/shard_map/ppermute | solution.py:938
  139.6 45.5 %collective-permute-start.23 = (bf16[256,2048]{1,0:T(8,128)(2,1)}, bf16[256,2048]{1,0:T(8,128)(2,1)}, u32[]{:S(2)}, u32[]{:S(2)}) collective-permute-start(bf16[256,2048]{1,0:T(8,128)(2,1)} %bitcast.149), channel_id=1, source_target_pairs={{0,2},{2,0},{1,3},{3,1},{4,6},{6,4},{5,7},{7,5},{8,10},{10,8},{9,1... | collective-permute-start | bytes 3145736 | tf_op jit(solution)/shard_map/ppermute | solution.py:938
  141.2 43.9 %collective-permute-start.26 = (bf16[192,2048]{1,0:T(8,128)(2,1)}, bf16[192,2048]{1,0:T(8,128)(2,1)}, u32[]{:S(2)}, u32[]{:S(2)}) collective-permute-start(bf16[192,2048]{1,0:T(8,128)(2,1)} %pad_maximum_fusion.13.refs_0_), channel_id=1, source_target_pairs={{0,4},{4,0},{1,5},{5,1},{2,6},{6,2},{3,7},{7,3},{8,12},{12,8},{9,1... | collective-permute-start | bytes 2359304 | tf_op jit(solution)/shard_map/ppermute | solution.py:938
  142.3 42.8 %collective-permute-start.24 = (bf16[128,2048]{1,0:T(8,128)(2,1)S(1)}, bf16[128,2048]{1,0:T(8,128)(2,1)}, u32[]{:S(2)}, u32[]{:S(2)}) collective-permute-start(bf16[128,2048]{1,0:T(8,128)(2,1)S(1)} %collective-permute-done.18.refs_2_), channel_id=1, source_target_pairs={{0,1},{1,0},{2,3},{3,2},{4,5},{5,4},{6,7},{7,6},{8,9},{9,8},{10,11... | collective-permute-start | bytes 1572872 | tf_op jit(solution)/shard_map/ppermute | solution.py:938
  143.1 42.0 %collective-permute-start.25 = (bf16[128,2048]{1,0:T(8,128)(2,1)}, bf16[128,2048]{1,0:T(8,128)(2,1)}, u32[]{:S(2)}, u32[]{:S(2)}) collective-permute-start(bf16[128,2048]{1,0:T(8,128)(2,1)} %collective-permute-done.21.refs_6_), channel_id=1, source_target_pairs={{0,1},{1,0},{2,3},{3,2},{4,5},{5,4},{6,7},{7,6},{8,9},{9,8},{10,11... | collective-permute-start | bytes 1572872 | tf_op jit(solution)/shard_map/ppermute | solution.py:938
  224.5 28.6 %collective-permute-start.35 = (bf16[256,2048]{1,0:T(8,128)(2,1)}, bf16[256,2048]{1,0:T(8,128)(2,1)}, u32[]{:S(2)}, u32[]{:S(2)}) collective-permute-start(bf16[256,2048]{1,0:T(8,128)(2,1)} %add_convert_fusion.27), channel_id=1, source_target_pairs={{0,16},{8,24},{16,0},{24,8},{1,17},{9,25},{17,1},{25,9},{2,18},{10... | collective-permute-start | bytes 3145736 | tf_op jit(solution)/shard_map/ppermute | solution.py:938
  225.0 28.2 %collective-permute-start.38 = (bf16[192,2048]{1,0:T(8,128)(2,1)S(1)}, bf16[192,2048]{1,0:T(8,128)(2,1)}, u32[]{:S(2)}, u32[]{:S(2)}) collective-permute-start(bf16[192,2048]{1,0:T(8,128)(2,1)S(1)} %copy-done.19), channel_id=1, source_target_pairs={{0,1},{1,0},{2,3},{3,2},{4,5},{5,4},{6,7},{7,6},{8,9},{9,8},{10,11... | collective-permute-start | bytes 2359304 | tf_op jit(solution)/shard_map/ppermute | solution.py:938
  225.7 27.4 %collective-permute-start.37 = (bf16[144,2048]{1,0:T(8,128)(2,1)S(1)}, bf16[144,2048]{1,0:T(8,128)(2,1)}, u32[]{:S(2)}, u32[]{:S(2)}) collective-permute-start(bf16[144,2048]{1,0:T(8,128)(2,1)S(1)} %copy-done.23), channel_id=1, source_target_pairs={{0,4},{4,0},{1,5},{5,1},{2,6},{6,2},{3,7},{7,3},{8,12},{12,8},{9,1... | collective-permute-start | bytes 1769480 | tf_op jit(solution)/shard_map/ppermute | solution.py:938
  254.8 33.2 %collective-permute-start.40 = (bf16[256,2048]{1,0:T(8,128)(2,1)S(1)}, bf16[256,2048]{1,0:T(8,128)(2,1)S(1)}, u32[]{:S(2)}, u32[]{:S(2)}) collective-permute-start(bf16[256,2048]{1,0:T(8,128)(2,1)S(1)} %add_convert_fusion.23), channel_id=1, source_target_pairs={{0,2},{2,0},{1,3},{3,1},{4,6},{6,4},{5,7},{7,5},{8,10},{10,8},{9,1... | collective-permute-start | bytes 3145736 | tf_op jit(solution)/shard_map/ppermute | solution.py:938
  254.9 33.1 %collective-permute-start.39 = (bf16[256,2048]{1,0:T(8,128)(2,1)S(1)}, bf16[256,2048]{1,0:T(8,128)(2,1)S(1)}, u32[]{:S(2)}, u32[]{:S(2)}) collective-permute-start(bf16[256,2048]{1,0:T(8,128)(2,1)S(1)} %copy-done.28), channel_id=1, source_target_pairs={{0,16},{8,24},{16,0},{24,8},{1,17},{9,25},{17,1},{25,9},{2,18},{10... | collective-permute-start | bytes 3145736 | tf_op jit(solution)/shard_map/ppermute | solution.py:938
  288.0 28.9 %collective-permute-start.46 = (bf16[1024,2048]{1,0:T(8,128)(2,1)}, bf16[1024,2048]{1,0:T(8,128)(2,1)}, u32[]{:S(2)}, u32[]{:S(2)}) collective-permute-start(bf16[1024,2048]{1,0:T(8,128)(2,1)} %constant_dynamic-update-slice_fusion.8.first.right_first), channel_id=1, source_target_pairs={{0,8},{8,0},{16,24},{24,16},{1,9},{9,1},{17,25},{25,17},{2,10},{10... | collective-permute-start | bytes 12582920 | tf_op jit(solution)/shard_map/ppermute | solution.py:938
  490.7 26.3 %collective-permute-start.60 = (bf16[1024,2048]{1,0:T(8,128)(2,1)S(1)}, bf16[1024,2048]{1,0:T(8,128)(2,1)S(1)}, u32[]{:S(2)}, u32[]{:S(2)}) collective-permute-start(bf16[1024,2048]{1,0:T(8,128)(2,1)S(1)} %convolution_convert_fusion), channel_id=1, source_target_pairs={{0,8},{8,0},{16,24},{24,16},{1,9},{9,1},{17,25},{25,17},{2,10},{10... | collective-permute-start | bytes 12582920 | tf_op jit(solution)/shard_map/ppermute | solution.py:938
  492.5 29.0 %collective-permute-start.61 = (bf16[144,2048]{1,0:T(8,128)(2,1)S(1)}, bf16[144,2048]{1,0:T(8,128)(2,1)S(1)}, u32[]{:S(2)}, u32[]{:S(2)}) collective-permute-start(bf16[144,2048]{1,0:T(8,128)(2,1)S(1)} %slice.566), channel_id=1, source_target_pairs={{0,4},{4,0},{1,5},{5,1},{2,6},{6,2},{3,7},{7,3},{8,12},{12,8},{9,1... | collective-permute-start | bytes 1769480 | tf_op jit(solution)/shard_map/ppermute | solution.py:938
  493.7 27.9 %collective-permute-start.59 = (bf16[240,2048]{1,0:T(8,128)(2,1)S(1)}, bf16[240,2048]{1,0:T(8,128)(2,1)S(1)}, u32[]{:S(2)}, u32[]{:S(2)}) collective-permute-start(bf16[240,2048]{1,0:T(8,128)(2,1)S(1)} %pad_maximum_fusion.12), channel_id=1, source_target_pairs={{0,1},{1,0},{2,3},{3,2},{4,5},{5,4},{6,7},{7,6},{8,9},{9,8},{10,11... | collective-permute-start | bytes 2949128 | tf_op jit(solution)/shard_map/ppermute | solution.py:938
  521.6 31.0 %collective-permute-start.63 = (bf16[256,2048]{1,0:T(8,128)(2,1)S(1)}, bf16[256,2048]{1,0:T(8,128)(2,1)S(1)}, u32[]{:S(2)}, u32[]{:S(2)}) collective-permute-start(bf16[256,2048]{1,0:T(8,128)(2,1)S(1)} %get-tuple-element.658), channel_id=1, source_target_pairs={{0,16},{8,24},{16,0},{24,8},{1,17},{9,25},{17,1},{25,9},{2,18},{10... | collective-permute-start | bytes 3145736 | tf_op jit(solution)/shard_map/ppermute | solution.py:938
  522.5 30.1 %collective-permute-start.65 = (bf16[240,2048]{1,0:T(8,128)(2,1)}, bf16[240,2048]{1,0:T(8,128)(2,1)S(1)}, u32[]{:S(2)}, u32[]{:S(2)}) collective-permute-start(bf16[240,2048]{1,0:T(8,128)(2,1)} %pad_maximum_fusion.10), channel_id=1, source_target_pairs={{0,1},{1,0},{2,3},{3,2},{4,5},{5,4},{6,7},{7,6},{8,9},{9,8},{10,11... | collective-permute-start | bytes 2949128 | tf_op jit(solution)/shard_map/ppermute | solution.py:938
  525.0 27.7 %collective-permute-start.64 = (bf16[144,2048]{1,0:T(8,128)(2,1)}, bf16[144,2048]{1,0:T(8,128)(2,1)S(1)}, u32[]{:S(2)}, u32[]{:S(2)}) collective-permute-start(bf16[144,2048]{1,0:T(8,128)(2,1)} %slice.505), channel_id=1, source_target_pairs={{0,4},{4,0},{1,5},{5,1},{2,6},{6,2},{3,7},{7,3},{8,12},{12,8},{9,1... | collective-permute-start | bytes 1769480 | tf_op jit(solution)/shard_map/ppermute | solution.py:938
  554.0 60.8 %collective-permute-start.67 = (bf16[256,2048]{1,0:T(8,128)(2,1)}, bf16[256,2048]{1,0:T(8,128)(2,1)}, u32[]{:S(2)}, u32[]{:S(2)}) collective-permute-start(bf16[256,2048]{1,0:T(8,128)(2,1)} %add_convert_fusion.11), channel_id=1, source_target_pairs={{0,2},{2,0},{1,3},{3,1},{4,6},{6,4},{5,7},{7,5},{8,10},{10,8},{9,1... | collective-permute-start | bytes 3145736 | tf_op jit(solution)/shard_map/ppermute | solution.py:938
  556.4 58.4 %collective-permute-start.68 = (bf16[256,2048]{1,0:T(8,128)(2,1)}, bf16[256,2048]{1,0:T(8,128)(2,1)}, u32[]{:S(2)}, u32[]{:S(2)}) collective-permute-start(bf16[256,2048]{1,0:T(8,128)(2,1)} %slice.506), channel_id=1, source_target_pairs={{0,1},{1,0},{2,3},{3,2},{4,5},{5,4},{6,7},{7,6},{8,9},{9,8},{10,11... | collective-permute-start | bytes 3145736 | tf_op jit(solution)/shard_map/ppermute | solution.py:938
  557.5 57.4 %collective-permute-start.70 = (bf16[288,2048]{1,0:T(8,128)(2,1)}, bf16[288,2048]{1,0:T(8,128)(2,1)S(1)}, u32[]{:S(2)}, u32[]{:S(2)}) collective-permute-start(bf16[288,2048]{1,0:T(8,128)(2,1)} %pad_maximum_fusion.6), channel_id=1, source_target_pairs={{0,1},{1,0},{2,3},{3,2},{4,5},{5,4},{6,7},{7,6},{8,9},{9,8},{10,11... | collective-permute-start | bytes 3538952 | tf_op jit(solution)/shard_map/ppermute | solution.py:938
  558.4 56.4 %collective-permute-start.66 = (bf16[256,2048]{1,0:T(8,128)(2,1)}, bf16[256,2048]{1,0:T(8,128)(2,1)}, u32[]{:S(2)}, u32[]{:S(2)}) collective-permute-start(bf16[256,2048]{1,0:T(8,128)(2,1)} %get-tuple-element.677), channel_id=1, source_target_pairs={{0,16},{8,24},{16,0},{24,8},{1,17},{9,25},{17,1},{25,9},{2,18},{10... | collective-permute-start | bytes 3145736 | tf_op jit(solution)/shard_map/ppermute | solution.py:938
  560.9 53.9 %collective-permute-start.69 = (bf16[240,2048]{1,0:T(8,128)(2,1)}, bf16[240,2048]{1,0:T(8,128)(2,1)}, u32[]{:S(2)}, u32[]{:S(2)}) collective-permute-start(bf16[240,2048]{1,0:T(8,128)(2,1)} %add_convert_fusion.28), channel_id=1, source_target_pairs={{0,4},{4,0},{1,5},{5,1},{2,6},{6,2},{3,7},{7,3},{8,12},{12,8},{9,1... | collective-permute-start | bytes 2949128 | tf_op jit(solution)/shard_map/ppermute | solution.py:938
  685.3 27.5 %collective-permute-start.82 = (bf16[128,2048]{1,0:T(8,128)(2,1)S(1)}, bf16[128,2048]{1,0:T(8,128)(2,1)S(1)}, u32[]{:S(2)}, u32[]{:S(2)}) collective-permute-start(bf16[128,2048]{1,0:T(8,128)(2,1)S(1)} %slice.572), channel_id=1, source_target_pairs={{0,4},{4,0},{1,5},{5,1},{2,6},{6,2},{3,7},{7,3},{8,12},{12,8},{9,1... | collective-permute-start | bytes 1572872 | tf_op jit(solution)/shard_map/ppermute | solution.py:938
  686.8 26.7 %collective-permute-start.83 = (bf16[272,2048]{1,0:T(8,128)(2,1)S(1)}, bf16[272,2048]{1,0:T(8,128)(2,1)S(1)}, u32[]{:S(2)}, u32[]{:S(2)}) collective-permute-start(bf16[272,2048]{1,0:T(8,128)(2,1)S(1)} %get-tuple-element.900), channel_id=1, source_target_pairs={{0,1},{1,0},{2,3},{3,2},{4,5},{5,4},{6,7},{7,6},{8,9},{9,8},{10,11... | collective-permute-start | bytes 3342344 | tf_op jit(solution)/shard_map/ppermute | solution.py:938
  715.6 37.3 %collective-permute-start.86 = (bf16[256,2048]{1,0:T(8,128)(2,1)}, bf16[256,2048]{1,0:T(8,128)(2,1)}, u32[]{:S(2)}, u32[]{:S(2)}) collective-permute-start(bf16[256,2048]{1,0:T(8,128)(2,1)} %add_convert_fusion.3), channel_id=1, source_target_pairs={{0,2},{2,0},{1,3},{3,1},{4,6},{6,4},{5,7},{7,5},{8,10},{10,8},{9,1... | collective-permute-start | bytes 3145736 | tf_op jit(solution)/shard_map/ppermute | solution.py:938
  717.2 35.6 %collective-permute-start.85 = (bf16[256,2048]{1,0:T(8,128)(2,1)}, bf16[256,2048]{1,0:T(8,128)(2,1)}, u32[]{:S(2)}, u32[]{:S(2)}) collective-permute-start(bf16[256,2048]{1,0:T(8,128)(2,1)} %get-tuple-element.738), channel_id=1, source_target_pairs={{0,16},{8,24},{16,0},{24,8},{1,17},{9,25},{17,1},{25,9},{2,18},{10... | collective-permute-start | bytes 3145736 | tf_op jit(solution)/shard_map/ppermute | solution.py:938
  719.1 32.3 %collective-permute-start.87 = (bf16[144,2048]{1,0:T(8,128)(2,1)S(1)}, bf16[144,2048]{1,0:T(8,128)(2,1)S(1)}, u32[]{:S(2)}, u32[]{:S(2)}) collective-permute-start(bf16[144,2048]{1,0:T(8,128)(2,1)S(1)} %slice.537), channel_id=1, source_target_pairs={{0,4},{4,0},{1,5},{5,1},{2,6},{6,2},{3,7},{7,3},{8,12},{12,8},{9,1... | collective-permute-start | bytes 1769480 | tf_op jit(solution)/shard_map/ppermute | solution.py:938
  (129 other events, 1837.5 us)
